TPU v7x, 256 devices: a whole 4x4x8 slice. The times are simulated.
256 devices in a mesh: gz: 256 (over y, z, x, core).
Axes of the slice: x: 4, y: 4, z: 8, core: 2. Of those that a mesh axis runs over, the one named last changes fastest.
Arguments:
- pressure_guess: float32 [2048, 64, 512], P('gz'), may hold values from -6 to 6
- source: float32 [2048, 64, 512], P('gz'), may hold values from -6 to 6
- conductance: float32 [2048, 64, 512], P('gz'), may hold values from 0.25 to 4
Outputs:
- pressure: float32 [2048, 64, 512], P('gz')
- correction_mid: float32 [1024, 32, 256], P('gz')
- correction_low: float32 [512, 16, 128], P('gz')
All inputs are finite; a program needn't handle non-finite values.
Results may differ from a plain program's by a relative error of at most 0.00002.
Values sent between devices are 32-bit elements; how exact they have to be, the bound alone decides.
A program may use at most 192 MiB of HBM per device.

v0:
```python
import jax
import jax.numpy as jnp
from jax import lax
from jax.sharding import PartitionSpec as P


def with_halo(x, sides, width):
    for axis, dim in sides:
        peers, length = (lax.axis_size(axis), x.shape[dim])
        up = [(i, (i + 1) % peers) for i in range(peers - 1)]
        down = [(j, i) for i, j in up]
        last = lax.slice_in_dim(x, length - width, length, axis=dim)
        first = lax.slice_in_dim(x, 0, width, axis=dim)
        before = lax.ppermute(last, axis, up)
        after = lax.ppermute(first, axis, down)
        x = jnp.concatenate([before, x, after], axis=dim)
    return x


def face_terms(cond_ext):
    padded = jnp.pad(cond_ext, ((0, 0), (1, 1), (1, 1)))
    centre = padded[1:-1, 1:-1, 1:-1]
    sides = [
        padded[2:, 1:-1, 1:-1],
        padded[:-2, 1:-1, 1:-1],
        padded[1:-1, 2:, 1:-1],
        padded[1:-1, :-2, 1:-1],
        padded[1:-1, 1:-1, 2:],
        padded[1:-1, 1:-1, :-2],
    ]
    faces = [0.5 * (centre + other) for other in sides]
    diag = faces[0]
    for face in faces[1:]:
        diag = diag + face
    return (faces, diag)


def gather_off(faces, field_ext):
    padded = jnp.pad(field_ext, ((0, 0), (1, 1), (1, 1)))
    sides = [
        padded[2:, 1:-1, 1:-1],
        padded[:-2, 1:-1, 1:-1],
        padded[1:-1, 2:, 1:-1],
        padded[1:-1, :-2, 1:-1],
        padded[1:-1, 1:-1, 2:],
        padded[1:-1, 1:-1, :-2],
    ]
    total = faces[0] * sides[0]
    for face, other in zip(faces[1:], sides[1:]):
        total = total + face * other
    return total


def red_mask(shape):
    zpos = lax.broadcasted_iota(jnp.int32, shape, 0)
    ypos = lax.broadcasted_iota(jnp.int32, shape, 1)
    xpos = lax.broadcasted_iota(jnp.int32, shape, 2)
    return (zpos + ypos + xpos) % 2 == 0


def restrict_axis(padded, axis):
    count = padded.shape[axis] - 2
    parts = [lax.slice_in_dim(padded, start, start + count - 1, 2, axis) for start in range(4)]
    return 0.125 * (parts[0] + 3.0 * parts[1] + 3.0 * parts[2] + parts[3])


def restrict(residual_ext):
    out = restrict_axis(residual_ext, 0)
    out = restrict_axis(jnp.pad(out, ((0, 0), (1, 1), (0, 0))), 1)
    return restrict_axis(jnp.pad(out, ((0, 0), (0, 0), (1, 1))), 2)


def coarsen(cond):
    depth, rows, cols = cond.shape
    grouped = cond.reshape(depth // 2, 2, rows // 2, 2, cols // 2, 2)
    return 0.125 * jnp.sum(grouped, axis=(1, 3, 5))


def smooth(start, rhs, cond, scale):
    cond_ext = with_halo(cond, (("gz", 0),), 2)
    faces, diag = face_terms(cond_ext[1:-1])
    red = red_mask(start.shape)
    start_ext = with_halo(start, (("gz", 0),), 1)
    off = gather_off(faces, start_ext)
    field = jnp.where(red, (rhs / scale + off) / diag, start)
    field_ext = with_halo(field, (("gz", 0),), 1)
    off = gather_off(faces, field_ext)
    field = jnp.where(red, field, (rhs / scale + off) / diag)
    return (field, faces, diag)


def descend(field, rhs, faces, diag, scale):
    field_ext = with_halo(field, (("gz", 0),), 1)
    residual = rhs - scale * (diag * field - gather_off(faces, field_ext))
    residual_ext = with_halo(residual, (("gz", 0),), 1)
    return restrict(residual_ext)


def on_device(pressure_guess, source, conductance):
    pressure, faces, diag = smooth(pressure_guess, source, conductance, 1.0)
    rhs_mid = descend(pressure, source, faces, diag, 1.0)
    cond_mid = coarsen(conductance)
    correction_mid, faces, diag = smooth(jnp.zeros_like(rhs_mid), rhs_mid, cond_mid, 0.25)
    rhs_low = descend(correction_mid, rhs_mid, faces, diag, 0.25)
    cond_low = coarsen(cond_mid)
    correction_low, faces, diag = smooth(jnp.zeros_like(rhs_low), rhs_low, cond_low, 0.0625)
    return (pressure, correction_mid, correction_low)


def solution(mesh):
    in_specs = (P("gz", None, None), P("gz", None, None), P("gz", None, None))
    out_specs = (P("gz", None, None), P("gz", None, None), P("gz", None, None))
    return jax.shard_map(
        on_device, mesh=mesh, in_specs=in_specs, out_specs=out_specs, check_vma=False
    )
```

profile of v0, /device:TPU:24, one launch (start us, length us, event | category | flops | bytes accessed | tf_op | source)
XLA Modules:
  0.0 304.5 jit_solution(9446317154053774115)
XLA Ops:
  1.2 9.6 %collective-permute-start.11 = (f32[1,32,256]{2,1,0:T(8,128)}, f32[1,32,256]{2,1,0:T(8,128)}, u32[]{:S(2)}, u32[]{:S(2)}) collective-permute-start(f32[1,32,256]{2,1,0:T(8,128)} %broadcast.112), channel_id=1, source_target_pairs={{1,0},{2,1},{3,2},{4,3},{5,4},{6,5},{7,6},{8,7},{9,8},{10,9},{11,1... | collective-permute-start | bytes 98312 | tf_op jit(solution)/shard_map/ppermute | solution.py:15
  10.8 1.9 collective-permute-start.13
  12.7 1.0 fusion.122
  13.7 7.9 %collective-permute-start.1 = (f32[1,64,512]{2,1,0:T(8,128)S(1)}, f32[1,64,512]{2,1,0:T(8,128)S(1)}, u32[]{:S(2)}, u32[]{:S(2)}) collective-permute-start(f32[1,64,512]{2,1,0:T(8,128)S(1)} %get-tuple-element.16), channel_id=1, source_target_pairs={{1,0},{2,1},{3,2},{4,3},{5,4},{6,5},{7,6},{8,7},{9,8},{10,9},{11,1... | collective-permute-start | bytes 393224 | tf_op jit(solution)/shard_map/ppermute | solution.py:15
  21.6 1.9 collective-permute-start.3
  23.5 1.1 fusion.121
  24.6 7.9 %collective-permute-start = (f32[2,64,512]{2,1,0:T(8,128)S(1)}, f32[2,64,512]{2,1,0:T(8,128)S(1)}, u32[]{:S(2)}, u32[]{:S(2)}) collective-permute-start(f32[2,64,512]{2,1,0:T(8,128)S(1)} %get-tuple-element.14), channel_id=1, source_target_pairs={{1,0},{2,1},{3,2},{4,3},{5,4},{6,5},{7,6},{8,7},{9,8},{10,9},{11,1... | collective-permute-start | bytes 786440 | tf_op jit(solution)/shard_map/ppermute | solution.py:15
  32.5 68.4 %reshape.13 = f32[4,2,32,2,256,2]{5,4,3,2,1,0:T(8,128)} reshape(f32[8,64,512]{2,1,0:T(8,128)S(1)} %copy-done) | data formatting | bytes 2097152 | tf_op jit(solution)/shard_map/reshape | solution.py:75
  100.9 21.5 %reduce_sum.18 = f32[4,32,256]{2,1,0:T(8,128)} reduce(f32[4,2,32,2,256,2]{5,4,3,2,1,0:T(8,128)} %reshape.13, f32[]{:T(128)} %constant.27.clone.1), dimensions={1,3,5}, to_apply=%region_0.1 | reduce | flops 229376 | bytes 1179652 | tf_op jit(solution)/shard_map/reduce_sum | solution.py:76
  122.4 1.9 collective-permute-start.2
  125.0 9.3 %collective-permute-done.2 = f32[2,64,512]{2,1,0:T(8,128)S(1)} collective-permute-done((f32[2,64,512]{2,1,0:T(8,128)S(1)}, f32[2,64,512]{2,1,0:T(8,128)S(1)}, u32[]{:S(2)}, u32[]{:S(2)}) %collective-permute-start.2) | collective-permute-done | bytes 262176 | tf_op jit(solution)/shard_map/ppermute | solution.py:14
  135.2 3.1 %fusion.27 = f32[8,64,512]{2,1,0:T(8,128)S(1)} fusion(f32[8,64,512]{2,1,0:T(8,128)S(1)} %copy-done.6, f32[8,64,512]{2,1,0:T(8,128)S(1)} %copy-done.3, f32[10,66,514]{2,1,0:T(8,128)S(1)} %select_maximum_fusion.4, f32[1,64,512]{2,1,0:T(8,128)S(1)} %copy-done.13, f32[1,64,512]{2,1,0:T(8,128)S(1)} %collective-permute-done.1, f32[8,64,512]{2,1,0:T(8,128)S(1)} %copy-done, ...), kind=kLoop, calls=%fused_computation.56 | loop fusion | flops 12845056 | bytes 13369344 | tf_op jit(solution)/shard_map/jit(_where)/select_n | solution.py:85
  138.4 1.9 collective-permute-start.4
  140.3 2.4 collective-permute-start.5
  142.8 8.0 %collective-permute-done.5 = f32[1,64,512]{2,1,0:T(8,128)S(1)} collective-permute-done((f32[1,64,512]{2,1,0:T(8,128)S(1)}, f32[1,64,512]{2,1,0:T(8,128)S(1)}, u32[]{:S(2)}, u32[]{:S(2)}) %collective-permute-start.5) | collective-permute-done | bytes 131104 | tf_op jit(solution)/shard_map/ppermute | solution.py:14
  151.4 3.1 %fusion.17 = f32[8,64,512]{2,1,0:T(8,128)S(1)} fusion(f32[8,64,512]{2,1,0:T(8,128)S(1)} %fusion.27, f32[8,64,512]{2,1,0:T(8,128)S(1)} %copy-done.3, f32[10,66,514]{2,1,0:T(8,128)S(1)} %select_maximum_fusion.2, f32[1,64,512]{2,1,0:T(8,128)S(1)} %collective-permute-done.5, f32[1,64,512]{2,1,0:T(8,128)S(1)} %collective-permute-done.4, ...), kind=kLoop, calls=%fused_computation.40 | loop fusion | flops 12845056 | bytes 13369344 | tf_op jit(solution)/shard_map/jit(_where)/select_n | solution.py:88
  156.2 1.9 collective-permute-start.6
  158.1 2.4 collective-permute-start.7
  161.2 7.4 %collective-permute-start.10 = (f32[2,32,256]{2,1,0:T(8,128)}, f32[2,32,256]{2,1,0:T(8,128)}, u32[]{:S(2)}, u32[]{:S(2)}) collective-permute-start(f32[2,32,256]{2,1,0:T(8,128)} %get-tuple-element.24), channel_id=1, source_target_pairs={{1,0},{2,1},{3,2},{4,3},{5,4},{6,5},{7,6},{8,7},{9,8},{10,9},{11,1... | collective-permute-start | bytes 196616 | tf_op jit(solution)/shard_map/ppermute | solution.py:15
  168.6 9.8 %mul.354 = f32[2,2,16,2,128,2]{5,4,3,2,1,0:T(8,128)} reshape(f32[4,32,256]{2,1,0:T(8,128)S(1)} %broadcast_multiply_fusion) | data formatting | bytes 262144 | tf_op jit(solution)/shard_map/mul | solution.py:76
  178.4 4.6 %reduce_sum.19 = f32[2,16,128]{2,1,0:T(8,128)} reduce(f32[2,2,16,2,128,2]{5,4,3,2,1,0:T(8,128)} %mul.354, f32[]{:T(128)} %constant.27.clone.1), dimensions={1,3,5}, to_apply=%region_1.2 | reduce | flops 28672 | bytes 147460 | tf_op jit(solution)/shard_map/reduce_sum | solution.py:76
  183.0 2.0 collective-permute-start.12
  185.1 1.9 select_maximum_fusion
  187.0 3.1 %fusion.7 = f32[8,64,512]{2,1,0:T(8,128)S(1)} fusion(f32[8,64,512]{2,1,0:T(8,128)S(1)} %copy-done.4, f32[10,66,514]{2,1,0:T(8,128)S(1)} %select_maximum_fusion, f32[8,64,512]{2,1,0:T(8,128)S(1)} %copy-done.2, f32[1,64,512]{2,1,0:T(8,128)} %collective-permute-done.7, f32[1,64,512]{2,1,0:T(8,128)} %collective-permute-done.6, f32[8,64,512]{2,1,0:T(8,128)S(1)} %copy-done, ...), kind=kLoop, calls=%fused_computation.24 | loop fusion | flops 9175040 | bytes 13369344 | tf_op jit(solution)/shard_map/sub | solution.py:94
  190.1 1.9 collective-permute-start.8
  192.1 7.9 %collective-permute-start.9 = (f32[1,64,512]{2,1,0:T(8,128)S(1)}, f32[1,64,512]{2,1,0:T(8,128)S(1)}, u32[]{:S(2)}, u32[]{:S(2)}) collective-permute-start(f32[1,64,512]{2,1,0:T(8,128)S(1)} %get-tuple-element.8), channel_id=1, source_target_pairs={{1,0},{2,1},{3,2},{4,3},{5,4},{6,5},{7,6},{8,7},{9,8},{10,9},{11,1... | collective-permute-start | bytes 393224 | tf_op jit(solution)/shard_map/ppermute | solution.py:15
  204.1 4.4 %slice.441 = f32[4,32,256]{2,1,0:T(8,128)S(1)} slice(f32[4,32,514]{2,1,0:T(8,128)S(1)} %pad.61), slice={[0:4:1], [0:32:1], [0:511:2]} | slice | bytes 262144 | tf_op jit(solution)/shard_map/slice | solution.py:63
  208.4 4.4 %slice.442 = f32[4,32,256]{2,1,0:T(8,128)S(1)} slice(f32[4,32,514]{2,1,0:T(8,128)S(1)} %pad.61), slice={[0:4:1], [0:32:1], [1:512:2]} | slice | bytes 262144 | tf_op jit(solution)/shard_map/slice | solution.py:63
  212.8 4.4 %slice.443 = f32[4,32,256]{2,1,0:T(8,128)S(1)} slice(f32[4,32,514]{2,1,0:T(8,128)S(1)} %pad.61), slice={[0:4:1], [0:32:1], [2:513:2]} | slice | bytes 262144 | tf_op jit(solution)/shard_map/slice | solution.py:63
  217.2 4.6 %slice.444 = f32[4,32,256]{2,1,0:T(8,128)S(1)} slice(f32[4,32,514]{2,1,0:T(8,128)S(1)} %pad.61), slice={[0:4:1], [0:32:1], [3:514:2]} | slice | bytes 262144 | tf_op jit(solution)/shard_map/slice | solution.py:63
  221.8 1.1 fusion.84
  222.9 8.0 %collective-permute-start.14 = (f32[1,32,256]{2,1,0:T(8,128)S(1)}, f32[1,32,256]{2,1,0:T(8,128)S(1)}, u32[]{:S(2)}, u32[]{:S(2)}) collective-permute-start(f32[1,32,256]{2,1,0:T(8,128)S(1)} %get-tuple-element.22), channel_id=1, source_target_pairs={{1,0},{2,1},{3,2},{4,3},{5,4},{6,5},{7,6},{8,7},{9,8},{10,9},{11,1... | collective-permute-start | bytes 98312 | tf_op jit(solution)/shard_map/ppermute | solution.py:15
  230.9 1.9 collective-permute-start.15
  232.9 7.9 %collective-permute-start.20 = (f32[2,16,128]{2,1,0:T(8,128)S(1)}, f32[2,16,128]{2,1,0:T(8,128)S(1)}, u32[]{:S(2)}, u32[]{:S(2)}) collective-permute-start(f32[2,16,128]{2,1,0:T(8,128)S(1)} %broadcast_multiply_fusion.1), channel_id=1, source_target_pairs={{1,0},{2,1},{3,2},{4,3},{5,4},{6,5},{7,6},{8,7},{9,8},{10,9},{11,1... | collective-permute-start | bytes 49160 | tf_op jit(solution)/shard_map/ppermute | solution.py:15
  240.7 1.9 collective-permute-start.22
  242.7 7.9 %collective-permute-start.21 = (f32[1,16,128]{2,1,0:T(8,128)S(1)}, f32[1,16,128]{2,1,0:T(8,128)S(1)}, u32[]{:S(2)}, u32[]{:S(2)}) collective-permute-start(f32[1,16,128]{2,1,0:T(8,128)S(1)} %broadcast.120), channel_id=1, source_target_pairs={{1,0},{2,1},{3,2},{4,3},{5,4},{6,5},{7,6},{8,7},{9,8},{10,9},{11,1... | collective-permute-start | bytes 24584 | tf_op jit(solution)/shard_map/ppermute | solution.py:15
  250.6 1.9 collective-permute-start.23
  252.7 1.1 fusion.69
  253.8 7.9 %collective-permute-start.16 = (f32[1,32,256]{2,1,0:T(8,128)S(1)}, f32[1,32,256]{2,1,0:T(8,128)S(1)}, u32[]{:S(2)}, u32[]{:S(2)}) collective-permute-start(f32[1,32,256]{2,1,0:T(8,128)S(1)} %get-tuple-element.20), channel_id=1, source_target_pairs={{1,0},{2,1},{3,2},{4,3},{5,4},{6,5},{7,6},{8,7},{9,8},{10,9},{11,1... | collective-permute-start | bytes 98312 | tf_op jit(solution)/shard_map/ppermute | solution.py:15
  261.7 1.9 collective-permute-start.17
  263.7 7.4 %collective-permute-done.17 = f32[1,32,256]{2,1,0:T(8,128)S(1)} collective-permute-done((f32[1,32,256]{2,1,0:T(8,128)S(1)}, f32[1,32,256]{2,1,0:T(8,128)S(1)}, u32[]{:S(2)}, u32[]{:S(2)}) %collective-permute-start.17) | collective-permute-done | bytes 32800 | tf_op jit(solution)/shard_map/ppermute | solution.py:14
  271.3 1.1 fusion.59
  272.4 1.9 collective-permute-start.18
  274.3 7.9 %collective-permute-start.19 = (f32[1,32,256]{2,1,0:T(8,128)S(1)}, f32[1,32,256]{2,1,0:T(8,128)S(1)}, u32[]{:S(2)}, u32[]{:S(2)}) collective-permute-start(f32[1,32,256]{2,1,0:T(8,128)S(1)} %get-tuple-element.18), channel_id=1, source_target_pairs={{1,0},{2,1},{3,2},{4,3},{5,4},{6,5},{7,6},{8,7},{9,8},{10,9},{11,1... | collective-permute-start | bytes 98312 | tf_op jit(solution)/shard_map/ppermute | solution.py:15
  282.3 1.4 collective-permute-done.19
  286.6 7.9 %collective-permute-start.24 = (f32[1,16,128]{2,1,0:T(8,128)S(1)}, f32[1,16,128]{2,1,0:T(8,128)S(1)}, u32[]{:S(2)}, u32[]{:S(2)}) collective-permute-start(f32[1,16,128]{2,1,0:T(8,128)S(1)} %get-tuple-element.26), channel_id=1, source_target_pairs={{1,0},{2,1},{3,2},{4,3},{5,4},{6,5},{7,6},{8,7},{9,8},{10,9},{11,1... | collective-permute-start | bytes 24584 | tf_op jit(solution)/shard_map/ppermute | solution.py:15
  294.5 1.9 collective-permute-start.25
  296.4 7.2 %collective-permute-done.25 = f32[1,16,128]{2,1,0:T(8,128)S(1)} collective-permute-done((f32[1,16,128]{2,1,0:T(8,128)S(1)}, f32[1,16,128]{2,1,0:T(8,128)S(1)}, u32[]{:S(2)}, u32[]{:S(2)}) %collective-permute-start.25) | collective-permute-done | bytes 8224 | tf_op jit(solution)/shard_map/ppermute | solution.py:14
  (99 shorter events, 13.2 us)
Async XLA Ops:
  0.6 31.9 %copy-start = (f32[8,64,512]{2,1,0:T(8,128)S(1)}, f32[8,64,512]{2,1,0:T(8,128)}, u32[]{:S(2)}) copy-start(f32[8,64,512]{2,1,0:T(8,128)} %param.5) | copy-start | bytes 3145732
  1.2 190.8 %collective-permute-start.11 = (f32[1,32,256]{2,1,0:T(8,128)}, f32[1,32,256]{2,1,0:T(8,128)}, u32[]{:S(2)}, u32[]{:S(2)}) collective-permute-start(f32[1,32,256]{2,1,0:T(8,128)} %broadcast.112), channel_id=1, source_target_pairs={{1,0},{2,1},{3,2},{4,3},{5,4},{6,5},{7,6},{8,7},{9,8},{10,9},{11,1... | collective-permute-start | bytes 98312 | tf_op jit(solution)/shard_map/ppermute | solution.py:15
  10.8 189.1 %collective-permute-start.13 = (f32[1,32,256]{2,1,0:T(8,128)}, f32[1,32,256]{2,1,0:T(8,128)}, u32[]{:S(2)}, u32[]{:S(2)}) collective-permute-start(f32[1,32,256]{2,1,0:T(8,128)} %broadcast.112), channel_id=1, source_target_pairs={{0,1},{1,2},{2,3},{3,4},{4,5},{5,6},{6,7},{7,8},{8,9},{9,10},{10,1... | collective-permute-start | bytes 98312 | tf_op jit(solution)/shard_map/ppermute | solution.py:14
  13.7 108.7 %collective-permute-start.1 = (f32[1,64,512]{2,1,0:T(8,128)S(1)}, f32[1,64,512]{2,1,0:T(8,128)S(1)}, u32[]{:S(2)}, u32[]{:S(2)}) collective-permute-start(f32[1,64,512]{2,1,0:T(8,128)S(1)} %get-tuple-element.16), channel_id=1, source_target_pairs={{1,0},{2,1},{3,2},{4,3},{5,4},{6,5},{7,6},{8,7},{9,8},{10,9},{11,1... | collective-permute-start | bytes 393224 | tf_op jit(solution)/shard_map/ppermute | solution.py:15
  21.6 102.7 %collective-permute-start.3 = (f32[1,64,512]{2,1,0:T(8,128)S(1)}, f32[1,64,512]{2,1,0:T(8,128)S(1)}, u32[]{:S(2)}, u32[]{:S(2)}) collective-permute-start(f32[1,64,512]{2,1,0:T(8,128)S(1)} %get-tuple-element.15), channel_id=1, source_target_pairs={{0,1},{1,2},{2,3},{3,4},{4,5},{5,6},{6,7},{7,8},{8,9},{9,10},{10,1... | collective-permute-start | bytes 393224 | tf_op jit(solution)/shard_map/ppermute | solution.py:14
  24.6 100.3 %collective-permute-start = (f32[2,64,512]{2,1,0:T(8,128)S(1)}, f32[2,64,512]{2,1,0:T(8,128)S(1)}, u32[]{:S(2)}, u32[]{:S(2)}) collective-permute-start(f32[2,64,512]{2,1,0:T(8,128)S(1)} %get-tuple-element.14), channel_id=1, source_target_pairs={{1,0},{2,1},{3,2},{4,3},{5,4},{6,5},{7,6},{8,7},{9,8},{10,9},{11,1... | collective-permute-start | bytes 786440 | tf_op jit(solution)/shard_map/ppermute | solution.py:15
  100.9 23.4 %copy-start.5 = (f32[8,64,512]{2,1,0:T(8,128)S(1)}, f32[8,64,512]{2,1,0:T(8,128)}, u32[]{:S(2)}) copy-start(f32[8,64,512]{2,1,0:T(8,128)} %param.3) | copy-start | bytes 3145732
  122.4 11.9 %collective-permute-start.2 = (f32[2,64,512]{2,1,0:T(8,128)S(1)}, f32[2,64,512]{2,1,0:T(8,128)S(1)}, u32[]{:S(2)}, u32[]{:S(2)}) collective-permute-start(f32[2,64,512]{2,1,0:T(8,128)S(1)} %get-tuple-element.13), channel_id=1, source_target_pairs={{0,1},{1,2},{2,3},{3,4},{4,5},{5,6},{6,7},{7,8},{8,9},{9,10},{10,1... | collective-permute-start | bytes 786440 | tf_op jit(solution)/shard_map/ppermute | solution.py:14
  124.3 0.7 copy-start.12
  124.9 10.0 %copy-start.3 = (f32[8,64,512]{2,1,0:T(8,128)S(1)}, f32[8,64,512]{2,1,0:T(8,128)}, u32[]{:S(2)}) copy-start(f32[8,64,512]{2,1,0:T(8,128)} %param.4) | copy-start | bytes 3145732
  124.9 10.0 %copy-start.6 = (f32[8,64,512]{2,1,0:T(8,128)S(1)}, f32[8,64,512]{2,1,0:T(8,128)}, u32[]{:S(2)}) copy-start(f32[8,64,512]{2,1,0:T(8,128)} %param.3) | copy-start | bytes 3145732
  134.3 0.9 copy-start.13
  135.2 7.5 %copy-start.7 = (f32[4,32,256]{2,1,0:T(8,128)S(1)}, f32[4,32,256]{2,1,0:T(8,128)}, u32[]{:S(2)}) copy-start(f32[4,32,256]{2,1,0:T(8,128)} %reduce_sum.18) | copy-start | bytes 393220
  138.4 4.4 %collective-permute-start.4 = (f32[1,64,512]{2,1,0:T(8,128)S(1)}, f32[1,64,512]{2,1,0:T(8,128)S(1)}, u32[]{:S(2)}, u32[]{:S(2)}) collective-permute-start(f32[1,64,512]{2,1,0:T(8,128)S(1)} %get-tuple-element.12), channel_id=1, source_target_pairs={{1,0},{2,1},{3,2},{4,3},{5,4},{6,5},{7,6},{8,7},{9,8},{10,9},{11,1... | collective-permute-start | bytes 393224 | tf_op jit(solution)/shard_map/ppermute | solution.py:15
  140.3 10.5 %collective-permute-start.5 = (f32[1,64,512]{2,1,0:T(8,128)S(1)}, f32[1,64,512]{2,1,0:T(8,128)S(1)}, u32[]{:S(2)}, u32[]{:S(2)}) collective-permute-start(f32[1,64,512]{2,1,0:T(8,128)S(1)} %get-tuple-element.11), channel_id=1, source_target_pairs={{0,1},{1,2},{2,3},{3,4},{4,5},{5,6},{6,7},{7,8},{8,9},{9,10},{10,1... | collective-permute-start | bytes 393224 | tf_op jit(solution)/shard_map/ppermute | solution.py:14
  154.5 1.0 copy-start.1
  156.2 26.8 %collective-permute-start.6 = (f32[1,64,512]{2,1,0:T(8,128)}, f32[1,64,512]{2,1,0:T(8,128)}, u32[]{:S(2)}, u32[]{:S(2)}) collective-permute-start(f32[1,64,512]{2,1,0:T(8,128)} %get-tuple-element.10), channel_id=1, source_target_pairs={{1,0},{2,1},{3,2},{4,3},{5,4},{6,5},{7,6},{8,7},{9,8},{10,9},{11,1... | collective-permute-start | bytes 393224 | tf_op jit(solution)/shard_map/ppermute | solution.py:15
  158.1 26.9 %collective-permute-start.7 = (f32[1,64,512]{2,1,0:T(8,128)}, f32[1,64,512]{2,1,0:T(8,128)}, u32[]{:S(2)}, u32[]{:S(2)}) collective-permute-start(f32[1,64,512]{2,1,0:T(8,128)} %get-tuple-element.9), channel_id=1, source_target_pairs={{0,1},{1,2},{2,3},{3,4},{4,5},{5,6},{6,7},{7,8},{8,9},{9,10},{10,1... | collective-permute-start | bytes 393224 | tf_op jit(solution)/shard_map/ppermute | solution.py:14
  161.2 39.7 %collective-permute-start.10 = (f32[2,32,256]{2,1,0:T(8,128)}, f32[2,32,256]{2,1,0:T(8,128)}, u32[]{:S(2)}, u32[]{:S(2)}) collective-permute-start(f32[2,32,256]{2,1,0:T(8,128)} %get-tuple-element.24), channel_id=1, source_target_pairs={{1,0},{2,1},{3,2},{4,3},{5,4},{6,5},{7,6},{8,7},{9,8},{10,9},{11,1... | collective-permute-start | bytes 196616 | tf_op jit(solution)/shard_map/ppermute | solution.py:15
  183.0 4.0 %copy-start.2 = (f32[8,64,512]{2,1,0:T(8,128)S(1)}, f32[8,64,512]{2,1,0:T(8,128)}, u32[]{:S(2)}) copy-start(f32[8,64,512]{2,1,0:T(8,128)} %copy-done.1) | copy-start | bytes 3145732
  183.0 4.0 %copy-start.4 = (f32[8,64,512]{2,1,0:T(8,128)S(1)}, f32[8,64,512]{2,1,0:T(8,128)}, u32[]{:S(2)}) copy-start(f32[8,64,512]{2,1,0:T(8,128)} %param.4) | copy-start | bytes 3145732
  183.0 17.9 %collective-permute-start.12 = (f32[2,32,256]{2,1,0:T(8,128)}, f32[2,32,256]{2,1,0:T(8,128)S(1)}, u32[]{:S(2)}, u32[]{:S(2)}) collective-permute-start(f32[2,32,256]{2,1,0:T(8,128)} %get-tuple-element.23), channel_id=1, source_target_pairs={{0,1},{1,2},{2,3},{3,4},{4,5},{5,6},{6,7},{7,8},{8,9},{9,10},{10,1... | collective-permute-start | bytes 196616 | tf_op jit(solution)/shard_map/ppermute | solution.py:14
  190.1 11.8 %collective-permute-start.8 = (f32[1,64,512]{2,1,0:T(8,128)S(1)}, f32[1,64,512]{2,1,0:T(8,128)S(1)}, u32[]{:S(2)}, u32[]{:S(2)}) collective-permute-start(f32[1,64,512]{2,1,0:T(8,128)S(1)} %get-tuple-element.7), channel_id=1, source_target_pairs={{0,1},{1,2},{2,3},{3,4},{4,5},{5,6},{6,7},{7,8},{8,9},{9,10},{10,1... | collective-permute-start | bytes 393224 | tf_op jit(solution)/shard_map/ppermute | solution.py:14
  192.1 10.4 %collective-permute-start.9 = (f32[1,64,512]{2,1,0:T(8,128)S(1)}, f32[1,64,512]{2,1,0:T(8,128)S(1)}, u32[]{:S(2)}, u32[]{:S(2)}) collective-permute-start(f32[1,64,512]{2,1,0:T(8,128)S(1)} %get-tuple-element.8), channel_id=1, source_target_pairs={{1,0},{2,1},{3,2},{4,3},{5,4},{6,5},{7,6},{8,7},{9,8},{10,9},{11,1... | collective-permute-start | bytes 393224 | tf_op jit(solution)/shard_map/ppermute | solution.py:15
  200.9 1.9 copy-start.10
  203.4 18.3 %copy-start.8 = (f32[4,32,256]{2,1,0:T(8,128)S(1)}, f32[4,32,256]{2,1,0:T(8,128)}, u32[]{:S(2)}) copy-start(f32[4,32,256]{2,1,0:T(8,128)} %reduce_sum.18) | copy-start | bytes 393220
  203.4 18.3 %copy-start.11 = (f32[2,32,256]{2,1,0:T(8,128)S(1)}, f32[2,32,256]{2,1,0:T(8,128)}, u32[]{:S(2)}) copy-start(f32[2,32,256]{2,1,0:T(8,128)} %copy-done.10) | copy-start | bytes 196612
  204.1 28.8 %copy-start.14 = (f32[2,16,128]{2,1,0:T(8,128)S(1)}, f32[2,16,128]{2,1,0:T(8,128)}, u32[]{:S(2)}) copy-start(f32[2,16,128]{2,1,0:T(8,128)} %reduce_sum.19) | copy-start | bytes 49156
  222.9 27.6 %collective-permute-start.14 = (f32[1,32,256]{2,1,0:T(8,128)S(1)}, f32[1,32,256]{2,1,0:T(8,128)S(1)}, u32[]{:S(2)}, u32[]{:S(2)}) collective-permute-start(f32[1,32,256]{2,1,0:T(8,128)S(1)} %get-tuple-element.22), channel_id=1, source_target_pairs={{1,0},{2,1},{3,2},{4,3},{5,4},{6,5},{7,6},{8,7},{9,8},{10,9},{11,1... | collective-permute-start | bytes 98312 | tf_op jit(solution)/shard_map/ppermute | solution.py:15
  230.9 21.6 %collective-permute-start.15 = (f32[1,32,256]{2,1,0:T(8,128)S(1)}, f32[1,32,256]{2,1,0:T(8,128)S(1)}, u32[]{:S(2)}, u32[]{:S(2)}) collective-permute-start(f32[1,32,256]{2,1,0:T(8,128)S(1)} %get-tuple-element.21), channel_id=1, source_target_pairs={{0,1},{1,2},{2,3},{3,4},{4,5},{5,6},{6,7},{7,8},{8,9},{9,10},{10,1... | collective-permute-start | bytes 98312 | tf_op jit(solution)/shard_map/ppermute | solution.py:14
  232.9 49.3 %collective-permute-start.20 = (f32[2,16,128]{2,1,0:T(8,128)S(1)}, f32[2,16,128]{2,1,0:T(8,128)S(1)}, u32[]{:S(2)}, u32[]{:S(2)}) collective-permute-start(f32[2,16,128]{2,1,0:T(8,128)S(1)} %broadcast_multiply_fusion.1), channel_id=1, source_target_pairs={{1,0},{2,1},{3,2},{4,3},{5,4},{6,5},{7,6},{8,7},{9,8},{10,9},{11,1... | collective-permute-start | bytes 49160 | tf_op jit(solution)/shard_map/ppermute | solution.py:15
  240.7 41.4 %collective-permute-start.22 = (f32[2,16,128]{2,1,0:T(8,128)S(1)}, f32[2,16,128]{2,1,0:T(8,128)S(1)}, u32[]{:S(2)}, u32[]{:S(2)}) collective-permute-start(f32[2,16,128]{2,1,0:T(8,128)S(1)} %broadcast_multiply_fusion.1), channel_id=1, source_target_pairs={{0,1},{1,2},{2,3},{3,4},{4,5},{5,6},{6,7},{7,8},{8,9},{9,10},{10,1... | collective-permute-start | bytes 49160 | tf_op jit(solution)/shard_map/ppermute | solution.py:14
  242.7 19.0 %collective-permute-start.21 = (f32[1,16,128]{2,1,0:T(8,128)S(1)}, f32[1,16,128]{2,1,0:T(8,128)S(1)}, u32[]{:S(2)}, u32[]{:S(2)}) collective-permute-start(f32[1,16,128]{2,1,0:T(8,128)S(1)} %broadcast.120), channel_id=1, source_target_pairs={{1,0},{2,1},{3,2},{4,3},{5,4},{6,5},{7,6},{8,7},{9,8},{10,9},{11,1... | collective-permute-start | bytes 24584 | tf_op jit(solution)/shard_map/ppermute | solution.py:15
  250.6 13.0 %collective-permute-start.23 = (f32[1,16,128]{2,1,0:T(8,128)S(1)}, f32[1,16,128]{2,1,0:T(8,128)S(1)}, u32[]{:S(2)}, u32[]{:S(2)}) collective-permute-start(f32[1,16,128]{2,1,0:T(8,128)S(1)} %broadcast.120), channel_id=1, source_target_pairs={{0,1},{1,2},{2,3},{3,4},{4,5},{5,6},{6,7},{7,8},{8,9},{9,10},{10,1... | collective-permute-start | bytes 24584 | tf_op jit(solution)/shard_map/ppermute | solution.py:14
  253.8 30.0 %copy-start.9 = (f32[4,32,256]{2,1,0:T(8,128)}, f32[4,32,256]{2,1,0:T(8,128)S(1)}, u32[]{:S(2)}) copy-start(f32[4,32,256]{2,1,0:T(8,128)S(1)} %fusion.69) | copy-start | bytes 393220
  253.8 9.9 %collective-permute-start.16 = (f32[1,32,256]{2,1,0:T(8,128)S(1)}, f32[1,32,256]{2,1,0:T(8,128)S(1)}, u32[]{:S(2)}, u32[]{:S(2)}) collective-permute-start(f32[1,32,256]{2,1,0:T(8,128)S(1)} %get-tuple-element.20), channel_id=1, source_target_pairs={{1,0},{2,1},{3,2},{4,3},{5,4},{6,5},{7,6},{8,7},{9,8},{10,9},{11,1... | collective-permute-start | bytes 98312 | tf_op jit(solution)/shard_map/ppermute | solution.py:15
  261.7 9.5 %collective-permute-start.17 = (f32[1,32,256]{2,1,0:T(8,128)S(1)}, f32[1,32,256]{2,1,0:T(8,128)S(1)}, u32[]{:S(2)}, u32[]{:S(2)}) collective-permute-start(f32[1,32,256]{2,1,0:T(8,128)S(1)} %get-tuple-element.19), channel_id=1, source_target_pairs={{0,1},{1,2},{2,3},{3,4},{4,5},{5,6},{6,7},{7,8},{8,9},{9,10},{10,1... | collective-permute-start | bytes 98312 | tf_op jit(solution)/shard_map/ppermute | solution.py:14
  272.4 9.9 %collective-permute-start.18 = (f32[1,32,256]{2,1,0:T(8,128)S(1)}, f32[1,32,256]{2,1,0:T(8,128)S(1)}, u32[]{:S(2)}, u32[]{:S(2)}) collective-permute-start(f32[1,32,256]{2,1,0:T(8,128)S(1)} %get-tuple-element.17), channel_id=1, source_target_pairs={{0,1},{1,2},{2,3},{3,4},{4,5},{5,6},{6,7},{7,8},{8,9},{9,10},{10,1... | collective-permute-start | bytes 98312 | tf_op jit(solution)/shard_map/ppermute | solution.py:14
  274.3 9.4 %collective-permute-start.19 = (f32[1,32,256]{2,1,0:T(8,128)S(1)}, f32[1,32,256]{2,1,0:T(8,128)S(1)}, u32[]{:S(2)}, u32[]{:S(2)}) collective-permute-start(f32[1,32,256]{2,1,0:T(8,128)S(1)} %get-tuple-element.18), channel_id=1, source_target_pairs={{1,0},{2,1},{3,2},{4,3},{5,4},{6,5},{7,6},{8,7},{9,8},{10,9},{11,1... | collective-permute-start | bytes 98312 | tf_op jit(solution)/shard_map/ppermute | solution.py:15
  286.6 9.8 %collective-permute-start.24 = (f32[1,16,128]{2,1,0:T(8,128)S(1)}, f32[1,16,128]{2,1,0:T(8,128)S(1)}, u32[]{:S(2)}, u32[]{:S(2)}) collective-permute-start(f32[1,16,128]{2,1,0:T(8,128)S(1)} %get-tuple-element.26), channel_id=1, source_target_pairs={{1,0},{2,1},{3,2},{4,3},{5,4},{6,5},{7,6},{8,7},{9,8},{10,9},{11,1... | collective-permute-start | bytes 24584 | tf_op jit(solution)/shard_map/ppermute | solution.py:15
  294.5 9.2 %collective-permute-start.25 = (f32[1,16,128]{2,1,0:T(8,128)S(1)}, f32[1,16,128]{2,1,0:T(8,128)S(1)}, u32[]{:S(2)}, u32[]{:S(2)}) collective-permute-start(f32[1,16,128]{2,1,0:T(8,128)S(1)} %get-tuple-element.25), channel_id=1, source_target_pairs={{0,1},{1,2},{2,3},{3,4},{4,5},{5,6},{6,7},{7,8},{8,9},{9,10},{10,1... | collective-permute-start | bytes 24584 | tf_op jit(solution)/shard_map/ppermute | solution.py:14
where the time goes:
time: 306 us; the launch traced here: 304 us
  starting transfers between devices  118 us (39%)
  local copies, waits for them, and re-layouts  105 us (34%)
  other arithmetic  46.3 us (15%)
  waiting for transfers between devices  34 us (11%)
    ppermute x13, starting transfers between devices, with_halo(): after = lax.ppermute(first, axis, down)  91.7 us
    reshape x1, local copies, waits for them, and re-layouts, coarsen(): grouped = cond.reshape(depth // 2, 2, rows // 2, 2, cols // 2, 2)  68.4 us
    ppermute x13, waiting for transfers between devices, with_halo(): before = lax.ppermute(last, axis, up)  32 us
    reduce_sum x2, other arithmetic, coarsen(): return 0.125 * jnp.sum(grouped, axis=(1, 3, 5))  26.1 us
    ppermute x13, starting transfers between devices, with_halo(): before = lax.ppermute(last, axis, up)  26 us
    slice x16, local copies, waits for them, and re-layouts, restrict_axis(): lax.slice_in_dim(padded, start, start + count - 1, 2, axis)  21 us
    mul x1, local copies, waits for them, and re-layouts, coarsen(): return 0.125 * jnp.sum(grouped, axis=(1, 3, 5))  9.8 us
    concatenate x13, other arithmetic, with_halo(): x = jnp.concatenate([before, x, after], axis=dim)  6.25 us
  transfers between devices with their start and end apart: 26, of which 7 were waited for; matrix products, arithmetic and copies ran while one was open for 41% of the time, Pallas kernels for 0%

commit v1 on v0

v1 whole, which is shorter than its diff:
```python
import jax
import jax.numpy as jnp
from jax import lax
from jax.experimental import pallas as pl
from jax.experimental.pallas import tpu as pltpu
from jax.sharding import PartitionSpec as P

F32 = jnp.float32
BF16 = jnp.bfloat16


def parity(shape, offset):
    rows = lax.broadcasted_iota(jnp.int32, shape, 0)
    cols = lax.broadcasted_iota(jnp.int32, shape, 1)
    return ((rows + cols + offset) & 1) == 0


def shifts(plane):
    ny, nx = plane.shape
    return (
        pltpu.roll(plane, ny - 1, 0),
        pltpu.roll(plane, 1, 0),
        pltpu.roll(plane, nx - 1, 1),
        pltpu.roll(plane, 1, 1),
    )


def insides(shape):
    rows = lax.broadcasted_iota(jnp.int32, shape, 0)
    cols = lax.broadcasted_iota(jnp.int32, shape, 1)
    return (rows < shape[0] - 1, rows > 0, cols < shape[1] - 1, cols > 0)


def side_faces(centre, other):
    faces, total = [], None
    for near, inside in zip(shifts(other), insides(centre.shape)):
        near = jnp.where(inside, near, 0.0)
        faces.append(jnp.where(inside, centre + near, 0.0))
        total = near if total is None else total + near
    return faces, total


def dot_parts(rows, weights):
    count = rows.shape[0]
    high = rows.astype(BF16)
    rest = rows - high.astype(F32)
    middle = rest.astype(BF16)
    low = (rest - middle.astype(F32)).astype(BF16)
    out = jnp.dot(
        jnp.concatenate([high, middle, low], axis=0), weights, preferred_element_type=F32
    )
    return out[:count] + (out[count : 2 * count] + out[2 * count :])


def weights_of(shape, inner, outer):
    fine = lax.broadcasted_iota(jnp.int32, shape, 0)
    coarse = lax.broadcasted_iota(jnp.int32, shape, 1)
    apart = fine - 2 * coarse
    near = (apart == 0) | (apart == 1)
    far = (apart == -1) | (apart == 2)
    return jnp.where(near, inner, jnp.where(far, outer, 0.0)).astype(BF16)


def kernel(
    size,
    g_hbm, b_hbm, c_hbm,
    p_ref, mid_ref, low_ref,
    craw, graw, braw,
    cr, cb, gb, rr, dl, rho,
    fpair, fro, frs, fbo, fbs,
    dr, db, nr,
    zbuf, zmid, wres, wsum,
    send_m, send_q, send_c1, send_c2, send_2, send_3,
    halo_c, halo_m, halo_q, halo_c1, halo_c2, halo_2, halo_3,
    load_sem,
    s_c, s_m, s_q, s_c1, s_c2, s_2, s_3,
    r_c, r_m, r_q, r_c1, r_c2, r_2, r_3,
):
    me = lax.axis_index("gz")
    nz, ny, nx = craw.shape
    pairs = nz // 2
    plane = (ny, nx)
    plane1 = (ny // 2, nx // 2)
    plane2 = (ny // 4, nx // 4)
    has = (me > 0, me < size - 1)

    loads = [
        pltpu.make_async_copy(src, dst, load_sem.at[i])
        for i, (src, dst) in enumerate(((c_hbm, craw), (g_hbm, graw), (b_hbm, braw)))
    ]
    for load in loads:
        load.start()

    barrier = pltpu.get_barrier_semaphore()
    for side in range(2):
        @pl.when(has[side])
        def _(side=side):
            pl.semaphore_signal(
                barrier, inc=1, device_id=(me + 2 * side - 1,),
                device_id_type=pl.DeviceIdType.MESH,
            )

    for ref in (cr, cb, gb, rr, dl, rho):
        ref[0] = jnp.zeros(plane, F32)
        ref[pairs + 1] = jnp.zeros(plane, F32)
    dl[1] = jnp.zeros(plane, F32)
    dl[pairs] = jnp.zeros(plane, F32)
    for ref, depth in ((zbuf, ny), (zmid, ny // 2)):
        for i in range(ref.shape[0]):
            for j in range(ref.shape[1]):
                ref[i, j, 0:8] = jnp.zeros((8, 128), F32)
                ref[i, j, depth + 8 : depth + 16] = jnp.zeros((8, 128), F32)
    for side in range(2):
        @pl.when(jnp.logical_not(has[side]))
        def _(side=side):
            for ref in (halo_c, halo_q):
                ref[side] = jnp.zeros(ref.shape[1:], F32)
            for ref in (halo_m, halo_c1, halo_c2, halo_2, halo_3):
                for i in range(ref.shape[1]):
                    ref[side, i] = jnp.zeros(ref.shape[2:], F32)
    wres[...] = weights_of(wres.shape, 3.0, 1.0)
    wsum[...] = weights_of(wsum.shape, 1.0, 0.0)

    def copy_out(side, src, dst, s_sem, r_sem):
        return pltpu.make_async_remote_copy(
            src_ref=src, dst_ref=dst.at[1 - side], send_sem=s_sem.at[side],
            recv_sem=r_sem.at[1 - side], device_id=(me + 2 * side - 1,),
            device_id_type=pl.DeviceIdType.MESH,
        )

    def send(src_of, dst, s_sem, r_sem):
        for side in range(2):
            @pl.when(has[side])
            def _(side=side):
                copy_out(side, src_of(side), dst, s_sem, r_sem).start()

    def wait_recv(side, present, dst, s_sem, r_sem):
        @pl.when(present)
        def _():
            pltpu.make_async_remote_copy(
                src_ref=dst.at[side], dst_ref=dst.at[side], send_sem=s_sem.at[side],
                recv_sem=r_sem.at[side], device_id=(me + 2 * side - 1,),
                device_id_type=pl.DeviceIdType.MESH,
            ).wait_recv()

    even = parity(plane, 0)

    def even_first(first, second):
        return jnp.where(parity(plane, 0), first, second)

    loads[0].wait()

    def put_rows(ref, k, value):
        for j in range(ref.shape[1]):
            ref[k, j, 8 : value.shape[0] + 8] = value[:, 128 * j : 128 * j + 128]

    def get_rows(ref, k, start, count):
        return jnp.concatenate(
            [ref[k, j, pl.ds(start, count, stride=2), :] for j in range(ref.shape[1])], axis=1
        )

    def pack(k, carry):
        low, high = craw[2 * k], craw[2 * k + 1]
        cr[k + 1] = even_first(low, high)
        cb[k + 1] = even_first(high, low)
        put_rows(zbuf, k, low + high)
        return carry

    lax.fori_loop(0, pairs, pack, 0)
    pl.semaphore_wait(barrier, jnp.where(has[0] & has[1], 2, 1))
    send(lambda side: craw.at[(nz - 1) * side], halo_c, s_c, r_c)

    def faces(k, carry):
        own, other = cr[k + 1], cb[k + 1]
        fpair[k] = own + other
        outer = even_first(cb[k], cb[k + 2])
        sides, total = side_faces(own, other)
        fro[k] = own + outer
        for i in range(4):
            frs[k, i] = sides[i]
        dr[k] = 6.0 * own + other + outer + total
        outer = even_first(cr[k + 2], cr[k])
        sides, total = side_faces(other, own)
        fbo[k] = other + outer
        for i in range(4):
            fbs[k, i] = sides[i]
        db[k] = 6.0 * other + own + outer + total
        return carry

    lax.fori_loop(0, pairs, faces, 0)

    def gather(k, centre, outer, f_outer, f_sides):
        total = fpair[k] * centre + f_outer[k] * outer
        for i, near in enumerate(shifts(centre)):
            total = total + f_sides[k, i] * near
        return total

    loads[1].wait()
    loads[2].wait()

    def pack_g(k, carry):
        gb[k + 1] = even_first(graw[2 * k + 1], graw[2 * k])
        return carry

    lax.fori_loop(0, pairs, pack_g, 0)

    def red(k, carry):
        rhs = even_first(braw[2 * k], braw[2 * k + 1])
        off = gather(k, gb[k + 1], even_first(gb[k], gb[k + 2]), fro, frs)
        top = 2.0 * rhs + off
        nr[k] = top
        rr[k + 1] = top / dr[k]
        return carry

    lax.fori_loop(0, pairs, red, 0)

    for side in range(2):
        k = (pairs - 1) * side
        mine = parity(plane, side)
        send_m[side, 0] = jnp.where(mine, dr[k], db[k])
        send_m[side, 1] = jnp.where(mine, nr[k], gb[k + 1])
        rhs = even_first(braw[2 * k + 1], braw[2 * k])
        part = 2.0 * rhs + fpair[k] * rr[k + 1]
        half = ny // 2
        send_q[side] = jnp.where(
            parity((half, nx), side), pltpu.roll(part[half:], 1, 0), part[:half]
        )
    send(lambda side: send_m.at[side], halo_m, s_m, r_m)
    send(lambda side: send_q.at[side], halo_q, s_q, r_q)

    def put_pressure(k, reds, blacks):
        p_ref[2 * k] = even_first(reds, blacks)
        p_ref[2 * k + 1] = even_first(blacks, reds)

    def black(k, carry):
        rhs = even_first(braw[2 * k + 1], braw[2 * k])
        reds = rr[k + 1]
        off = gather(k, reds, even_first(rr[k + 2], rr[k]), fbo, fbs)
        new = (2.0 * rhs + off) / db[k]
        dl[k + 1] = new - gb[k + 1]
        put_pressure(k, reds, new)
        return carry

    lax.fori_loop(1, pairs - 1, black, 0)

    def residual(k, carry):
        rho[k + 1] = gather(k, dl[k + 1], even_first(dl[k], dl[k + 2]), fro, frs)
        return carry

    lax.fori_loop(1, pairs - 1, residual, 0)

    ny1, ny2 = ny // 2, ny // 4
    rows = [
        get_rows(zbuf, k, 8, ny1) + get_rows(zbuf, k, 9, ny1)
        for k in range(pairs)
    ]
    sums = 0.125 * dot_parts(jnp.concatenate(rows, axis=0), wsum[...])
    c1 = [sums[k * ny1 : (k + 1) * ny1] for k in range(pairs)]

    def plane_sum(value):
        total = None
        for near, inside in zip(shifts(value), insides(value.shape)):
            near = jnp.where(inside, near, 0.0)
            total = near if total is None else total + near
        return total

    def diagonals(coefs):
        out = []
        for k, coef in enumerate(coefs):
            total = 6.0 * coef + plane_sum(coef)
            if k > 0:
                total = total + coefs[k - 1]
            if k < len(coefs) - 1:
                total = total + coefs[k + 1]
            out.append(total)
        return out

    d1 = diagonals(c1)
    for k in range(pairs // 2):
        put_rows(zmid, k, c1[2 * k] + c1[2 * k + 1])
    rows = [
        get_rows(zmid, k, 8, ny2) + get_rows(zmid, k, 9, ny2)
        for k in range(pairs // 2)
    ]
    weights = wsum[0 : nx // 2, 0 : nx // 4]
    sums = 0.125 * dot_parts(jnp.concatenate(rows, axis=0), weights)
    c2 = [sums[k * ny2 : (k + 1) * ny2] for k in range(pairs // 2)]
    d2 = diagonals(c2)
    for side in range(2):
        send_c1[side, 0] = c1[-side]
        send_c1[side, 1] = d1[-side]
        send_c2[side, 0] = c2[-side]
        send_c2[side, 1] = d2[-side]
    send(lambda side: send_c1.at[side], halo_c1, s_c1, r_c1)
    send(lambda side: send_c2.at[side], halo_c2, s_c2, r_c2)

    def finish(step, carry):
        side = (step + 1 + me) % 2
        present = jnp.where(side == 0, me, size - 1 - me) > 0
        wait_recv(side, present, halo_c, s_c, r_c)
        wait_recv(side, present, halo_m, s_m, r_m)
        wait_recv(side, present, halo_q, s_q, r_q)
        k = (pairs - 1) * side
        here = (nz - 1) * side
        mine = parity(plane, side)
        inside = jnp.where(present, 1.0, 0.0)
        hc, hd, hm = halo_c[side], halo_m[side, 0], halo_m[side, 1]
        c0, g0 = craw[here], graw[here]
        face = c0 + hc
        top = jnp.where(mine, nr[k], hm) + face * jnp.where(mine, hm, g0)
        value = top / jnp.where(mine, dr[k] + hc, hd + c0)
        value = jnp.where(mine, value, inside * value)
        reds = jnp.where(mine, value, rr[k + 1])
        rr[k + 1] = reds
        hq = halo_q[side]
        off = jnp.concatenate([hq, pltpu.roll(hq, ny // 2 - 1, 0)], axis=0)
        off = off + face * value
        sides, _ = side_faces(hc, hc)
        for f, near in zip(sides, shifts(value)):
            off = off + f * near
        halo_delta = inside * (off / (hd + c0) - hm)

        rhs = even_first(braw[2 * k + 1], braw[2 * k])
        off = gather(k, reds, even_first(rr[k + 2], rr[k]), fbo, fbs)
        off = off + jnp.where(mine, 0.0, face * value)
        new = (2.0 * rhs + off) / (db[k] + jnp.where(mine, 0.0, hc))
        delta = new - gb[k + 1]
        dl[k + 1] = delta
        put_pressure(k, reds, new)

        off = gather(k, delta, even_first(dl[k], dl[k + 2]), fro, frs)
        rho[k + 1] = off + jnp.where(mine, face * halo_delta, 0.0)
        inner = k + 1 - 2 * side
        more = (cr[inner + 1] + cb[k + 1]) * delta
        rho[inner + 1] = rho[inner + 1] + jnp.where(mine, more, 0.0)
        return carry

    lax.fori_loop(0, 2, finish, 0)

    def thin(k, carry):
        put_rows(zbuf, k, 3.0 * rho[k + 1] + even_first(rho[k + 2], rho[k]))
        return carry

    lax.fori_loop(0, pairs, thin, 0)
    put_rows(zbuf, pairs, even_first(rho[1], 0.0))
    put_rows(zbuf, pairs + 1, even_first(0.0, rho[pairs]))

    def restrict(ref, count, out_rows, weights, scale):
        rows = [
            (get_rows(ref, k, 7, out_rows) + get_rows(ref, k, 10, out_rows))
            + 3.0 * (get_rows(ref, k, 8, out_rows) + get_rows(ref, k, 9, out_rows))
            for k in range(count)
        ]
        out = scale * dot_parts(jnp.concatenate(rows, axis=0), weights)
        return [out[k * out_rows : (k + 1) * out_rows] for k in range(count)]

    parts = restrict(zbuf, pairs + 2, ny1, wres[...], 0.5 ** 10)
    rhs1, edge1 = parts[:pairs], parts[pairs:]
    for side in range(2):
        k = (pairs - 1) * side
        inner = k + 1 - 2 * side
        send_2[side, 0] = rhs1[k]
        send_2[side, 1] = edge1[side]
        send_2[side, 2] = (c1[k] + c1[inner]) * (8.0 * rhs1[inner] / d1[inner])
    send(lambda side: send_2.at[side], halo_2, s_2, r_2)

    for side in range(2):
        wait_recv(side, has[side], halo_c1, s_c1, r_c1)
        wait_recv(side, has[side], halo_c2, s_c2, r_c2)
        wait_recv(side, has[side], halo_2, s_2, r_2)
    inside = [jnp.where(has[side], 1.0, 0.0) for side in range(2)]

    def with_ends(own, low, high):
        return [low] + list(own) + [high]

    def red_black(rhs, coefs, diags, seconds, factor, depth):
        masks = [parity(rhs[0].shape, i - 1) for i in range(depth + 2)]
        reds = []
        for i in range(depth + 2):
            value = jnp.where(masks[i], factor * rhs[i] / diags[i], 0.0)
            if i == 0:
                value = inside[0] * value
            if i == depth + 1:
                value = inside[1] * value
            reds.append(value)
        return masks, reds

    def off_of(coefs, fields, i):
        around = plane_sum(fields[i])
        weighted = plane_sum(coefs[i] * fields[i])
        for j in (i - 1, i + 1):
            if 0 <= j < len(fields):
                around = around + fields[j]
                weighted = weighted + coefs[j] * fields[j]
        return coefs[i] * around + weighted

    ends = [halo_2[0, 0] + edge1[0], halo_2[1, 0] + edge1[1]]
    rhs1[0] = rhs1[0] + halo_2[0, 1]
    rhs1[-1] = rhs1[-1] + halo_2[1, 1]
    d1 = with_ends(d1, halo_c1[0, 1] + c1[0], halo_c1[1, 1] + c1[-1])
    d1[1] = d1[1] + halo_c1[0, 0]
    d1[-2] = d1[-2] + halo_c1[1, 0]
    c1 = with_ends(c1, halo_c1[0, 0], halo_c1[1, 0])
    rhs1 = with_ends(rhs1, ends[0], ends[1])
    masks, reds = red_black(rhs1, c1, d1, None, 8.0, pairs)
    blacks = []
    for i in range(pairs + 2):
        top = 8.0 * rhs1[i] + off_of(c1, reds, i)
        if i == 0:
            top = inside[0] * (top + halo_2[0, 2])
        if i == pairs + 1:
            top = inside[1] * (top + halo_2[1, 2])
        blacks.append(jnp.where(masks[i], 0.0, top / d1[i]))
    for i in range(1, pairs + 1):
        mid_ref[i - 1] = reds[i] + blacks[i]
    res = [
        jnp.where(masks[i], off_of(c1, blacks, i), 0.0) for i in range(1, pairs + 1)
    ]

    put_rows(zmid, 0, 3.0 * (res[0] + res[1]) + res[2])
    put_rows(zmid, 1, 3.0 * (res[2] + res[3]) + res[1])
    put_rows(zmid, 2, res[0])
    put_rows(zmid, 3, res[3])
    parts = restrict(zmid, 4, ny2, wres[0 : nx // 2, 0 : nx // 4], 0.5 ** 12)
    rhs2, edge2 = parts[:2], parts[2:]
    for side in range(2):
        send_3[side, 0] = rhs2[side]
        send_3[side, 1] = edge2[side]
    send(lambda side: send_3.at[side], halo_3, s_3, r_3)
    for side in range(2):
        wait_recv(side, has[side], halo_3, s_3, r_3)
    ends = [halo_3[side, 0] + edge2[side] for side in range(2)]
    rhs2 = [rhs2[side] + halo_3[side, 1] for side in range(2)]
    d2 = with_ends(d2, halo_c2[0, 1] + c2[0], halo_c2[1, 1] + c2[1])
    d2[1] = d2[1] + halo_c2[0, 0]
    d2[2] = d2[2] + halo_c2[1, 0]
    c2 = with_ends(c2, halo_c2[0, 0], halo_c2[1, 0])
    rhs2 = with_ends(rhs2, ends[0], ends[1])
    masks, reds = red_black(rhs2, c2, d2, None, 32.0, 2)
    for i in (1, 2):
        top = 32.0 * rhs2[i] + off_of(c2, reds, i)
        low_ref[i - 1] = jnp.where(masks[i], reds[i], top / d2[i])

    for side in range(2):
        @pl.when(has[side])
        def _(side=side):
            for src, dst, s_sem, r_sem in (
                (craw.at[(nz - 1) * side], halo_c, s_c, r_c),
                (send_m.at[side], halo_m, s_m, r_m),
                (send_q.at[side], halo_q, s_q, r_q),
                (send_c1.at[side], halo_c1, s_c1, r_c1),
                (send_c2.at[side], halo_c2, s_c2, r_c2),
                (send_2.at[side], halo_2, s_2, r_2),
                (send_3.at[side], halo_3, s_3, r_3),
            ):
                copy_out(side, src, dst, s_sem, r_sem).wait_send()


def on_device(size, pressure_guess, source, conductance):
    nz, ny, nx = pressure_guess.shape
    pairs = nz // 2
    ny1, nx1, ny2, nx2 = ny // 2, nx // 2, ny // 4, nx // 4

    def vmem(*shape):
        return pltpu.VMEM(shape, F32)

    slab = [vmem(nz, ny, nx)] * 3
    padded = [vmem(pairs + 2, ny, nx)] * 6
    faces = [
        vmem(pairs, ny, nx), vmem(pairs, ny, nx), vmem(pairs, 4, ny, nx),
        vmem(pairs, ny, nx), vmem(pairs, 4, ny, nx),
    ]
    sums = [vmem(pairs, ny, nx)] * 3
    work = [
        vmem(pairs + 2, nx // 128, ny + 16, 128), vmem(4, nx1 // 128, ny1 + 16, 128),
        pltpu.VMEM((nx, nx1), BF16), pltpu.VMEM((nx, nx1), BF16),
    ]
    messages = [
        vmem(2, 2, ny, nx), vmem(2, ny1, nx), vmem(2, 2, ny1, nx1), vmem(2, 2, ny2, nx2),
        vmem(2, 3, ny1, nx1), vmem(2, 2, ny2, nx2),
    ]
    halos = [vmem(2, ny, nx)] + messages
    sems = [pltpu.SemaphoreType.DMA((3,))] + [pltpu.SemaphoreType.DMA((2,))] * 14

    def run(*refs):
        kernel(size, *refs)

    return pl.pallas_call(
        run,
        out_shape=(
            jax.ShapeDtypeStruct((nz, ny, nx), F32),
            jax.ShapeDtypeStruct((pairs, ny1, nx1), F32),
            jax.ShapeDtypeStruct((pairs // 2, ny2, nx2), F32),
        ),
        in_specs=[pl.BlockSpec(memory_space=pl.ANY)] * 3,
        out_specs=tuple([pl.BlockSpec(memory_space=pltpu.VMEM)] * 3),
        scratch_shapes=slab + padded + faces + sums + work + messages + halos + sems,
        compiler_params=pltpu.CompilerParams(
            collective_id=0, has_side_effects=True, vmem_limit_bytes=48 * 2 ** 20
        ),
    )(pressure_guess, source, conductance)


def solution(mesh):
    size = mesh.shape["gz"]
    spec = P("gz", None, None)
    return jax.shard_map(
        lambda *args: on_device(size, *args), mesh=mesh,
        in_specs=(spec, spec, spec), out_specs=(spec, spec, spec), check_vma=False,
    )
```

time: 306 us -> 34 us (0.11)
  starting transfers between devices: 118 us -> 0 us
  local copies, waits for them, and re-layouts: 105 us -> 5.9 us
  other arithmetic: 46.3 us -> 0 us
  waiting for transfers between devices: 34 us -> 0 us
  Pallas kernels: 0 us -> 27.3 us
    ppermute x26 -> x0, starting transfers between devices: 118 us -> none  [the longest x13 91.7 us: with_halo(): after = lax.ppermute(first, axis, down)]
    reshape x1 -> x0, local copies, waits for them, and re-layouts: 68.4 us -> none  [coarsen(): grouped = cond.reshape(depth // 2, 2, rows // 2, 2, cols // 2, 2)]
    ppermute x26 -> x0, waiting for transfers between devices: 34 us -> none  [the longest x13 32 us: with_halo(): before = lax.ppermute(last, axis, up)]
    pallas_call x0 -> x1, Pallas kernels: none -> 27.3 us  [on_device(): pl.pallas_call(run, out_shape=(jax.ShapeDtypeStruct((nz, ny, nx), F32), j...]
    reduce_sum x2 -> x0, other arithmetic: 26.1 us -> none  [coarsen(): return 0.125 * jnp.sum(grouped, axis=(1, 3, 5))]
    slice x26 -> x0, local copies, waits for them, and re-layouts: 24.5 us -> none  [the longest x16 21 us: restrict_axis(): lax.slice_in_dim(padded, start, start + count - 1, 2, axis)]
    mul x1 -> x0, local copies, waits for them, and re-layouts: 9.8 us -> none  [coarsen(): return 0.125 * jnp.sum(grouped, axis=(1, 3, 5))]
    select_n x6 -> x0, other arithmetic: 9.3 us -> none  [the longest x3 4.95 us: smooth(): field = jnp.where(red, field, (rhs / scale + off) / diag)]
  transfers between devices with their start and end apart: 26 -> 0, of which waited for: 7 -> 0; matrix products, arithmetic and copies ran while one was open for 41% -> 0% of each run, Pallas kernels for 0% -> 0%
where the time goes in v1:
time: 34 us; the launch traced here: 33.8 us
  Pallas kernels  27.3 us (80%)
  local copies, waits for them, and re-layouts  5.9 us (17%)
  between operations  0.65 us (2%)
    pallas_call x1, Pallas kernels, on_device(): pl.pallas_call(run, out_shape=(jax.ShapeDtypeStruct((nz, ny, nx), F32), j...  27.3 us
    unnamed x9, local copies, waits for them, and re-layouts  5.9 us

profile of v1, /device:TPU:24, one launch (start us, length us, event | category | flops | bytes accessed | tf_op | source)
XLA Modules:
  0.0 33.8 jit_solution(4636689553372162439)
XLA Ops:
  0.6 0.0 copy-start
  0.6 1.2 %copy-done = f32[8,64,512]{2,1,0:T(8,128)S(1)} copy-done((f32[8,64,512]{2,1,0:T(8,128)S(1)}, f32[8,64,512]{2,1,0:T(8,128)}, u32[]{:S(2)}) %copy-start) | copy-done | bytes 1048600
  1.9 0.0 copy-start.1
  1.9 1.2 %copy-done.1 = f32[8,64,512]{2,1,0:T(8,128)S(1)} copy-done((f32[8,64,512]{2,1,0:T(8,128)S(1)}, f32[8,64,512]{2,1,0:T(8,128)}, u32[]{:S(2)}) %copy-start.1) | copy-done | bytes 1048600
  3.1 0.0 copy-start.2
  3.1 1.2 %copy-done.2 = f32[8,64,512]{2,1,0:T(8,128)S(1)} copy-done((f32[8,64,512]{2,1,0:T(8,128)S(1)}, f32[8,64,512]{2,1,0:T(8,128)}, u32[]{:S(2)}) %copy-start.2) | copy-done | bytes 1048600
  4.3 27.3 %shard_map.58 = (f32[8,64,512]{2,1,0:T(8,128)S(1)}, f32[4,32,256]{2,1,0:T(8,128)S(1)}, f32[2,16,128]{2,1,0:T(8,128)S(1)}) custom-call(f32[8,64,512]{2,1,0:T(8,128)S(1)} %copy-done, f32[8,64,512]{2,1,0:T(8,128)S(1)} %copy-done.1, f32[8,64,512]{2,1,0:T(8,128)S(1)} %copy-done.2), custom_call_target="tpu_custom_call" | custom-call | tf_op jit(solution)/shard_map/pallas_call | solution.py:488
  31.6 1.0 %copy.9 = f32[8,64,512]{2,1,0:T(8,128)} copy(f32[8,64,512]{2,1,0:T(8,128)S(1)} %get-tuple-element.6) | data formatting | bytes 2097152
  32.6 0.7 %copy.10 = f32[4,32,256]{2,1,0:T(8,128)} copy(f32[4,32,256]{2,1,0:T(8,128)S(1)} %get-tuple-element.7) | data formatting | bytes 262144
  33.2 0.6 %copy.11 = f32[2,16,128]{2,1,0:T(8,128)} copy(f32[2,16,128]{2,1,0:T(8,128)S(1)} %get-tuple-element.8) | data formatting | bytes 32768
Async XLA Ops:
  0.6 1.2 %copy-start = (f32[8,64,512]{2,1,0:T(8,128)S(1)}, f32[8,64,512]{2,1,0:T(8,128)}, u32[]{:S(2)}) copy-start(f32[8,64,512]{2,1,0:T(8,128)} %refs_0_.1) | copy-start | bytes 3145732
  1.9 1.2 %copy-start.1 = (f32[8,64,512]{2,1,0:T(8,128)S(1)}, f32[8,64,512]{2,1,0:T(8,128)}, u32[]{:S(2)}) copy-start(f32[8,64,512]{2,1,0:T(8,128)} %refs_1_.1) | copy-start | bytes 3145732
  3.1 1.2 %copy-start.2 = (f32[8,64,512]{2,1,0:T(8,128)S(1)}, f32[8,64,512]{2,1,0:T(8,128)}, u32[]{:S(2)}) copy-start(f32[8,64,512]{2,1,0:T(8,128)} %refs_2_.1) | copy-start | bytes 3145732

commit v2 on v1

--- a/solution.py
+++ b/solution.py
@@ -70,11 +70,12 @@
     fpair, fro, frs, fbo, fbs,
     dr, db, nr,
     zbuf, zmid, wres, wsum,
-    send_m, send_q, send_c1, send_c2, send_2, send_3,
-    halo_c, halo_m, halo_q, halo_c1, halo_c2, halo_2, halo_3,
+    v1, cof1, dia1,
+    send_d, send_m, send_q, send_c1, send_c2, send_2, send_3,
+    halo_c, halo_d, halo_m, halo_q, halo_c1, halo_c2, halo_2, halo_3,
     load_sem,
-    s_c, s_m, s_q, s_c1, s_c2, s_2, s_3,
-    r_c, r_m, r_q, r_c1, r_c2, r_2, r_3,
+    s_c, s_d, s_m, s_q, s_c1, s_c2, s_2, s_3,
+    r_c, r_d, r_m, r_q, r_c1, r_c2, r_2, r_3,
 ):
     me = lax.axis_index("gz")
     nz, ny, nx = craw.shape
@@ -113,9 +114,9 @@
     for side in range(2):
         @pl.when(jnp.logical_not(has[side]))
         def _(side=side):
-            for ref in (halo_c, halo_q):
+            for ref in (halo_c, halo_d, halo_m, halo_q):
                 ref[side] = jnp.zeros(ref.shape[1:], F32)
-            for ref in (halo_m, halo_c1, halo_c2, halo_2, halo_3):
+            for ref in (halo_c1, halo_c2, halo_2, halo_3):
                 for i in range(ref.shape[1]):
                     ref[side, i] = jnp.zeros(ref.shape[2:], F32)
     wres[...] = weights_of(wres.shape, 3.0, 1.0)
@@ -187,22 +188,15 @@
         db[k] = 6.0 * other + own + outer + total
         return carry
 
-    lax.fori_loop(0, pairs, faces, 0)
-
     def gather(k, centre, outer, f_outer, f_sides):
         total = fpair[k] * centre + f_outer[k] * outer
         for i, near in enumerate(shifts(centre)):
             total = total + f_sides[k, i] * near
         return total
 
-    loads[1].wait()
-    loads[2].wait()
-
     def pack_g(k, carry):
         gb[k + 1] = even_first(graw[2 * k + 1], graw[2 * k])
         return carry
-
-    lax.fori_loop(0, pairs, pack_g, 0)
 
     def red(k, carry):
         rhs = even_first(braw[2 * k], braw[2 * k + 1])
@@ -212,21 +206,43 @@
         rr[k + 1] = top / dr[k]
         return carry
 
-    lax.fori_loop(0, pairs, red, 0)
-
-    for side in range(2):
+    def put_diagonal(side, carry):
         k = (pairs - 1) * side
-        mine = parity(plane, side)
-        send_m[side, 0] = jnp.where(mine, dr[k], db[k])
-        send_m[side, 1] = jnp.where(mine, nr[k], gb[k + 1])
+        send_d[side] = jnp.where(parity(plane, side), dr[k], db[k])
+        return carry
+
+    def put_field(side, carry):
+        k = (pairs - 1) * side
+        send_m[side] = jnp.where(parity(plane, side), nr[k], gb[k + 1])
+        return carry
+
+    def put_second(side, carry):
+        k = (pairs - 1) * side
         rhs = even_first(braw[2 * k + 1], braw[2 * k])
         part = 2.0 * rhs + fpair[k] * rr[k + 1]
         half = ny // 2
         send_q[side] = jnp.where(
             parity((half, nx), side), pltpu.roll(part[half:], 1, 0), part[:half]
         )
+        return carry
+
+    def at_ends(body):
+        lax.fori_loop(0, 2, lambda i, carry: body((pairs - 1) * i, carry), 0)
+
+    at_ends(faces)
+    lax.fori_loop(0, 2, put_diagonal, 0)
+    send(lambda side: send_d.at[side], halo_d, s_d, r_d)
+    loads[1].wait()
+    lax.fori_loop(0, pairs, pack_g, 0)
+    loads[2].wait()
+    at_ends(red)
+    lax.fori_loop(0, 2, put_field, 0)
     send(lambda side: send_m.at[side], halo_m, s_m, r_m)
+    lax.fori_loop(0, 2, put_second, 0)
     send(lambda side: send_q.at[side], halo_q, s_q, r_q)
+
+    lax.fori_loop(1, pairs - 1, faces, 0)
+    lax.fori_loop(1, pairs - 1, red, 0)
 
     def put_pressure(k, reds, blacks):
         p_ref[2 * k] = even_first(reds, blacks)
@@ -276,6 +292,9 @@
         return out
 
     d1 = diagonals(c1)
+    for k in range(pairs):
+        cof1[k] = c1[k]
+        dia1[k] = d1[k]
     for k in range(pairs // 2):
         put_rows(zmid, k, c1[2 * k] + c1[2 * k + 1])
     rows = [
@@ -294,17 +313,27 @@
     send(lambda side: send_c1.at[side], halo_c1, s_c1, r_c1)
     send(lambda side: send_c2.at[side], halo_c2, s_c2, r_c2)
 
+    def restrict(ref, count, out_rows, weights, scale):
+        rows = [
+            (get_rows(ref, k, 7, out_rows) + get_rows(ref, k, 10, out_rows))
+            + 3.0 * (get_rows(ref, k, 8, out_rows) + get_rows(ref, k, 9, out_rows))
+            for k in range(count)
+        ]
+        out = scale * dot_parts(jnp.concatenate(rows, axis=0), weights)
+        return [out[k * out_rows : (k + 1) * out_rows] for k in range(count)]
+
     def finish(step, carry):
         side = (step + 1 + me) % 2
         present = jnp.where(side == 0, me, size - 1 - me) > 0
         wait_recv(side, present, halo_c, s_c, r_c)
+        wait_recv(side, present, halo_d, s_d, r_d)
         wait_recv(side, present, halo_m, s_m, r_m)
         wait_recv(side, present, halo_q, s_q, r_q)
         k = (pairs - 1) * side
         here = (nz - 1) * side
         mine = parity(plane, side)
         inside = jnp.where(present, 1.0, 0.0)
-        hc, hd, hm = halo_c[side], halo_m[side, 0], halo_m[side, 1]
+        hc, hd, hm = halo_c[side], halo_d[side], halo_m[side]
         c0, g0 = craw[here], graw[here]
         face = c0 + hc
         top = jnp.where(mine, nr[k], hm) + face * jnp.where(mine, hm, g0)
@@ -333,37 +362,27 @@
         inner = k + 1 - 2 * side
         more = (cr[inner + 1] + cb[k + 1]) * delta
         rho[inner + 1] = rho[inner + 1] + jnp.where(mine, more, 0.0)
+
+        for i, at in enumerate((k, inner)):
+            put_rows(zbuf, i, 3.0 * rho[at + 1] + even_first(rho[at + 2], rho[at]))
+        put_rows(zbuf, 2, jnp.where(mine, rho[k + 1], 0.0))
+        parts = restrict(zbuf, 3, ny1, wres[...], 0.5 ** 10)
+        for i in range(3):
+            v1[side, i] = parts[i]
+        send_2[side, 0] = parts[0]
+        send_2[side, 1] = parts[2]
+        send_2[side, 2] = (cof1[k] + cof1[inner]) * (8.0 * parts[1] / dia1[inner])
+
+        @pl.when(present)
+        def _():
+            copy_out(side, send_2.at[side], halo_2, s_2, r_2).start()
+
         return carry
 
     lax.fori_loop(0, 2, finish, 0)
 
-    def thin(k, carry):
-        put_rows(zbuf, k, 3.0 * rho[k + 1] + even_first(rho[k + 2], rho[k]))
-        return carry
-
-    lax.fori_loop(0, pairs, thin, 0)
-    put_rows(zbuf, pairs, even_first(rho[1], 0.0))
-    put_rows(zbuf, pairs + 1, even_first(0.0, rho[pairs]))
-
-    def restrict(ref, count, out_rows, weights, scale):
-        rows = [
-            (get_rows(ref, k, 7, out_rows) + get_rows(ref, k, 10, out_rows))
-            + 3.0 * (get_rows(ref, k, 8, out_rows) + get_rows(ref, k, 9, out_rows))
-            for k in range(count)
-        ]
-        out = scale * dot_parts(jnp.concatenate(rows, axis=0), weights)
-        return [out[k * out_rows : (k + 1) * out_rows] for k in range(count)]
-
-    parts = restrict(zbuf, pairs + 2, ny1, wres[...], 0.5 ** 10)
-    rhs1, edge1 = parts[:pairs], parts[pairs:]
-    for side in range(2):
-        k = (pairs - 1) * side
-        inner = k + 1 - 2 * side
-        send_2[side, 0] = rhs1[k]
-        send_2[side, 1] = edge1[side]
-        send_2[side, 2] = (c1[k] + c1[inner]) * (8.0 * rhs1[inner] / d1[inner])
-    send(lambda side: send_2.at[side], halo_2, s_2, r_2)
-
+    rhs1 = [v1[0, 0], v1[0, 1], v1[1, 1], v1[1, 0]]
+    edge1 = [v1[0, 2], v1[1, 2]]
     for side in range(2):
         wait_recv(side, has[side], halo_c1, s_c1, r_c1)
         wait_recv(side, has[side], halo_c2, s_c2, r_c2)
@@ -446,6 +465,7 @@
         def _(side=side):
             for src, dst, s_sem, r_sem in (
                 (craw.at[(nz - 1) * side], halo_c, s_c, r_c),
+                (send_d.at[side], halo_d, s_d, r_d),
                 (send_m.at[side], halo_m, s_m, r_m),
                 (send_q.at[side], halo_q, s_q, r_q),
                 (send_c1.at[side], halo_c1, s_c1, r_c1),
@@ -474,31 +494,51 @@
     work = [
         vmem(pairs + 2, nx // 128, ny + 16, 128), vmem(4, nx1 // 128, ny1 + 16, 128),
         pltpu.VMEM((nx, nx1), BF16), pltpu.VMEM((nx, nx1), BF16),
+        vmem(2, 3, ny1, nx1), vmem(pairs, ny1, nx1), vmem(pairs, ny1, nx1),
     ]
     messages = [
-        vmem(2, 2, ny, nx), vmem(2, ny1, nx), vmem(2, 2, ny1, nx1), vmem(2, 2, ny2, nx2),
+        vmem(2, ny, nx), vmem(2, ny, nx), vmem(2, ny1, nx), vmem(2, 2, ny1, nx1), vmem(2, 2, ny2, nx2),
         vmem(2, 3, ny1, nx1), vmem(2, 2, ny2, nx2),
     ]
     halos = [vmem(2, ny, nx)] + messages
-    sems = [pltpu.SemaphoreType.DMA((3,))] + [pltpu.SemaphoreType.DMA((2,))] * 14
+    sems = [pltpu.SemaphoreType.DMA((3,))] + [pltpu.SemaphoreType.DMA((2,))] * 16
 
     def run(*refs):
         kernel(size, *refs)
 
-    return pl.pallas_call(
+    shapes = ((nz, ny, nx), (pairs, ny1, nx1), (pairs // 2, ny2, nx2))
+    inputs = [
+        pltpu.with_memory_space_constraint(value, pltpu.HBM)
+        for value in (pressure_guess, source, conductance)
+    ]
+    results = pl.pallas_call(
         run,
-        out_shape=(
-            jax.ShapeDtypeStruct((nz, ny, nx), F32),
-            jax.ShapeDtypeStruct((pairs, ny1, nx1), F32),
-            jax.ShapeDtypeStruct((pairs // 2, ny2, nx2), F32),
-        ),
+        out_shape=tuple(pltpu.VMEM(shape, F32) for shape in shapes),
         in_specs=[pl.BlockSpec(memory_space=pl.ANY)] * 3,
         out_specs=tuple([pl.BlockSpec(memory_space=pltpu.VMEM)] * 3),
         scratch_shapes=slab + padded + faces + sums + work + messages + halos + sems,
         compiler_params=pltpu.CompilerParams(
             collective_id=0, has_side_effects=True, vmem_limit_bytes=48 * 2 ** 20
         ),
-    )(pressure_guess, source, conductance)
+    )(*inputs)
+    return pl.pallas_call(
+        write_out,
+        out_shape=tuple(jax.ShapeDtypeStruct(shape, F32) for shape in shapes),
+        in_specs=[pl.BlockSpec(memory_space=pl.ANY)] * 3,
+        out_specs=tuple([pl.BlockSpec(memory_space=pl.ANY)] * 3),
+        scratch_shapes=[pltpu.SemaphoreType.DMA((3,))],
+    )(*[pltpu.with_memory_space_constraint(value, pltpu.VMEM) for value in results])
+
+
+def write_out(p_src, mid_src, low_src, p_dst, mid_dst, low_dst, sem):
+    copies = [
+        pltpu.make_async_copy(src, dst, sem.at[i])
+        for i, (src, dst) in enumerate(((p_src, p_dst), (mid_src, mid_dst), (low_src, low_dst)))
+    ]
+    for copy in copies:
+        copy.start()
+    for copy in copies:
+        copy.wait()
 
 
 def solution(mesh):

time: 34 us -> 29 us (0.85)
  local copies, waits for them, and re-layouts: 5.9 us -> 0 us
  Pallas kernels: 27.3 us -> 28.3 us
    unnamed x9 -> x0, local copies, waits for them, and re-layouts: 5.9 us -> none
    pallas_call x1 -> x2, Pallas kernels: 27.3 us -> 28.3 us  [the longest x1 27.2 us: on_device(): pl.pallas_call(run, out_shape=tuple((pltpu.VMEM(shape, F32) for shape in...]
where the time goes in v2:
time: 29 us; the launch traced here: 28.9 us
  Pallas kernels  28.3 us (98%)
  between operations  0.64 us (2%)
    pallas_call x1, Pallas kernels, on_device(): pl.pallas_call(run, out_shape=tuple((pltpu.VMEM(shape, F32) for shape in...  27.2 us
    pallas_call x1, Pallas kernels, on_device(): pl.pallas_call(write_out, out_shape=tuple((jax.ShapeDtypeStruct(shape, F3...  1.03 us

profile of v2, /device:TPU:24, one launch (start us, length us, event | category | flops | bytes accessed | tf_op | source)
XLA Modules:
  0.0 28.9 jit_solution(1564759810832559593)
XLA Ops:
  0.6 27.2 %shard_map.58 = (f32[8,64,512]{2,1,0:T(8,128)S(1)}, f32[4,32,256]{2,1,0:T(8,128)S(1)}, f32[2,16,128]{2,1,0:T(8,128)S(1)}) custom-call(f32[8,64,512]{2,1,0:T(8,128)} %refs_0_.1, f32[8,64,512]{2,1,0:T(8,128)} %refs_1_.1, f32[8,64,512]{2,1,0:T(8,128)} %refs_2_.1), custom_call_target="tpu_custom_call" | custom-call | tf_op jit(solution)/shard_map/pallas_call | solution.py:514
  27.9 1.0 %shard_map.59 = (f32[8,64,512]{2,1,0:T(8,128)}, f32[4,32,256]{2,1,0:T(8,128)}, f32[2,16,128]{2,1,0:T(8,128)}) custom-call(f32[8,64,512]{2,1,0:T(8,128)S(1)} %get-tuple-element.6.p_src, f32[4,32,256]{2,1,0:T(8,128)S(1)} %get-tuple-element.7.mid_src, f32[2,16,128]{2,1,0:T(8,128)S(1)} %get-tuple-element.8.low_src), custom_call_target="tpu_custom_call" | custom-call | tf_op jit(solution)/shard_map/pallas_call | solution.py:524

commit v3 on v2

--- a/solution.py
+++ b/solution.py
@@ -71,11 +71,12 @@
     dr, db, nr,
     zbuf, zmid, wres, wsum,
     v1, cof1, dia1,
+    cof2, dia2,
     send_d, send_m, send_q, send_c1, send_c2, send_2, send_3,
-    halo_c, halo_d, halo_m, halo_q, halo_c1, halo_c2, halo_2, halo_3,
+    halo_c, halo_d, halo_m, halo_q, halo_c1, halo_c2, halo_2, halo_n, halo_f, halo_3,
     load_sem,
-    s_c, s_d, s_m, s_q, s_c1, s_c2, s_2, s_3,
-    r_c, r_d, r_m, r_q, r_c1, r_c2, r_2, r_3,
+    s_c, s_d, s_m, s_q, s_c1, s_c2, s_2, s_n, s_f, s_3,
+    r_c, r_d, r_m, r_q, r_c1, r_c2, r_2, r_n, r_f, r_3,
 ):
     me = lax.axis_index("gz")
     nz, ny, nx = craw.shape
@@ -84,6 +85,9 @@
     plane1 = (ny // 2, nx // 2)
     plane2 = (ny // 4, nx // 4)
     has = (me > 0, me < size - 1)
+    far = me % 2
+    near = 1 - far
+    has_far = jnp.where(far == 0, me, size - 1 - me) > 0
 
     loads = [
         pltpu.make_async_copy(src, dst, load_sem.at[i])
@@ -116,7 +120,7 @@
         def _(side=side):
             for ref in (halo_c, halo_d, halo_m, halo_q):
                 ref[side] = jnp.zeros(ref.shape[1:], F32)
-            for ref in (halo_c1, halo_c2, halo_2, halo_3):
+            for ref in (halo_c1, halo_c2, halo_2, halo_f):
                 for i in range(ref.shape[1]):
                     ref[side, i] = jnp.zeros(ref.shape[2:], F32)
     wres[...] = weights_of(wres.shape, 3.0, 1.0)
@@ -305,11 +309,15 @@
     sums = 0.125 * dot_parts(jnp.concatenate(rows, axis=0), weights)
     c2 = [sums[k * ny2 : (k + 1) * ny2] for k in range(pairs // 2)]
     d2 = diagonals(c2)
+    for k in range(2):
+        cof2[k] = c2[k]
+        dia2[k] = d2[k]
     for side in range(2):
-        send_c1[side, 0] = c1[-side]
-        send_c1[side, 1] = d1[-side]
-        send_c2[side, 0] = c2[-side]
-        send_c2[side, 1] = d2[-side]
+        ends = (3 * side, 1 + side, 2 - side)
+        for i, value in enumerate((c1[ends[0]], d1[ends[0]], c1[ends[1]], d1[ends[1]], c1[ends[2]])):
+            send_c1[side, i] = value
+        send_c2[side, 0] = c2[side]
+        send_c2[side, 1] = d2[side]
     send(lambda side: send_c1.at[side], halo_c1, s_c1, r_c1)
     send(lambda side: send_c2.at[side], halo_c2, s_c2, r_c2)
 
@@ -323,8 +331,8 @@
         return [out[k * out_rows : (k + 1) * out_rows] for k in range(count)]
 
     def finish(step, carry):
-        side = (step + 1 + me) % 2
-        present = jnp.where(side == 0, me, size - 1 - me) > 0
+        side = jnp.where(step == 0, near, far)
+        present = (step == 0) | has_far
         wait_recv(side, present, halo_c, s_c, r_c)
         wait_recv(side, present, halo_d, s_d, r_d)
         wait_recv(side, present, halo_m, s_m, r_m)
@@ -345,8 +353,8 @@
         off = jnp.concatenate([hq, pltpu.roll(hq, ny // 2 - 1, 0)], axis=0)
         off = off + face * value
         sides, _ = side_faces(hc, hc)
-        for f, near in zip(sides, shifts(value)):
-            off = off + f * near
+        for f, shifted in zip(sides, shifts(value)):
+            off = off + f * shifted
         halo_delta = inside * (off / (hd + c0) - hm)
 
         rhs = even_first(braw[2 * k + 1], braw[2 * k])
@@ -375,105 +383,150 @@
 
         @pl.when(present)
         def _():
-            copy_out(side, send_2.at[side], halo_2, s_2, r_2).start()
+            copy_out(side, send_2.at[side, 0:2], halo_2, s_2, r_2).start()
+
+        @pl.when(step == 0)
+        def _():
+            copy_out(side, send_2.at[side, 2], halo_n, s_n, r_n).start()
 
         return carry
 
     lax.fori_loop(0, 2, finish, 0)
 
-    rhs1 = [v1[0, 0], v1[0, 1], v1[1, 1], v1[1, 0]]
-    edge1 = [v1[0, 2], v1[1, 2]]
+    def mask1(j):
+        return parity(plane1, j + far + 4)
+
+    def at1(j):
+        return 3 * far + j * (1 - 2 * far)
+
+    inside = jnp.where(has_far, 1.0, 0.0)
+    true = me >= 0
+    cof = {j: cof1[at1(j)] for j in range(4)}
+    dia = {j: dia1[at1(j)] for j in range(4)}
+
+    def flat(j, field):
+        return cof[j] * plane_sum(field) + plane_sum(cof[j] * field)
+
+    def across(i, j, field):
+        return (cof[i] + cof[j]) * field
+
+    def red_of(j, right):
+        return jnp.where(mask1(j), 8.0 * right / dia[j], 0.0)
+
+    def black_of(j, top):
+        return jnp.where(mask1(j), 0.0, top / dia[j])
+
+    wait_recv(near, true, halo_c1, s_c1, r_c1)
+    wait_recv(near, true, halo_2, s_2, r_2)
+    wait_recv(near, true, halo_n, s_n, r_n)
+    cof[4] = halo_c1[near, 0]
+    dia[4] = halo_c1[near, 1] + cof[3]
+    dia[3] = dia[3] + cof[4]
+    rhs = {
+        4: halo_2[near, 0] + v1[near, 2],
+        3: v1[near, 0] + halo_2[near, 1],
+        2: v1[near, 1],
+        1: v1[far, 1],
+    }
+    red = {j: red_of(j, rhs[j]) for j in (1, 2, 3, 4)}
+    black = {}
+    black[4] = black_of(4, 8.0 * rhs[4] + halo_n[near] + flat(4, red[4]) + across(4, 3, red[3]))
+    for j in (3, 2):
+        black[j] = black_of(
+            j, 8.0 * rhs[j] + flat(j, red[j]) + across(j, j + 1, red[j + 1]) + across(j, j - 1, red[j - 1])
+        )
+    part1 = 8.0 * rhs[1] + flat(1, red[1]) + across(1, 2, red[2])
+    part2 = flat(2, black[2]) + across(2, 3, black[3])
+    cross = across(1, 2, black[2])
+    send_2[far, 2] = jnp.where(mask1(0), part2, across(0, 1, red[1]))
+    send_2[far, 3] = jnp.where(mask1(1), cross, part1)
+
+    @pl.when(has_far)
+    def _():
+        copy_out(far, send_2.at[far, 2:4], halo_f, s_f, r_f).start()
+
+    wait_recv(far, has_far, halo_c1, s_c1, r_c1)
+    cof.update({-1: halo_c1[far, 0], -2: halo_c1[far, 2], -3: halo_c1[far, 4]})
+    dia.update({-1: halo_c1[far, 1] + cof[0], -2: halo_c1[far, 3], 0: dia[0] + cof[-1]})
+    wait_recv(far, has_far, halo_2, s_2, r_2)
+    rhs[0] = v1[far, 0] + halo_2[far, 1]
+    rhs[-1] = halo_2[far, 0] + v1[far, 2]
+    red[0] = red_of(0, rhs[0])
+    red[-1] = inside * red_of(-1, rhs[-1])
+    black[0] = black_of(0, 8.0 * rhs[0] + flat(0, red[0]) + across(0, -1, red[-1]) + across(0, 1, red[1]))
+    black[1] = black_of(1, part1 + across(1, 0, red[0]))
+    wait_recv(far, has_far, halo_f, s_f, r_f)
+    black[-1] = inside * black_of(-1, 8.0 * rhs[-1] + halo_f[far, 0] + flat(-1, red[-1]) + across(-1, 0, red[0]))
+    black[-2] = inside * black_of(-2, halo_f[far, 1] + across(-2, -1, red[-1]))
+    res = {
+        3: flat(3, black[3]) + across(3, 2, black[2]) + across(3, 4, black[4]),
+        2: part2 + across(2, 1, black[1]),
+        1: flat(1, black[1]) + across(1, 0, black[0]) + cross,
+        0: flat(0, black[0]) + across(0, -1, black[-1]) + across(0, 1, black[1]),
+        -1: flat(-1, black[-1]) + across(-1, -2, black[-2]) + across(-1, 0, black[0]),
+        -2: halo_f[far, 1] + flat(-2, black[-2]) + across(-2, -1, black[-1]),
+        -3: halo_f[far, 0] + across(-3, -2, black[-2]),
+    }
+    res = {
+        j: jnp.where(mask1(j) if j >= 0 else mask1(j) & has_far, value, 0.0)
+        for j, value in res.items()
+    }
+
+    put_rows(zmid, 0, 3.0 * (res[3] + res[2]) + res[1])
+    put_rows(zmid, 1, res[3])
+    put_rows(zmid, 2, 3.0 * (res[0] + res[1]) + (res[-1] + res[2]))
+    put_rows(zmid, 3, 3.0 * (res[-1] + res[-2]) + (res[0] + res[-3]))
+    parts = restrict(zmid, 4, ny2, wres[0 : nx // 2, 0 : nx // 4], 0.5 ** 12)
+    send_3[0] = parts[0]
+    send_3[1] = parts[1]
+    copy_out(near, send_3, halo_3, s_3, r_3).start()
+    for j in range(4):
+        mid_ref[at1(j)] = red[j] + black[j]
+
+    wait_recv(near, true, halo_c2, s_c2, r_c2)
+    wait_recv(far, has_far, halo_c2, s_c2, r_c2)
+    wait_recv(near, true, halo_3, s_3, r_3)
+
+    def mask2(j):
+        return parity(plane2, j + far + 4)
+
+    def at2(j):
+        return far + j * (1 - 2 * far)
+
+    cof = {-1: halo_c2[far, 0], 0: cof2[at2(0)], 1: cof2[at2(1)], 2: halo_c2[near, 0]}
+    dia = {
+        -1: halo_c2[far, 1] + cof[0], 0: dia2[at2(0)] + cof[-1],
+        1: dia2[at2(1)] + cof[2], 2: halo_c2[near, 1] + cof[1],
+    }
+    rhs = {
+        -1: parts[3], 0: parts[2], 1: parts[0] + halo_3[near, 1], 2: halo_3[near, 0] + parts[1],
+    }
+    red = {j: jnp.where(mask2(j), 32.0 * rhs[j] / dia[j], 0.0) for j in rhs}
+    red[-1] = inside * red[-1]
+    for j in (0, 1):
+        top = 32.0 * rhs[j] + flat(j, red[j]) + across(j, j - 1, red[j - 1]) + across(j, j + 1, red[j + 1])
+        low_ref[at2(j)] = jnp.where(mask2(j), red[j], top / dia[j])
+
+    def wait_sent(side, present, messages):
+        @pl.when(present)
+        def _():
+            for src, dst, s_sem, r_sem in messages:
+                copy_out(side, src, dst, s_sem, r_sem).wait_send()
+
     for side in range(2):
-        wait_recv(side, has[side], halo_c1, s_c1, r_c1)
-        wait_recv(side, has[side], halo_c2, s_c2, r_c2)
-        wait_recv(side, has[side], halo_2, s_2, r_2)
-    inside = [jnp.where(has[side], 1.0, 0.0) for side in range(2)]
-
-    def with_ends(own, low, high):
-        return [low] + list(own) + [high]
-
-    def red_black(rhs, coefs, diags, seconds, factor, depth):
-        masks = [parity(rhs[0].shape, i - 1) for i in range(depth + 2)]
-        reds = []
-        for i in range(depth + 2):
-            value = jnp.where(masks[i], factor * rhs[i] / diags[i], 0.0)
-            if i == 0:
-                value = inside[0] * value
-            if i == depth + 1:
-                value = inside[1] * value
-            reds.append(value)
-        return masks, reds
-
-    def off_of(coefs, fields, i):
-        around = plane_sum(fields[i])
-        weighted = plane_sum(coefs[i] * fields[i])
-        for j in (i - 1, i + 1):
-            if 0 <= j < len(fields):
-                around = around + fields[j]
-                weighted = weighted + coefs[j] * fields[j]
-        return coefs[i] * around + weighted
-
-    ends = [halo_2[0, 0] + edge1[0], halo_2[1, 0] + edge1[1]]
-    rhs1[0] = rhs1[0] + halo_2[0, 1]
-    rhs1[-1] = rhs1[-1] + halo_2[1, 1]
-    d1 = with_ends(d1, halo_c1[0, 1] + c1[0], halo_c1[1, 1] + c1[-1])
-    d1[1] = d1[1] + halo_c1[0, 0]
-    d1[-2] = d1[-2] + halo_c1[1, 0]
-    c1 = with_ends(c1, halo_c1[0, 0], halo_c1[1, 0])
-    rhs1 = with_ends(rhs1, ends[0], ends[1])
-    masks, reds = red_black(rhs1, c1, d1, None, 8.0, pairs)
-    blacks = []
-    for i in range(pairs + 2):
-        top = 8.0 * rhs1[i] + off_of(c1, reds, i)
-        if i == 0:
-            top = inside[0] * (top + halo_2[0, 2])
-        if i == pairs + 1:
-            top = inside[1] * (top + halo_2[1, 2])
-        blacks.append(jnp.where(masks[i], 0.0, top / d1[i]))
-    for i in range(1, pairs + 1):
-        mid_ref[i - 1] = reds[i] + blacks[i]
-    res = [
-        jnp.where(masks[i], off_of(c1, blacks, i), 0.0) for i in range(1, pairs + 1)
-    ]
-
-    put_rows(zmid, 0, 3.0 * (res[0] + res[1]) + res[2])
-    put_rows(zmid, 1, 3.0 * (res[2] + res[3]) + res[1])
-    put_rows(zmid, 2, res[0])
-    put_rows(zmid, 3, res[3])
-    parts = restrict(zmid, 4, ny2, wres[0 : nx // 2, 0 : nx // 4], 0.5 ** 12)
-    rhs2, edge2 = parts[:2], parts[2:]
-    for side in range(2):
-        send_3[side, 0] = rhs2[side]
-        send_3[side, 1] = edge2[side]
-    send(lambda side: send_3.at[side], halo_3, s_3, r_3)
-    for side in range(2):
-        wait_recv(side, has[side], halo_3, s_3, r_3)
-    ends = [halo_3[side, 0] + edge2[side] for side in range(2)]
-    rhs2 = [rhs2[side] + halo_3[side, 1] for side in range(2)]
-    d2 = with_ends(d2, halo_c2[0, 1] + c2[0], halo_c2[1, 1] + c2[1])
-    d2[1] = d2[1] + halo_c2[0, 0]
-    d2[2] = d2[2] + halo_c2[1, 0]
-    c2 = with_ends(c2, halo_c2[0, 0], halo_c2[1, 0])
-    rhs2 = with_ends(rhs2, ends[0], ends[1])
-    masks, reds = red_black(rhs2, c2, d2, None, 32.0, 2)
-    for i in (1, 2):
-        top = 32.0 * rhs2[i] + off_of(c2, reds, i)
-        low_ref[i - 1] = jnp.where(masks[i], reds[i], top / d2[i])
-
-    for side in range(2):
-        @pl.when(has[side])
-        def _(side=side):
-            for src, dst, s_sem, r_sem in (
-                (craw.at[(nz - 1) * side], halo_c, s_c, r_c),
-                (send_d.at[side], halo_d, s_d, r_d),
-                (send_m.at[side], halo_m, s_m, r_m),
-                (send_q.at[side], halo_q, s_q, r_q),
-                (send_c1.at[side], halo_c1, s_c1, r_c1),
-                (send_c2.at[side], halo_c2, s_c2, r_c2),
-                (send_2.at[side], halo_2, s_2, r_2),
-                (send_3.at[side], halo_3, s_3, r_3),
-            ):
-                copy_out(side, src, dst, s_sem, r_sem).wait_send()
+        wait_sent(side, has[side], (
+            (craw.at[(nz - 1) * side], halo_c, s_c, r_c),
+            (send_d.at[side], halo_d, s_d, r_d),
+            (send_m.at[side], halo_m, s_m, r_m),
+            (send_q.at[side], halo_q, s_q, r_q),
+            (send_c1.at[side], halo_c1, s_c1, r_c1),
+            (send_c2.at[side], halo_c2, s_c2, r_c2),
+            (send_2.at[side, 0:2], halo_2, s_2, r_2),
+        ))
+    wait_sent(near, true, (
+        (send_2.at[near, 2], halo_n, s_n, r_n), (send_3, halo_3, s_3, r_3),
+    ))
+    wait_sent(far, has_far, ((send_2.at[far, 2:4], halo_f, s_f, r_f),))
 
 
 def on_device(size, pressure_guess, source, conductance):
@@ -495,13 +548,16 @@
         vmem(pairs + 2, nx // 128, ny + 16, 128), vmem(4, nx1 // 128, ny1 + 16, 128),
         pltpu.VMEM((nx, nx1), BF16), pltpu.VMEM((nx, nx1), BF16),
         vmem(2, 3, ny1, nx1), vmem(pairs, ny1, nx1), vmem(pairs, ny1, nx1),
+        vmem(2, ny2, nx2), vmem(2, ny2, nx2),
     ]
     messages = [
-        vmem(2, ny, nx), vmem(2, ny, nx), vmem(2, ny1, nx), vmem(2, 2, ny1, nx1), vmem(2, 2, ny2, nx2),
-        vmem(2, 3, ny1, nx1), vmem(2, 2, ny2, nx2),
-    ]
-    halos = [vmem(2, ny, nx)] + messages
-    sems = [pltpu.SemaphoreType.DMA((3,))] + [pltpu.SemaphoreType.DMA((2,))] * 16
+        vmem(2, ny, nx), vmem(2, ny, nx), vmem(2, ny1, nx), vmem(2, 5, ny1, nx1), vmem(2, 2, ny2, nx2),
+    ]
+    sent = messages + [vmem(2, 4, ny1, nx1), vmem(2, ny2, nx2)]
+    halos = [vmem(2, ny, nx)] + messages + [
+        vmem(2, 2, ny1, nx1), vmem(2, ny1, nx1), vmem(2, 2, ny1, nx1), vmem(2, 2, ny2, nx2),
+    ]
+    sems = [pltpu.SemaphoreType.DMA((3,))] + [pltpu.SemaphoreType.DMA((2,))] * 20
 
     def run(*refs):
         kernel(size, *refs)
@@ -516,7 +572,7 @@
         out_shape=tuple(pltpu.VMEM(shape, F32) for shape in shapes),
         in_specs=[pl.BlockSpec(memory_space=pl.ANY)] * 3,
         out_specs=tuple([pl.BlockSpec(memory_space=pltpu.VMEM)] * 3),
-        scratch_shapes=slab + padded + faces + sums + work + messages + halos + sems,
+        scratch_shapes=slab + padded + faces + sums + work + sent + halos + sems,
         compiler_params=pltpu.CompilerParams(
             collective_id=0, has_side_effects=True, vmem_limit_bytes=48 * 2 ** 20
         ),

time: 29 us -> 27.7 us (0.955)
  the two profiles are of different devices: /device:TPU:24 before, /device:TPU:25 now
where the time goes in v3:
time: 27.7 us; the launch traced here: 27.6 us
  Pallas kernels  27 us (97%)
  between operations  0.64 us (2%)
    pallas_call x1, Pallas kernels, on_device(): pl.pallas_call(run, out_shape=tuple((pltpu.VMEM(shape, F32) for shape in...  26 us
    pallas_call x1, Pallas kernels, on_device(): pl.pallas_call(write_out, out_shape=tuple((jax.ShapeDtypeStruct(shape, F3...  1.03 us

profile of v3, /device:TPU:25, one launch (start us, length us, event | category | flops | bytes accessed | tf_op | source)
XLA Modules:
  0.0 27.6 jit_solution(7820012529676563978)
XLA Ops:
  0.6 26.0 %shard_map.58 = (f32[8,64,512]{2,1,0:T(8,128)S(1)}, f32[4,32,256]{2,1,0:T(8,128)S(1)}, f32[2,16,128]{2,1,0:T(8,128)S(1)}) custom-call(f32[8,64,512]{2,1,0:T(8,128)} %refs_0_.1, f32[8,64,512]{2,1,0:T(8,128)} %refs_1_.1, f32[8,64,512]{2,1,0:T(8,128)} %refs_2_.1), custom_call_target="tpu_custom_call" | custom-call | tf_op jit(solution)/shard_map/pallas_call | solution.py:570
  26.6 1.0 %shard_map.59 = (f32[8,64,512]{2,1,0:T(8,128)}, f32[4,32,256]{2,1,0:T(8,128)}, f32[2,16,128]{2,1,0:T(8,128)}) custom-call(f32[8,64,512]{2,1,0:T(8,128)S(1)} %get-tuple-element.6.p_src, f32[4,32,256]{2,1,0:T(8,128)S(1)} %get-tuple-element.7.mid_src, f32[2,16,128]{2,1,0:T(8,128)S(1)} %get-tuple-element.8.low_src), custom_call_target="tpu_custom_call" | custom-call | tf_op jit(solution)/shard_map/pallas_call | solution.py:580

commit v4 on v3

--- a/solution.py
+++ b/solution.py
@@ -70,7 +70,7 @@
     fpair, fro, frs, fbo, fbs,
     dr, db, nr,
     zbuf, zmid, wres, wsum,
-    v1, cof1, dia1,
+    v1, val, cof1, dia1,
     cof2, dia2,
     send_d, send_m, send_q, send_c1, send_c2, send_2, send_3,
     halo_c, halo_d, halo_m, halo_q, halo_c1, halo_c2, halo_2, halo_n, halo_f, halo_3,
@@ -212,7 +212,10 @@
 
     def put_diagonal(side, carry):
         k = (pairs - 1) * side
-        send_d[side] = jnp.where(parity(plane, side), dr[k], db[k])
+        half = ny // 2
+        send_d[side] = jnp.where(
+            parity((half, nx), side), dr[k, 0:half], pltpu.roll(dr[k, half:ny], 1, 0)
+        )
         return carry
 
     def put_field(side, carry):
@@ -224,10 +227,7 @@
         k = (pairs - 1) * side
         rhs = even_first(braw[2 * k + 1], braw[2 * k])
         part = 2.0 * rhs + fpair[k] * rr[k + 1]
-        half = ny // 2
-        send_q[side] = jnp.where(
-            parity((half, nx), side), pltpu.roll(part[half:], 1, 0), part[:half]
-        )
+        send_q[side] = jnp.where(parity(plane, side), pltpu.roll(db[k], 1, 0), part)
         return carry
 
     def at_ends(body):
@@ -321,11 +321,11 @@
     send(lambda side: send_c1.at[side], halo_c1, s_c1, r_c1)
     send(lambda side: send_c2.at[side], halo_c2, s_c2, r_c2)
 
-    def restrict(ref, count, out_rows, weights, scale):
+    def restrict(ref, first, count, out_rows, weights, scale):
         rows = [
             (get_rows(ref, k, 7, out_rows) + get_rows(ref, k, 10, out_rows))
             + 3.0 * (get_rows(ref, k, 8, out_rows) + get_rows(ref, k, 9, out_rows))
-            for k in range(count)
+            for k in range(first, first + count)
         ]
         out = scale * dot_parts(jnp.concatenate(rows, axis=0), weights)
         return [out[k * out_rows : (k + 1) * out_rows] for k in range(count)]
@@ -336,12 +336,12 @@
         wait_recv(side, present, halo_c, s_c, r_c)
         wait_recv(side, present, halo_d, s_d, r_d)
         wait_recv(side, present, halo_m, s_m, r_m)
-        wait_recv(side, present, halo_q, s_q, r_q)
         k = (pairs - 1) * side
         here = (nz - 1) * side
         mine = parity(plane, side)
         inside = jnp.where(present, 1.0, 0.0)
         hc, hd, hm = halo_c[side], halo_d[side], halo_m[side]
+        hd = jnp.concatenate([hd, pltpu.roll(hd, ny // 2 - 1, 0)], axis=0)
         c0, g0 = craw[here], graw[here]
         face = c0 + hc
         top = jnp.where(mine, nr[k], hm) + face * jnp.where(mine, hm, g0)
@@ -349,13 +349,7 @@
         value = jnp.where(mine, value, inside * value)
         reds = jnp.where(mine, value, rr[k + 1])
         rr[k + 1] = reds
-        hq = halo_q[side]
-        off = jnp.concatenate([hq, pltpu.roll(hq, ny // 2 - 1, 0)], axis=0)
-        off = off + face * value
-        sides, _ = side_faces(hc, hc)
-        for f, shifted in zip(sides, shifts(value)):
-            off = off + f * shifted
-        halo_delta = inside * (off / (hd + c0) - hm)
+        val[side] = value
 
         rhs = even_first(braw[2 * k + 1], braw[2 * k])
         off = gather(k, reds, even_first(rr[k + 2], rr[k]), fbo, fbs)
@@ -365,8 +359,7 @@
         dl[k + 1] = delta
         put_pressure(k, reds, new)
 
-        off = gather(k, delta, even_first(dl[k], dl[k + 2]), fro, frs)
-        rho[k + 1] = off + jnp.where(mine, face * halo_delta, 0.0)
+        rho[k + 1] = gather(k, delta, even_first(dl[k], dl[k + 2]), fro, frs)
         inner = k + 1 - 2 * side
         more = (cr[inner + 1] + cb[k + 1]) * delta
         rho[inner + 1] = rho[inner + 1] + jnp.where(mine, more, 0.0)
@@ -374,7 +367,7 @@
         for i, at in enumerate((k, inner)):
             put_rows(zbuf, i, 3.0 * rho[at + 1] + even_first(rho[at + 2], rho[at]))
         put_rows(zbuf, 2, jnp.where(mine, rho[k + 1], 0.0))
-        parts = restrict(zbuf, 3, ny1, wres[...], 0.5 ** 10)
+        parts = restrict(zbuf, 0, 3, ny1, wres[...], 0.5 ** 10)
         for i in range(3):
             v1[side, i] = parts[i]
         send_2[side, 0] = parts[0]
@@ -391,7 +384,28 @@
 
         return carry
 
+    def beyond(side, present):
+        wait_recv(side, present, halo_q, s_q, r_q)
+        k = (pairs - 1) * side
+        mine = parity(plane, side)
+        inside = jnp.where(present, 1.0, 0.0)
+        hc, hq, value = halo_c[side], halo_q[side], val[side]
+        c0 = craw[(nz - 1) * side]
+        face = c0 + hc
+        off = hq + face * value
+        sides, _ = side_faces(hc, hc)
+        for f, shifted in zip(sides, shifts(value)):
+            off = off + f * shifted
+        delta = off / (pltpu.roll(hq, ny - 1, 0) + c0) - halo_m[side]
+        put_rows(zbuf, 0, jnp.where(mine, inside * (face * delta), 0.0))
+        put_rows(zbuf, 1, jnp.where(mine, 0.0, inside * (face * dl[k + 1])))
+        here, there = restrict(zbuf, 0, 2, ny1, wres[...], 0.5 ** 10)
+        v1[side, 0] = v1[side, 0] + 3.0 * here
+        v1[side, 2] = v1[side, 2] + here
+        v1[side, 3] = there
+
     lax.fori_loop(0, 2, finish, 0)
+    beyond(near, me >= 0)
 
     def mask1(j):
         return parity(plane1, j + far + 4)
@@ -423,8 +437,8 @@
     dia[4] = halo_c1[near, 1] + cof[3]
     dia[3] = dia[3] + cof[4]
     rhs = {
-        4: halo_2[near, 0] + v1[near, 2],
-        3: v1[near, 0] + halo_2[near, 1],
+        4: halo_2[near, 0] + 3.0 * v1[near, 3] + v1[near, 2],
+        3: v1[near, 0] + (halo_2[near, 1] + v1[near, 3]),
         2: v1[near, 1],
         1: v1[far, 1],
     }
@@ -445,41 +459,46 @@
     def _():
         copy_out(far, send_2.at[far, 2:4], halo_f, s_f, r_f).start()
 
+    beyond(far, has_far)
     wait_recv(far, has_far, halo_c1, s_c1, r_c1)
     cof.update({-1: halo_c1[far, 0], -2: halo_c1[far, 2], -3: halo_c1[far, 4]})
     dia.update({-1: halo_c1[far, 1] + cof[0], -2: halo_c1[far, 3], 0: dia[0] + cof[-1]})
     wait_recv(far, has_far, halo_2, s_2, r_2)
-    rhs[0] = v1[far, 0] + halo_2[far, 1]
-    rhs[-1] = halo_2[far, 0] + v1[far, 2]
+    rhs[0] = v1[far, 0] + (halo_2[far, 1] + v1[far, 3])
+    rhs[-1] = halo_2[far, 0] + 3.0 * v1[far, 3] + v1[far, 2]
     red[0] = red_of(0, rhs[0])
     red[-1] = inside * red_of(-1, rhs[-1])
     black[0] = black_of(0, 8.0 * rhs[0] + flat(0, red[0]) + across(0, -1, red[-1]) + across(0, 1, red[1]))
     black[1] = black_of(1, part1 + across(1, 0, red[0]))
-    wait_recv(far, has_far, halo_f, s_f, r_f)
-    black[-1] = inside * black_of(-1, 8.0 * rhs[-1] + halo_f[far, 0] + flat(-1, red[-1]) + across(-1, 0, red[0]))
-    black[-2] = inside * black_of(-2, halo_f[far, 1] + across(-2, -1, red[-1]))
     res = {
         3: flat(3, black[3]) + across(3, 2, black[2]) + across(3, 4, black[4]),
         2: part2 + across(2, 1, black[1]),
         1: flat(1, black[1]) + across(1, 0, black[0]) + cross,
+    }
+    res = {j: jnp.where(mask1(j), value, 0.0) for j, value in res.items()}
+    weights2 = wres[0 : nx // 2, 0 : nx // 4]
+    put_rows(zmid, 0, 3.0 * (res[3] + res[2]) + res[1])
+    put_rows(zmid, 1, res[3])
+    parts = restrict(zmid, 0, 2, ny2, weights2, 0.5 ** 12)
+    send_3[0] = parts[0]
+    send_3[1] = parts[1]
+    copy_out(near, send_3, halo_3, s_3, r_3).start()
+
+    wait_recv(far, has_far, halo_f, s_f, r_f)
+    black[-1] = inside * black_of(-1, 8.0 * rhs[-1] + halo_f[far, 0] + flat(-1, red[-1]) + across(-1, 0, red[0]))
+    black[-2] = inside * black_of(-2, halo_f[far, 1] + across(-2, -1, red[-1]))
+    more = {
         0: flat(0, black[0]) + across(0, -1, black[-1]) + across(0, 1, black[1]),
         -1: flat(-1, black[-1]) + across(-1, -2, black[-2]) + across(-1, 0, black[0]),
         -2: halo_f[far, 1] + flat(-2, black[-2]) + across(-2, -1, black[-1]),
         -3: halo_f[far, 0] + across(-3, -2, black[-2]),
     }
-    res = {
-        j: jnp.where(mask1(j) if j >= 0 else mask1(j) & has_far, value, 0.0)
-        for j, value in res.items()
-    }
-
-    put_rows(zmid, 0, 3.0 * (res[3] + res[2]) + res[1])
-    put_rows(zmid, 1, res[3])
+    for j, value in more.items():
+        res[j] = jnp.where(mask1(j) if j == 0 else mask1(j) & has_far, value, 0.0)
+
     put_rows(zmid, 2, 3.0 * (res[0] + res[1]) + (res[-1] + res[2]))
     put_rows(zmid, 3, 3.0 * (res[-1] + res[-2]) + (res[0] + res[-3]))
-    parts = restrict(zmid, 4, ny2, wres[0 : nx // 2, 0 : nx // 4], 0.5 ** 12)
-    send_3[0] = parts[0]
-    send_3[1] = parts[1]
-    copy_out(near, send_3, halo_3, s_3, r_3).start()
+    parts = parts + restrict(zmid, 2, 2, ny2, weights2, 0.5 ** 12)
     for j in range(4):
         mid_ref[at1(j)] = red[j] + black[j]
 
@@ -547,11 +566,11 @@
     work = [
         vmem(pairs + 2, nx // 128, ny + 16, 128), vmem(4, nx1 // 128, ny1 + 16, 128),
         pltpu.VMEM((nx, nx1), BF16), pltpu.VMEM((nx, nx1), BF16),
-        vmem(2, 3, ny1, nx1), vmem(pairs, ny1, nx1), vmem(pairs, ny1, nx1),
+        vmem(2, 4, ny1, nx1), vmem(2, ny, nx), vmem(pairs, ny1, nx1), vmem(pairs, ny1, nx1),
         vmem(2, ny2, nx2), vmem(2, ny2, nx2),
     ]
     messages = [
-        vmem(2, ny, nx), vmem(2, ny, nx), vmem(2, ny1, nx), vmem(2, 5, ny1, nx1), vmem(2, 2, ny2, nx2),
+        vmem(2, ny1, nx), vmem(2, ny, nx), vmem(2, ny, nx), vmem(2, 5, ny1, nx1), vmem(2, 2, ny2, nx2),
     ]
     sent = messages + [vmem(2, 4, ny1, nx1), vmem(2, ny2, nx2)]
     halos = [vmem(2, ny, nx)] + messages + [

time: 27.7 us -> 25.3 us (0.913)
  Pallas kernels: 27 us -> 24.5 us
    pallas_call x1, Pallas kernels: 26 us -> 23.5 us  [on_device(): pl.pallas_call(run, out_shape=tuple((pltpu.VMEM(shape, F32) for shape in...]
where the time goes in v4:
time: 25.3 us; the launch traced here: 25.2 us
  Pallas kernels  24.5 us (97%)
  between operations  0.64 us (3%)
    pallas_call x1, Pallas kernels, on_device(): pl.pallas_call(run, out_shape=tuple((pltpu.VMEM(shape, F32) for shape in...  23.5 us
    pallas_call x1, Pallas kernels, on_device(): pl.pallas_call(write_out, out_shape=tuple((jax.ShapeDtypeStruct(shape, F3...  1.03 us

profile of v4, /device:TPU:25, one launch (start us, length us, event | category | flops | bytes accessed | tf_op | source)
XLA Modules:
  0.0 25.2 jit_solution(17856763997079522155)
XLA Ops:
  0.6 23.5 %shard_map.58 = (f32[8,64,512]{2,1,0:T(8,128)S(1)}, f32[4,32,256]{2,1,0:T(8,128)S(1)}, f32[2,16,128]{2,1,0:T(8,128)S(1)}) custom-call(f32[8,64,512]{2,1,0:T(8,128)} %refs_0_.1, f32[8,64,512]{2,1,0:T(8,128)} %refs_1_.1, f32[8,64,512]{2,1,0:T(8,128)} %refs_2_.1), custom_call_target="tpu_custom_call" | custom-call | tf_op jit(solution)/shard_map/pallas_call | solution.py:589
  24.1 1.0 %shard_map.59 = (f32[8,64,512]{2,1,0:T(8,128)}, f32[4,32,256]{2,1,0:T(8,128)}, f32[2,16,128]{2,1,0:T(8,128)}) custom-call(f32[8,64,512]{2,1,0:T(8,128)S(1)} %get-tuple-element.6.p_src, f32[4,32,256]{2,1,0:T(8,128)S(1)} %get-tuple-element.7.mid_src, f32[2,16,128]{2,1,0:T(8,128)S(1)} %get-tuple-element.8.low_src), custom_call_target="tpu_custom_call" | custom-call | tf_op jit(solution)/shard_map/pallas_call | solution.py:599

commit v5 on v4

--- a/solution.py
+++ b/solution.py
@@ -70,13 +70,13 @@
     fpair, fro, frs, fbo, fbs,
     dr, db, nr,
     zbuf, zmid, wres, wsum,
-    v1, val, cof1, dia1,
+    v1, topb, cof1, dia1,
     cof2, dia2,
-    send_d, send_m, send_q, send_c1, send_c2, send_2, send_3,
-    halo_c, halo_d, halo_m, halo_q, halo_c1, halo_c2, halo_2, halo_n, halo_f, halo_3,
+    send_a, send_d, send_q, send_c1, send_c2, send_2, send_3,
+    halo_a, halo_d, halo_q, halo_c1, halo_c2, halo_2, halo_n, halo_f, halo_3,
     load_sem,
-    s_c, s_d, s_m, s_q, s_c1, s_c2, s_2, s_n, s_f, s_3,
-    r_c, r_d, r_m, r_q, r_c1, r_c2, r_2, r_n, r_f, r_3,
+    s_a, s_d, s_q, s_c1, s_c2, s_2, s_n, s_f, s_3,
+    r_a, r_d, r_q, r_c1, r_c2, r_2, r_n, r_f, r_3,
 ):
     me = lax.axis_index("gz")
     nz, ny, nx = craw.shape
@@ -118,9 +118,9 @@
     for side in range(2):
         @pl.when(jnp.logical_not(has[side]))
         def _(side=side):
-            for ref in (halo_c, halo_d, halo_m, halo_q):
+            for ref in (halo_a, halo_q):
                 ref[side] = jnp.zeros(ref.shape[1:], F32)
-            for ref in (halo_c1, halo_c2, halo_2, halo_f):
+            for ref in (halo_d, halo_c1, halo_c2, halo_2, halo_f):
                 for i in range(ref.shape[1]):
                     ref[side, i] = jnp.zeros(ref.shape[2:], F32)
     wres[...] = weights_of(wres.shape, 3.0, 1.0)
@@ -133,9 +133,9 @@
             device_id_type=pl.DeviceIdType.MESH,
         )
 
-    def send(src_of, dst, s_sem, r_sem):
+    def send(src_of, dst, s_sem, r_sem, allowed=True):
         for side in range(2):
-            @pl.when(has[side])
+            @pl.when(has[side] & allowed)
             def _(side=side):
                 copy_out(side, src_of(side), dst, s_sem, r_sem).start()
 
@@ -172,8 +172,6 @@
         return carry
 
     lax.fori_loop(0, pairs, pack, 0)
-    pl.semaphore_wait(barrier, jnp.where(has[0] & has[1], 2, 1))
-    send(lambda side: craw.at[(nz - 1) * side], halo_c, s_c, r_c)
 
     def faces(k, carry):
         own, other = cr[k + 1], cb[k + 1]
@@ -210,40 +208,50 @@
         rr[k + 1] = top / dr[k]
         return carry
 
+    def put_first(side, carry):
+        here = (nz - 1) * side
+        send_a[side] = jnp.where(parity(plane, side), pltpu.roll(craw[here], 1, 0), graw[here])
+        return carry
+
     def put_diagonal(side, carry):
         k = (pairs - 1) * side
-        half = ny // 2
-        send_d[side] = jnp.where(
-            parity((half, nx), side), dr[k, 0:half], pltpu.roll(dr[k, half:ny], 1, 0)
-        )
-        return carry
-
-    def put_field(side, carry):
-        k = (pairs - 1) * side
-        send_m[side] = jnp.where(parity(plane, side), nr[k], gb[k + 1])
-        return carry
-
-    def put_second(side, carry):
+        mine = parity(plane, side)
+        send_d[side, 0] = jnp.where(mine, dr[k], db[k])
+        send_d[side, 1] = jnp.where(mine, craw[(nz - 1) * side], fpair[k])
+        return carry
+
+    def put_tops(side, carry):
         k = (pairs - 1) * side
         rhs = even_first(braw[2 * k + 1], braw[2 * k])
-        part = 2.0 * rhs + fpair[k] * rr[k + 1]
-        send_q[side] = jnp.where(parity(plane, side), pltpu.roll(db[k], 1, 0), part)
+        send_q[side] = jnp.where(parity(plane, side), nr[k], 2.0 * rhs + fpair[k] * rr[k + 1])
         return carry
 
     def at_ends(body):
         lax.fori_loop(0, 2, lambda i, carry: body((pairs - 1) * i, carry), 0)
 
+    def enter(allowed):
+        @pl.when(allowed)
+        def _():
+            pl.semaphore_wait(barrier, jnp.where(has[0] & has[1], 2, 1))
+
+    odd = far == 1
     at_ends(faces)
     lax.fori_loop(0, 2, put_diagonal, 0)
-    send(lambda side: send_d.at[side], halo_d, s_d, r_d)
+    enter(odd)
+    send(lambda side: send_d.at[side], halo_d, s_d, r_d, odd)
     loads[1].wait()
+    lax.fori_loop(0, 2, put_first, 0)
+    send(lambda side: send_a.at[side], halo_a, s_a, r_a, odd)
     lax.fori_loop(0, pairs, pack_g, 0)
     loads[2].wait()
     at_ends(red)
-    lax.fori_loop(0, 2, put_field, 0)
-    send(lambda side: send_m.at[side], halo_m, s_m, r_m)
-    lax.fori_loop(0, 2, put_second, 0)
-    send(lambda side: send_q.at[side], halo_q, s_q, r_q)
+    lax.fori_loop(0, 2, put_tops, 0)
+    send(lambda side: send_q.at[side], halo_q, s_q, r_q, odd)
+    even_core = far == 0
+    enter(even_core)
+    send(lambda side: send_a.at[side], halo_a, s_a, r_a, even_core)
+    send(lambda side: send_d.at[side], halo_d, s_d, r_d, even_core)
+    send(lambda side: send_q.at[side], halo_q, s_q, r_q, even_core)
 
     lax.fori_loop(1, pairs - 1, faces, 0)
     lax.fori_loop(1, pairs - 1, red, 0)
@@ -314,8 +322,9 @@
         dia2[k] = d2[k]
     for side in range(2):
         ends = (3 * side, 1 + side, 2 - side)
-        for i, value in enumerate((c1[ends[0]], d1[ends[0]], c1[ends[1]], d1[ends[1]], c1[ends[2]])):
-            send_c1[side, i] = value
+        for i, end in enumerate(ends):
+            send_c1[side, 2 * i] = c1[end]
+            send_c1[side, 2 * i + 1] = d1[end]
         send_c2[side, 0] = c2[side]
         send_c2[side, 1] = d2[side]
     send(lambda side: send_c1.at[side], halo_c1, s_c1, r_c1)
@@ -330,82 +339,94 @@
         out = scale * dot_parts(jnp.concatenate(rows, axis=0), weights)
         return [out[k * out_rows : (k + 1) * out_rows] for k in range(count)]
 
-    def finish(step, carry):
-        side = jnp.where(step == 0, near, far)
-        present = (step == 0) | has_far
-        wait_recv(side, present, halo_c, s_c, r_c)
-        wait_recv(side, present, halo_d, s_d, r_d)
-        wait_recv(side, present, halo_m, s_m, r_m)
+    def first_stage(side, present, is_near):
+        wait_recv(side, present, halo_a, s_a, r_a)
         k = (pairs - 1) * side
-        here = (nz - 1) * side
         mine = parity(plane, side)
-        inside = jnp.where(present, 1.0, 0.0)
-        hc, hd, hm = halo_c[side], halo_d[side], halo_m[side]
-        hd = jnp.concatenate([hd, pltpu.roll(hd, ny // 2 - 1, 0)], axis=0)
-        c0, g0 = craw[here], graw[here]
-        face = c0 + hc
-        top = jnp.where(mine, nr[k], hm) + face * jnp.where(mine, hm, g0)
-        value = top / jnp.where(mine, dr[k] + hc, hd + c0)
-        value = jnp.where(mine, value, inside * value)
+        field = halo_a[side]
+        coef = pltpu.roll(field, ny - 1, 0)
+        face = craw[(nz - 1) * side] + coef
+        value = (nr[k] + face * field) / (dr[k] + coef)
         reds = jnp.where(mine, value, rr[k + 1])
         rr[k + 1] = reds
-        val[side] = value
-
         rhs = even_first(braw[2 * k + 1], braw[2 * k])
-        off = gather(k, reds, even_first(rr[k + 2], rr[k]), fbo, fbs)
-        off = off + jnp.where(mine, 0.0, face * value)
-        new = (2.0 * rhs + off) / (db[k] + jnp.where(mine, 0.0, hc))
+        top = 2.0 * rhs + gather(k, reds, even_first(rr[k + 2], rr[k]), fbo, fbs)
+        topb[side] = top
+        new = top / db[k]
         delta = new - gb[k + 1]
         dl[k + 1] = delta
         put_pressure(k, reds, new)
-
-        rho[k + 1] = gather(k, delta, even_first(dl[k], dl[k + 2]), fro, frs)
+        own = gather(k, delta, even_first(dl[k], dl[k + 2]), fro, frs)
+        rho[k + 1] = own
         inner = k + 1 - 2 * side
         more = (cr[inner + 1] + cb[k + 1]) * delta
         rho[inner + 1] = rho[inner + 1] + jnp.where(mine, more, 0.0)
 
         for i, at in enumerate((k, inner)):
             put_rows(zbuf, i, 3.0 * rho[at + 1] + even_first(rho[at + 2], rho[at]))
-        put_rows(zbuf, 2, jnp.where(mine, rho[k + 1], 0.0))
+        put_rows(zbuf, 2, jnp.where(mine, own, 0.0))
         parts = restrict(zbuf, 0, 3, ny1, wres[...], 0.5 ** 10)
         for i in range(3):
             v1[side, i] = parts[i]
         send_2[side, 0] = parts[0]
         send_2[side, 1] = parts[2]
-        send_2[side, 2] = (cof1[k] + cof1[inner]) * (8.0 * parts[1] / dia1[inner])
 
         @pl.when(present)
         def _():
             copy_out(side, send_2.at[side, 0:2], halo_2, s_2, r_2).start()
 
-        @pl.when(step == 0)
-        def _():
+        if is_near:
+            send_2[side, 2] = (cof1[k] + cof1[inner]) * (8.0 * parts[1] / dia1[inner])
             copy_out(side, send_2.at[side, 2], halo_n, s_n, r_n).start()
 
-        return carry
-
-    def beyond(side, present):
+    def second_stage(side, present):
+        wait_recv(side, present, halo_d, s_d, r_d)
         wait_recv(side, present, halo_q, s_q, r_q)
         k = (pairs - 1) * side
+        here = (nz - 1) * side
         mine = parity(plane, side)
-        inside = jnp.where(present, 1.0, 0.0)
-        hc, hq, value = halo_c[side], halo_q[side], val[side]
-        c0 = craw[(nz - 1) * side]
+        black_there = mine & present
+        field = halo_a[side]
+        diagonal, coef, tops = halo_d[side, 0], halo_d[side, 1], halo_q[side]
+        c0, g0 = craw[here], graw[here]
+        hc = jnp.where(mine, pltpu.roll(field, ny - 1, 0), coef)
         face = c0 + hc
-        off = hq + face * value
+        value = jnp.where(present, (tops + face * g0) / (diagonal + c0), 0.0)
         sides, _ = side_faces(hc, hc)
+        short = tops
         for f, shifted in zip(sides, shifts(value)):
-            off = off + f * shifted
-        delta = off / (pltpu.roll(hq, ny - 1, 0) + c0) - halo_m[side]
-        put_rows(zbuf, 0, jnp.where(mine, inside * (face * delta), 0.0))
-        put_rows(zbuf, 1, jnp.where(mine, 0.0, inside * (face * dl[k + 1])))
-        here, there = restrict(zbuf, 0, 2, ny1, wres[...], 0.5 ** 10)
-        v1[side, 0] = v1[side, 0] + 3.0 * here
-        v1[side, 2] = v1[side, 2] + here
-        v1[side, 3] = there
-
-    lax.fori_loop(0, 2, finish, 0)
-    beyond(near, me >= 0)
+            short = short + f * shifted
+        reds = rr[k + 1]
+        new = (jnp.where(mine, short, topb[side]) + face * jnp.where(mine, reds, value)) / (
+            jnp.where(mine, diagonal + c0, db[k] + hc)
+        )
+        old = dl[k + 1]
+        delta = new - gb[k + 1]
+        change = jnp.where(mine, 0.0, delta - old)
+        dl[k + 1] = jnp.where(mine, old, delta)
+        p_ref[here] = jnp.where(mine, reds, new)
+        delta_there = jnp.where(black_there, new - field, 0.0)
+        change_there = jnp.where(black_there, new - short / diagonal, 0.0)
+        add = fpair[k] * change
+        for i, shifted in enumerate(shifts(change)):
+            add = add + frs[k, i] * shifted
+        put_rows(zbuf, 0, jnp.where(mine, add + face * delta_there, 0.0))
+        put_rows(zbuf, 1, jnp.where(mine, 0.0, add))
+        add = face * delta
+        for f, shifted in zip(sides, shifts(change_there)):
+            add = add + f * shifted
+        put_rows(zbuf, 2, jnp.where(mine | jnp.logical_not(present), 0.0, add))
+        put_rows(zbuf, 3, jnp.where(black_there, coef * change_there, 0.0))
+        parts = restrict(zbuf, 0, 4, ny1, wres[...], 0.5 ** 10)
+        v1[side, 0] = v1[side, 0] + 3.0 * (parts[0] + parts[1])
+        v1[side, 1] = v1[side, 1] + parts[1]
+        v1[side, 2] = v1[side, 2] + parts[0]
+        v1[side, 3] = parts[2]
+        v1[side, 4] = parts[3]
+
+    true = me >= 0
+    first_stage(near, true, True)
+    second_stage(near, true)
 
     def mask1(j):
         return parity(plane1, j + far + 4)
@@ -414,7 +435,6 @@
         return 3 * far + j * (1 - 2 * far)
 
     inside = jnp.where(has_far, 1.0, 0.0)
-    true = me >= 0
     cof = {j: cof1[at1(j)] for j in range(4)}
     dia = {j: dia1[at1(j)] for j in range(4)}
 
@@ -433,39 +453,58 @@
     wait_recv(near, true, halo_c1, s_c1, r_c1)
     wait_recv(near, true, halo_2, s_2, r_2)
     wait_recv(near, true, halo_n, s_n, r_n)
-    cof[4] = halo_c1[near, 0]
-    dia[4] = halo_c1[near, 1] + cof[3]
-    dia[3] = dia[3] + cof[4]
+    cof.update({4: halo_c1[near, 0], 5: halo_c1[near, 2]})
+    dia.update({3: dia[3] + cof[4], 4: halo_c1[near, 1] + cof[3], 5: halo_c1[near, 3]})
     rhs = {
-        4: halo_2[near, 0] + 3.0 * v1[near, 3] + v1[near, 2],
+        4: halo_2[near, 0] + 3.0 * (v1[near, 3] + v1[near, 4]) + v1[near, 2],
         3: v1[near, 0] + (halo_2[near, 1] + v1[near, 3]),
         2: v1[near, 1],
-        1: v1[far, 1],
     }
-    red = {j: red_of(j, rhs[j]) for j in (1, 2, 3, 4)}
+    red = {j: red_of(j, rhs[j]) for j in (2, 3, 4)}
     black = {}
-    black[4] = black_of(4, 8.0 * rhs[4] + halo_n[near] + flat(4, red[4]) + across(4, 3, red[3]))
-    for j in (3, 2):
-        black[j] = black_of(
-            j, 8.0 * rhs[j] + flat(j, red[j]) + across(j, j + 1, red[j + 1]) + across(j, j - 1, red[j - 1])
-        )
-    part1 = 8.0 * rhs[1] + flat(1, red[1]) + across(1, 2, red[2])
-    part2 = flat(2, black[2]) + across(2, 3, black[3])
-    cross = across(1, 2, black[2])
-    send_2[far, 2] = jnp.where(mask1(0), part2, across(0, 1, red[1]))
+    beyond = halo_n[near] + across(4, 5, red_of(5, v1[near, 4]))
+    black[4] = black_of(4, 8.0 * rhs[4] + beyond + flat(4, red[4]) + across(4, 3, red[3]))
+    black[3] = black_of(
+        3, 8.0 * rhs[3] + flat(3, red[3]) + across(3, 4, red[4]) + across(3, 2, red[2])
+    )
+    base1 = across(1, 2, red[2])
+    base2 = 8.0 * rhs[2] + flat(2, red[2]) + across(2, 3, red[3])
+    base3 = across(2, 3, black[3])
+
+    def middle():
+        right = v1[far, 1]
+        red1 = red_of(1, right)
+        black2 = black_of(2, base2 + across(2, 1, red1))
+        part1 = 8.0 * right + flat(1, red1) + base1
+        part2 = flat(2, black2) + base3
+        return red1, black2, part1, part2, across(1, 2, black2)
+
+    first_stage(far, has_far, False)
+    red1, black2, part1, part2, cross = middle()
+    send_2[far, 2] = jnp.where(mask1(0), part2, across(0, 1, red1))
     send_2[far, 3] = jnp.where(mask1(1), cross, part1)
 
     @pl.when(has_far)
     def _():
         copy_out(far, send_2.at[far, 2:4], halo_f, s_f, r_f).start()
 
-    beyond(far, has_far)
+    second_stage(far, has_far)
+    red[1], black[2], part1, part2, cross = middle()
     wait_recv(far, has_far, halo_c1, s_c1, r_c1)
     cof.update({-1: halo_c1[far, 0], -2: halo_c1[far, 2], -3: halo_c1[far, 4]})
-    dia.update({-1: halo_c1[far, 1] + cof[0], -2: halo_c1[far, 3], 0: dia[0] + cof[-1]})
+    dia.update({
+        -1: halo_c1[far, 1] + cof[0], -2: halo_c1[far, 3], -3: halo_c1[far, 5], 0: dia[0] + cof[-1],
+    })
+    there1, there2 = v1[far, 3], v1[far, 4]
+    more_red = jnp.where(has_far, red_of(-2, there2), 0.0)
+    more_black = jnp.where(has_far, black_of(-3, across(-3, -2, more_red)), 0.0)
+    fix1 = jnp.where(mask1(-1), flat(-3, more_black), across(-1, -2, more_red))
+    fix2 = jnp.where(mask1(-2), across(-2, -3, more_black), 8.0 * there2 + flat(-2, more_red))
+    end0 = v1[far, 0] + there1
+    end1 = 3.0 * (there1 + there2) + v1[far, 2]
     wait_recv(far, has_far, halo_2, s_2, r_2)
-    rhs[0] = v1[far, 0] + (halo_2[far, 1] + v1[far, 3])
-    rhs[-1] = halo_2[far, 0] + 3.0 * v1[far, 3] + v1[far, 2]
+    rhs[0] = halo_2[far, 1] + end0
+    rhs[-1] = halo_2[far, 0] + end1
     red[0] = red_of(0, rhs[0])
     red[-1] = inside * red_of(-1, rhs[-1])
     black[0] = black_of(0, 8.0 * rhs[0] + flat(0, red[0]) + across(0, -1, red[-1]) + across(0, 1, red[1]))
@@ -485,13 +524,14 @@
     copy_out(near, send_3, halo_3, s_3, r_3).start()
 
     wait_recv(far, has_far, halo_f, s_f, r_f)
-    black[-1] = inside * black_of(-1, 8.0 * rhs[-1] + halo_f[far, 0] + flat(-1, red[-1]) + across(-1, 0, red[0]))
-    black[-2] = inside * black_of(-2, halo_f[far, 1] + across(-2, -1, red[-1]))
+    seconds = (halo_f[far, 0] + fix1, halo_f[far, 1] + fix2)
+    black[-1] = inside * black_of(-1, 8.0 * rhs[-1] + seconds[0] + flat(-1, red[-1]) + across(-1, 0, red[0]))
+    black[-2] = inside * black_of(-2, seconds[1] + across(-2, -1, red[-1]))
     more = {
         0: flat(0, black[0]) + across(0, -1, black[-1]) + across(0, 1, black[1]),
         -1: flat(-1, black[-1]) + across(-1, -2, black[-2]) + across(-1, 0, black[0]),
-        -2: halo_f[far, 1] + flat(-2, black[-2]) + across(-2, -1, black[-1]),
-        -3: halo_f[far, 0] + across(-3, -2, black[-2]),
+        -2: seconds[1] + flat(-2, black[-2]) + across(-2, -1, black[-1]),
+        -3: seconds[0] + across(-3, -2, black[-2]),
     }
     for j, value in more.items():
         res[j] = jnp.where(mask1(j) if j == 0 else mask1(j) & has_far, value, 0.0)
@@ -534,9 +574,8 @@
 
     for side in range(2):
         wait_sent(side, has[side], (
-            (craw.at[(nz - 1) * side], halo_c, s_c, r_c),
+            (send_a.at[side], halo_a, s_a, r_a),
             (send_d.at[side], halo_d, s_d, r_d),
-            (send_m.at[side], halo_m, s_m, r_m),
             (send_q.at[side], halo_q, s_q, r_q),
             (send_c1.at[side], halo_c1, s_c1, r_c1),
             (send_c2.at[side], halo_c2, s_c2, r_c2),
@@ -566,17 +605,17 @@
     work = [
         vmem(pairs + 2, nx // 128, ny + 16, 128), vmem(4, nx1 // 128, ny1 + 16, 128),
         pltpu.VMEM((nx, nx1), BF16), pltpu.VMEM((nx, nx1), BF16),
-        vmem(2, 4, ny1, nx1), vmem(2, ny, nx), vmem(pairs, ny1, nx1), vmem(pairs, ny1, nx1),
+        vmem(2, 5, ny1, nx1), vmem(2, ny, nx), vmem(pairs, ny1, nx1), vmem(pairs, ny1, nx1),
         vmem(2, ny2, nx2), vmem(2, ny2, nx2),
     ]
     messages = [
-        vmem(2, ny1, nx), vmem(2, ny, nx), vmem(2, ny, nx), vmem(2, 5, ny1, nx1), vmem(2, 2, ny2, nx2),
+        vmem(2, ny, nx), vmem(2, 2, ny, nx), vmem(2, ny, nx), vmem(2, 6, ny1, nx1), vmem(2, 2, ny2, nx2),
     ]
     sent = messages + [vmem(2, 4, ny1, nx1), vmem(2, ny2, nx2)]
-    halos = [vmem(2, ny, nx)] + messages + [
+    halos = messages + [
         vmem(2, 2, ny1, nx1), vmem(2, ny1, nx1), vmem(2, 2, ny1, nx1), vmem(2, 2, ny2, nx2),
     ]
-    sems = [pltpu.SemaphoreType.DMA((3,))] + [pltpu.SemaphoreType.DMA((2,))] * 20
+    sems = [pltpu.SemaphoreType.DMA((3,))] + [pltpu.SemaphoreType.DMA((2,))] * 18
 
     def run(*refs):
         kernel(size, *refs)

time: 25.3 us -> 23.7 us (0.937)
  Pallas kernels: 24.5 us -> 22.9 us
    pallas_call x1, Pallas kernels: 23.5 us -> 21.9 us  [on_device(): pl.pallas_call(run, out_shape=tuple((pltpu.VMEM(shape, F32) for shape in...]
where the time goes in v5:
time: 23.7 us; the launch traced here: 23.6 us
  Pallas kernels  22.9 us (97%)
  between operations  0.64 us (3%)
    pallas_call x1, Pallas kernels, on_device(): pl.pallas_call(run, out_shape=tuple((pltpu.VMEM(shape, F32) for shape in...  21.9 us
    pallas_call x1, Pallas kernels, on_device(): pl.pallas_call(write_out, out_shape=tuple((jax.ShapeDtypeStruct(shape, F3...  1.03 us

profile of v5, /device:TPU:25, one launch (start us, length us, event | category | flops | bytes accessed | tf_op | source)
XLA Modules:
  0.0 23.6 jit_solution(16209187666405463358)
XLA Ops:
  0.6 21.9 %shard_map.58 = (f32[8,64,512]{2,1,0:T(8,128)S(1)}, f32[4,32,256]{2,1,0:T(8,128)S(1)}, f32[2,16,128]{2,1,0:T(8,128)S(1)}) custom-call(f32[8,64,512]{2,1,0:T(8,128)} %refs_0_.1, f32[8,64,512]{2,1,0:T(8,128)} %refs_1_.1, f32[8,64,512]{2,1,0:T(8,128)} %refs_2_.1), custom_call_target="tpu_custom_call" | custom-call | tf_op jit(solution)/shard_map/pallas_call | solution.py:628
  22.6 1.0 %shard_map.59 = (f32[8,64,512]{2,1,0:T(8,128)}, f32[4,32,256]{2,1,0:T(8,128)}, f32[2,16,128]{2,1,0:T(8,128)}) custom-call(f32[8,64,512]{2,1,0:T(8,128)S(1)} %get-tuple-element.6.p_src, f32[4,32,256]{2,1,0:T(8,128)S(1)} %get-tuple-element.7.mid_src, f32[2,16,128]{2,1,0:T(8,128)S(1)} %get-tuple-element.8.low_src), custom_call_target="tpu_custom_call" | custom-call | tf_op jit(solution)/shard_map/pallas_call | solution.py:638

commit v6 on v5

--- a/solution.py
+++ b/solution.py
@@ -72,11 +72,11 @@
     zbuf, zmid, wres, wsum,
     v1, topb, cof1, dia1,
     cof2, dia2,
-    send_a, send_d, send_q, send_c1, send_c2, send_2, send_3,
-    halo_a, halo_d, halo_q, halo_c1, halo_c2, halo_2, halo_n, halo_f, halo_3,
+    send_a, send_h, send_d, send_q, send_c1, send_c2, send_2, send_3,
+    halo_a, halo_h, halo_d, halo_q, halo_c1, halo_c2, halo_2, halo_n, halo_f, halo_3,
     load_sem,
-    s_a, s_d, s_q, s_c1, s_c2, s_2, s_n, s_f, s_3,
-    r_a, r_d, r_q, r_c1, r_c2, r_2, r_n, r_f, r_3,
+    s_a, s_h, s_d, s_q, s_c1, s_c2, s_2, s_n, s_f, s_3,
+    r_a, r_h, r_d, r_q, r_c1, r_c2, r_2, r_n, r_f, r_3,
 ):
     me = lax.axis_index("gz")
     nz, ny, nx = craw.shape
@@ -89,13 +89,6 @@
     near = 1 - far
     has_far = jnp.where(far == 0, me, size - 1 - me) > 0
 
-    loads = [
-        pltpu.make_async_copy(src, dst, load_sem.at[i])
-        for i, (src, dst) in enumerate(((c_hbm, craw), (g_hbm, graw), (b_hbm, braw)))
-    ]
-    for load in loads:
-        load.start()
-
     barrier = pltpu.get_barrier_semaphore()
     for side in range(2):
         @pl.when(has[side])
@@ -104,6 +97,13 @@
                 barrier, inc=1, device_id=(me + 2 * side - 1,),
                 device_id_type=pl.DeviceIdType.MESH,
             )
+
+    loads = [
+        pltpu.make_async_copy(src, dst, load_sem.at[i])
+        for i, (src, dst) in enumerate(((c_hbm, craw), (g_hbm, graw), (b_hbm, braw)))
+    ]
+    for load in loads:
+        load.start()
 
     for ref in (cr, cb, gb, rr, dl, rho):
         ref[0] = jnp.zeros(plane, F32)
@@ -118,9 +118,9 @@
     for side in range(2):
         @pl.when(jnp.logical_not(has[side]))
         def _(side=side):
-            for ref in (halo_a, halo_q):
+            for ref in (halo_a, halo_h, halo_d, halo_q):
                 ref[side] = jnp.zeros(ref.shape[1:], F32)
-            for ref in (halo_d, halo_c1, halo_c2, halo_2, halo_f):
+            for ref in (halo_c1, halo_c2, halo_2, halo_f):
                 for i in range(ref.shape[1]):
                     ref[side, i] = jnp.zeros(ref.shape[2:], F32)
     wres[...] = weights_of(wres.shape, 3.0, 1.0)
@@ -216,8 +216,12 @@
     def put_diagonal(side, carry):
         k = (pairs - 1) * side
         mine = parity(plane, side)
-        send_d[side, 0] = jnp.where(mine, dr[k], db[k])
-        send_d[side, 1] = jnp.where(mine, craw[(nz - 1) * side], fpair[k])
+        send_d[side] = jnp.where(mine, dr[k], fpair[k])
+        coef = craw[(nz - 1) * side]
+        half = ny // 2
+        send_h[side] = jnp.where(
+            parity((half, nx), side), coef[:half], pltpu.roll(coef[half:], 1, 0)
+        )
         return carry
 
     def put_tops(side, carry):
@@ -238,6 +242,7 @@
     at_ends(faces)
     lax.fori_loop(0, 2, put_diagonal, 0)
     enter(odd)
+    send(lambda side: send_h.at[side], halo_h, s_h, r_h, odd)
     send(lambda side: send_d.at[side], halo_d, s_d, r_d, odd)
     loads[1].wait()
     lax.fori_loop(0, 2, put_first, 0)
@@ -250,6 +255,7 @@
     even_core = far == 0
     enter(even_core)
     send(lambda side: send_a.at[side], halo_a, s_a, r_a, even_core)
+    send(lambda side: send_h.at[side], halo_h, s_h, r_h, even_core)
     send(lambda side: send_d.at[side], halo_d, s_d, r_d, even_core)
     send(lambda side: send_q.at[side], halo_q, s_q, r_q, even_core)
 
@@ -323,8 +329,8 @@
     for side in range(2):
         ends = (3 * side, 1 + side, 2 - side)
         for i, end in enumerate(ends):
-            send_c1[side, 2 * i] = c1[end]
-            send_c1[side, 2 * i + 1] = d1[end]
+            send_c1[side, i] = c1[end]
+        send_c1[side, 3] = d1[ends[2]]
         send_c2[side, 0] = c2[side]
         send_c2[side, 1] = d2[side]
     send(lambda side: send_c1.at[side], halo_c1, s_c1, r_c1)
@@ -362,24 +368,30 @@
         more = (cr[inner + 1] + cb[k + 1]) * delta
         rho[inner + 1] = rho[inner + 1] + jnp.where(mine, more, 0.0)
 
-        for i, at in enumerate((k, inner)):
-            put_rows(zbuf, i, 3.0 * rho[at + 1] + even_first(rho[at + 2], rho[at]))
-        put_rows(zbuf, 2, jnp.where(mine, own, 0.0))
-        parts = restrict(zbuf, 0, 3, ny1, wres[...], 0.5 ** 10)
-        for i in range(3):
-            v1[side, i] = parts[i]
+        def along_z(at):
+            return 3.0 * rho[at + 1] + even_first(rho[at + 2], rho[at])
+
+        put_rows(zbuf, 0, along_z(k))
+        put_rows(zbuf, 1, jnp.where(mine, own, 0.0))
+        parts = restrict(zbuf, 0, 2, ny1, wres[...], 0.5 ** 10)
         send_2[side, 0] = parts[0]
-        send_2[side, 1] = parts[2]
+        send_2[side, 1] = parts[1]
 
         @pl.when(present)
         def _():
             copy_out(side, send_2.at[side, 0:2], halo_2, s_2, r_2).start()
 
+        v1[side, 0] = parts[0]
+        v1[side, 2] = parts[1]
+        put_rows(zbuf, 2, along_z(inner))
+        (middle,) = restrict(zbuf, 2, 1, ny1, wres[...], 0.5 ** 10)
+        v1[side, 1] = middle
         if is_near:
-            send_2[side, 2] = (cof1[k] + cof1[inner]) * (8.0 * parts[1] / dia1[inner])
+            send_2[side, 2] = (cof1[k] + cof1[inner]) * (8.0 * middle / dia1[inner])
             copy_out(side, send_2.at[side, 2], halo_n, s_n, r_n).start()
 
     def second_stage(side, present):
+        wait_recv(side, present, halo_h, s_h, r_h)
         wait_recv(side, present, halo_d, s_d, r_d)
         wait_recv(side, present, halo_q, s_q, r_q)
         k = (pairs - 1) * side
@@ -387,12 +399,14 @@
         mine = parity(plane, side)
         black_there = mine & present
         field = halo_a[side]
-        diagonal, coef, tops = halo_d[side, 0], halo_d[side, 1], halo_q[side]
+        half, mixed, tops = halo_h[side], halo_d[side], halo_q[side]
         c0, g0 = craw[here], graw[here]
-        hc = jnp.where(mine, pltpu.roll(field, ny - 1, 0), coef)
+        half = jnp.concatenate([half, pltpu.roll(half, ny // 2 - 1, 0)], axis=0)
+        hc = jnp.where(mine, pltpu.roll(field, ny - 1, 0), half)
         face = c0 + hc
-        value = jnp.where(present, (tops + face * g0) / (diagonal + c0), 0.0)
-        sides, _ = side_faces(hc, hc)
+        value = jnp.where(present, (tops + face * g0) / (mixed + c0), 0.0)
+        sides, around = side_faces(hc, hc)
+        diagonal = 5.0 * hc + around + mixed
         short = tops
         for f, shifted in zip(sides, shifts(value)):
             short = short + f * shifted
@@ -416,7 +430,7 @@
         for f, shifted in zip(sides, shifts(change_there)):
             add = add + f * shifted
         put_rows(zbuf, 2, jnp.where(mine | jnp.logical_not(present), 0.0, add))
-        put_rows(zbuf, 3, jnp.where(black_there, coef * change_there, 0.0))
+        put_rows(zbuf, 3, jnp.where(black_there, mixed * change_there, 0.0))
         parts = restrict(zbuf, 0, 4, ny1, wres[...], 0.5 ** 10)
         v1[side, 0] = v1[side, 0] + 3.0 * (parts[0] + parts[1])
         v1[side, 1] = v1[side, 1] + parts[1]
@@ -434,27 +448,45 @@
     def at1(j):
         return 3 * far + j * (1 - 2 * far)
 
-    inside = jnp.where(has_far, 1.0, 0.0)
     cof = {j: cof1[at1(j)] for j in range(4)}
     dia = {j: dia1[at1(j)] for j in range(4)}
+    fac, for_red, for_black = {}, {}, {}
+
+    def prepare(j, mask, factor, present=None):
+        fac[j] = side_faces(cof[j], cof[j])[0]
+        if j in dia:
+            for_red[j] = jnp.where(mask, factor / dia[j], 0.0)
+            for_black[j] = jnp.where(mask, 0.0, 1.0 / dia[j])
+            if present is not None:
+                for_red[j] = jnp.where(present, for_red[j], 0.0)
+                for_black[j] = jnp.where(present, for_black[j], 0.0)
 
     def flat(j, field):
-        return cof[j] * plane_sum(field) + plane_sum(cof[j] * field)
+        total = None
+        for face, shifted in zip(fac[j], shifts(field)):
+            term = face * shifted
+            total = term if total is None else total + term
+        return total
 
     def across(i, j, field):
         return (cof[i] + cof[j]) * field
 
     def red_of(j, right):
-        return jnp.where(mask1(j), 8.0 * right / dia[j], 0.0)
+        return for_red[j] * right
 
     def black_of(j, top):
-        return jnp.where(mask1(j), 0.0, top / dia[j])
+        return for_black[j] * top
 
     wait_recv(near, true, halo_c1, s_c1, r_c1)
+    def diagonal_of(j):
+        return 6.0 * cof[j] + plane_sum(cof[j]) + (cof[j - 1] + cof[j + 1])
+
+    cof.update({4 + i: halo_c1[near, i] for i in range(3)})
+    dia.update({3: dia[3] + cof[4], 4: diagonal_of(4), 5: diagonal_of(5)})
+    for j in (1, 2, 3, 4, 5):
+        prepare(j, mask1(j), 8.0)
     wait_recv(near, true, halo_2, s_2, r_2)
     wait_recv(near, true, halo_n, s_n, r_n)
-    cof.update({4: halo_c1[near, 0], 5: halo_c1[near, 2]})
-    dia.update({3: dia[3] + cof[4], 4: halo_c1[near, 1] + cof[3], 5: halo_c1[near, 3]})
     rhs = {
         4: halo_2[near, 0] + 3.0 * (v1[near, 3] + v1[near, 4]) + v1[near, 2],
         3: v1[near, 0] + (halo_2[near, 1] + v1[near, 3]),
@@ -491,23 +523,49 @@
     second_stage(far, has_far)
     red[1], black[2], part1, part2, cross = middle()
     wait_recv(far, has_far, halo_c1, s_c1, r_c1)
-    cof.update({-1: halo_c1[far, 0], -2: halo_c1[far, 2], -3: halo_c1[far, 4]})
+    cof.update({-1 - i: halo_c1[far, i] for i in range(3)})
     dia.update({
-        -1: halo_c1[far, 1] + cof[0], -2: halo_c1[far, 3], -3: halo_c1[far, 5], 0: dia[0] + cof[-1],
+        -1: diagonal_of(-1), -2: diagonal_of(-2), -3: halo_c1[far, 3], 0: dia[0] + cof[-1],
     })
+    prepare(0, mask1(0), 8.0)
+    for j in (-1, -2, -3):
+        prepare(j, mask1(j), 8.0, has_far)
     there1, there2 = v1[far, 3], v1[far, 4]
-    more_red = jnp.where(has_far, red_of(-2, there2), 0.0)
-    more_black = jnp.where(has_far, black_of(-3, across(-3, -2, more_red)), 0.0)
+    more_red = red_of(-2, there2)
+    more_black = black_of(-3, across(-3, -2, more_red))
     fix1 = jnp.where(mask1(-1), flat(-3, more_black), across(-1, -2, more_red))
     fix2 = jnp.where(mask1(-2), across(-2, -3, more_black), 8.0 * there2 + flat(-2, more_red))
+    base0 = across(0, 1, red[1])
     end0 = v1[far, 0] + there1
     end1 = 3.0 * (there1 + there2) + v1[far, 2]
+    wait_recv(near, true, halo_c2, s_c2, r_c2)
+    wait_recv(far, has_far, halo_c2, s_c2, r_c2)
+
+    def mask2(j):
+        return parity(plane2, j + far + 4)
+
+    def at2(j):
+        return far + j * (1 - 2 * far)
+
+    levels = cof, dia, fac, for_red, for_black
+    cof = {-1: halo_c2[far, 0], 0: cof2[at2(0)], 1: cof2[at2(1)], 2: halo_c2[near, 0]}
+    dia = {
+        -1: halo_c2[far, 1] + cof[0], 0: dia2[at2(0)] + cof[-1],
+        1: dia2[at2(1)] + cof[2], 2: halo_c2[near, 1] + cof[1],
+    }
+    fac, for_red, for_black = {}, {}, {}
+    for j in (0, 1, 2):
+        prepare(j, mask2(j), 32.0)
+    prepare(-1, mask2(-1), 32.0, has_far)
+    low_cof, low_fac, low_red, low_black = cof, fac, for_red, for_black
+    cof, dia, fac, for_red, for_black = levels
+
     wait_recv(far, has_far, halo_2, s_2, r_2)
     rhs[0] = halo_2[far, 1] + end0
     rhs[-1] = halo_2[far, 0] + end1
     red[0] = red_of(0, rhs[0])
-    red[-1] = inside * red_of(-1, rhs[-1])
-    black[0] = black_of(0, 8.0 * rhs[0] + flat(0, red[0]) + across(0, -1, red[-1]) + across(0, 1, red[1]))
+    red[-1] = red_of(-1, rhs[-1])
+    black[0] = black_of(0, 8.0 * rhs[0] + base0 + across(0, -1, red[-1]) + flat(0, red[0]))
     black[1] = black_of(1, part1 + across(1, 0, red[0]))
     res = {
         3: flat(3, black[3]) + across(3, 2, black[2]) + across(3, 4, black[4]),
@@ -525,8 +583,8 @@
 
     wait_recv(far, has_far, halo_f, s_f, r_f)
     seconds = (halo_f[far, 0] + fix1, halo_f[far, 1] + fix2)
-    black[-1] = inside * black_of(-1, 8.0 * rhs[-1] + seconds[0] + flat(-1, red[-1]) + across(-1, 0, red[0]))
-    black[-2] = inside * black_of(-2, seconds[1] + across(-2, -1, red[-1]))
+    black[-1] = black_of(-1, 8.0 * rhs[-1] + seconds[0] + flat(-1, red[-1]) + across(-1, 0, red[0]))
+    black[-2] = black_of(-2, seconds[1] + across(-2, -1, red[-1]))
     more = {
         0: flat(0, black[0]) + across(0, -1, black[-1]) + across(0, 1, black[1]),
         -1: flat(-1, black[-1]) + across(-1, -2, black[-2]) + across(-1, 0, black[0]),
@@ -542,29 +600,18 @@
     for j in range(4):
         mid_ref[at1(j)] = red[j] + black[j]
 
-    wait_recv(near, true, halo_c2, s_c2, r_c2)
-    wait_recv(far, has_far, halo_c2, s_c2, r_c2)
+    cof, fac, for_red, for_black = low_cof, low_fac, low_red, low_black
+    rhs = {-1: parts[3], 0: parts[2]}
+    red = {j: red_of(j, rhs[j]) for j in (-1, 0)}
+    base0 = 32.0 * rhs[0] + flat(0, red[0]) + across(0, -1, red[-1])
+    base1 = across(1, 0, red[0])
     wait_recv(near, true, halo_3, s_3, r_3)
-
-    def mask2(j):
-        return parity(plane2, j + far + 4)
-
-    def at2(j):
-        return far + j * (1 - 2 * far)
-
-    cof = {-1: halo_c2[far, 0], 0: cof2[at2(0)], 1: cof2[at2(1)], 2: halo_c2[near, 0]}
-    dia = {
-        -1: halo_c2[far, 1] + cof[0], 0: dia2[at2(0)] + cof[-1],
-        1: dia2[at2(1)] + cof[2], 2: halo_c2[near, 1] + cof[1],
-    }
-    rhs = {
-        -1: parts[3], 0: parts[2], 1: parts[0] + halo_3[near, 1], 2: halo_3[near, 0] + parts[1],
-    }
-    red = {j: jnp.where(mask2(j), 32.0 * rhs[j] / dia[j], 0.0) for j in rhs}
-    red[-1] = inside * red[-1]
-    for j in (0, 1):
-        top = 32.0 * rhs[j] + flat(j, red[j]) + across(j, j - 1, red[j - 1]) + across(j, j + 1, red[j + 1])
-        low_ref[at2(j)] = jnp.where(mask2(j), red[j], top / dia[j])
+    rhs.update({1: parts[0] + halo_3[near, 1], 2: halo_3[near, 0] + parts[1]})
+    red.update({j: red_of(j, rhs[j]) for j in (1, 2)})
+    low_ref[at2(0)] = red[0] + black_of(0, base0 + across(0, 1, red[1]))
+    low_ref[at2(1)] = red[1] + black_of(
+        1, 32.0 * rhs[1] + base1 + across(1, 2, red[2]) + flat(1, red[1])
+    )
 
     def wait_sent(side, present, messages):
         @pl.when(present)
@@ -575,6 +622,7 @@
     for side in range(2):
         wait_sent(side, has[side], (
             (send_a.at[side], halo_a, s_a, r_a),
+            (send_h.at[side], halo_h, s_h, r_h),
             (send_d.at[side], halo_d, s_d, r_d),
             (send_q.at[side], halo_q, s_q, r_q),
             (send_c1.at[side], halo_c1, s_c1, r_c1),
@@ -609,13 +657,13 @@
         vmem(2, ny2, nx2), vmem(2, ny2, nx2),
     ]
     messages = [
-        vmem(2, ny, nx), vmem(2, 2, ny, nx), vmem(2, ny, nx), vmem(2, 6, ny1, nx1), vmem(2, 2, ny2, nx2),
+        vmem(2, ny, nx), vmem(2, ny1, nx), vmem(2, ny, nx), vmem(2, ny, nx), vmem(2, 4, ny1, nx1), vmem(2, 2, ny2, nx2),
     ]
     sent = messages + [vmem(2, 4, ny1, nx1), vmem(2, ny2, nx2)]
     halos = messages + [
         vmem(2, 2, ny1, nx1), vmem(2, ny1, nx1), vmem(2, 2, ny1, nx1), vmem(2, 2, ny2, nx2),
     ]
-    sems = [pltpu.SemaphoreType.DMA((3,))] + [pltpu.SemaphoreType.DMA((2,))] * 18
+    sems = [pltpu.SemaphoreType.DMA((3,))] + [pltpu.SemaphoreType.DMA((2,))] * 20
 
     def run(*refs):
         kernel(size, *refs)

time: 23.7 us -> 22.9 us (0.966)
  Pallas kernels: 22.9 us -> 22.2 us
    pallas_call x1, Pallas kernels: 21.9 us -> 21.2 us  [on_device(): pl.pallas_call(run, out_shape=tuple((pltpu.VMEM(shape, F32) for shape in...]
where the time goes in v6:
time: 22.9 us
  Pallas kernels  22.2 us (97%)
  between operations  0.64 us (3%)
    pallas_call x1, Pallas kernels, on_device(): pl.pallas_call(run, out_shape=tuple((pltpu.VMEM(shape, F32) for shape in...  21.2 us
    pallas_call x1, Pallas kernels, on_device(): pl.pallas_call(write_out, out_shape=tuple((jax.ShapeDtypeStruct(shape, F3...  1.03 us

profile of v6, /device:TPU:25, one launch (start us, length us, event | category | flops | bytes accessed | tf_op | source)
XLA Modules:
  0.0 22.9 jit_solution(16313497971955485312)
XLA Ops:
  0.6 21.2 %shard_map.58 = (f32[8,64,512]{2,1,0:T(8,128)S(1)}, f32[4,32,256]{2,1,0:T(8,128)S(1)}, f32[2,16,128]{2,1,0:T(8,128)S(1)}) custom-call(f32[8,64,512]{2,1,0:T(8,128)} %refs_0_.1, f32[8,64,512]{2,1,0:T(8,128)} %refs_1_.1, f32[8,64,512]{2,1,0:T(8,128)} %refs_2_.1), custom_call_target="tpu_custom_call" | custom-call | tf_op jit(solution)/shard_map/pallas_call | solution.py:676
  21.8 1.0 %shard_map.59 = (f32[8,64,512]{2,1,0:T(8,128)}, f32[4,32,256]{2,1,0:T(8,128)}, f32[2,16,128]{2,1,0:T(8,128)}) custom-call(f32[8,64,512]{2,1,0:T(8,128)S(1)} %get-tuple-element.6.p_src, f32[4,32,256]{2,1,0:T(8,128)S(1)} %get-tuple-element.7.mid_src, f32[2,16,128]{2,1,0:T(8,128)S(1)} %get-tuple-element.8.low_src), custom_call_target="tpu_custom_call" | custom-call | tf_op jit(solution)/shard_map/pallas_call | solution.py:686

commit v7 on v6

--- a/solution.py
+++ b/solution.py
@@ -70,13 +70,13 @@
     fpair, fro, frs, fbo, fbs,
     dr, db, nr,
     zbuf, zmid, wres, wsum,
-    v1, topb, cof1, dia1,
+    v1, topb, hsum, hside, c1_there, cof1, dia1,
     cof2, dia2,
-    send_a, send_h, send_d, send_q, send_c1, send_c2, send_2, send_3,
-    halo_a, halo_h, halo_d, halo_q, halo_c1, halo_c2, halo_2, halo_n, halo_f, halo_3,
+    send_x, send_q, send_c1, send_c2, send_2, send_3,
+    halo_c, halo_x, halo_q, halo_c1, halo_c2, halo_2, halo_n, halo_f, halo_3,
     load_sem,
-    s_a, s_h, s_d, s_q, s_c1, s_c2, s_2, s_n, s_f, s_3,
-    r_a, r_h, r_d, r_q, r_c1, r_c2, r_2, r_n, r_f, r_3,
+    s_c, s_x, s_q, s_c1, s_c2, s_2, s_n, s_f, s_3,
+    r_c, r_x, r_q, r_c1, r_c2, r_2, r_n, r_f, r_3,
 ):
     me = lax.axis_index("gz")
     nz, ny, nx = craw.shape
@@ -105,11 +105,43 @@
     for load in loads:
         load.start()
 
+    def copy_out(side, src, dst, s_sem, r_sem):
+        return pltpu.make_async_remote_copy(
+            src_ref=src, dst_ref=dst.at[1 - side], send_sem=s_sem.at[side],
+            recv_sem=r_sem.at[1 - side], device_id=(me + 2 * side - 1,),
+            device_id_type=pl.DeviceIdType.MESH,
+        )
+
+    def send(src_of, dst, s_sem, r_sem, allowed=True):
+        for side in range(2):
+            @pl.when(has[side] & allowed)
+            def _(side=side):
+                copy_out(side, src_of(side), dst, s_sem, r_sem).start()
+
+    def wait_recv(side, present, dst, s_sem, r_sem):
+        @pl.when(present)
+        def _():
+            pltpu.make_async_remote_copy(
+                src_ref=dst.at[side], dst_ref=dst.at[side], send_sem=s_sem.at[side],
+                recv_sem=r_sem.at[side], device_id=(me + 2 * side - 1,),
+                device_id_type=pl.DeviceIdType.MESH,
+            ).wait_recv()
+
+    def enter(allowed):
+        @pl.when(allowed)
+        def _():
+            pl.semaphore_wait(barrier, jnp.where(has[0] & has[1], 2, 1))
+
+    def send_coefficients(allowed):
+        send(lambda side: c_hbm.at[pl.ds((nz - 2) * side, 2)], halo_c, s_c, r_c, allowed)
+
+    odd, even_core = far == 1, far == 0
+    enter(odd)
+    send_coefficients(odd)
+
     for ref in (cr, cb, gb, rr, dl, rho):
         ref[0] = jnp.zeros(plane, F32)
         ref[pairs + 1] = jnp.zeros(plane, F32)
-    dl[1] = jnp.zeros(plane, F32)
-    dl[pairs] = jnp.zeros(plane, F32)
     for ref, depth in ((zbuf, ny), (zmid, ny // 2)):
         for i in range(ref.shape[0]):
             for j in range(ref.shape[1]):
@@ -118,35 +150,13 @@
     for side in range(2):
         @pl.when(jnp.logical_not(has[side]))
         def _(side=side):
-            for ref in (halo_a, halo_h, halo_d, halo_q):
+            for ref in (halo_x, halo_q, halo_c2):
                 ref[side] = jnp.zeros(ref.shape[1:], F32)
-            for ref in (halo_c1, halo_c2, halo_2, halo_f):
+            for ref in (halo_c, halo_c1, halo_2, halo_f):
                 for i in range(ref.shape[1]):
                     ref[side, i] = jnp.zeros(ref.shape[2:], F32)
     wres[...] = weights_of(wres.shape, 3.0, 1.0)
     wsum[...] = weights_of(wsum.shape, 1.0, 0.0)
-
-    def copy_out(side, src, dst, s_sem, r_sem):
-        return pltpu.make_async_remote_copy(
-            src_ref=src, dst_ref=dst.at[1 - side], send_sem=s_sem.at[side],
-            recv_sem=r_sem.at[1 - side], device_id=(me + 2 * side - 1,),
-            device_id_type=pl.DeviceIdType.MESH,
-        )
-
-    def send(src_of, dst, s_sem, r_sem, allowed=True):
-        for side in range(2):
-            @pl.when(has[side] & allowed)
-            def _(side=side):
-                copy_out(side, src_of(side), dst, s_sem, r_sem).start()
-
-    def wait_recv(side, present, dst, s_sem, r_sem):
-        @pl.when(present)
-        def _():
-            pltpu.make_async_remote_copy(
-                src_ref=dst.at[side], dst_ref=dst.at[side], send_sem=s_sem.at[side],
-                recv_sem=r_sem.at[side], device_id=(me + 2 * side - 1,),
-                device_id_type=pl.DeviceIdType.MESH,
-            ).wait_recv()
 
     even = parity(plane, 0)
 
@@ -208,20 +218,8 @@
         rr[k + 1] = top / dr[k]
         return carry
 
-    def put_first(side, carry):
-        here = (nz - 1) * side
-        send_a[side] = jnp.where(parity(plane, side), pltpu.roll(craw[here], 1, 0), graw[here])
-        return carry
-
-    def put_diagonal(side, carry):
-        k = (pairs - 1) * side
-        mine = parity(plane, side)
-        send_d[side] = jnp.where(mine, dr[k], fpair[k])
-        coef = craw[(nz - 1) * side]
-        half = ny // 2
-        send_h[side] = jnp.where(
-            parity((half, nx), side), coef[:half], pltpu.roll(coef[half:], 1, 0)
-        )
+    def put_mixed(side, carry):
+        send_x[side] = jnp.where(parity(plane, side), craw[2 + (nz - 5) * side], graw[(nz - 1) * side])
         return carry
 
     def put_tops(side, carry):
@@ -233,30 +231,18 @@
     def at_ends(body):
         lax.fori_loop(0, 2, lambda i, carry: body((pairs - 1) * i, carry), 0)
 
-    def enter(allowed):
-        @pl.when(allowed)
-        def _():
-            pl.semaphore_wait(barrier, jnp.where(has[0] & has[1], 2, 1))
-
-    odd = far == 1
     at_ends(faces)
-    lax.fori_loop(0, 2, put_diagonal, 0)
-    enter(odd)
-    send(lambda side: send_h.at[side], halo_h, s_h, r_h, odd)
-    send(lambda side: send_d.at[side], halo_d, s_d, r_d, odd)
     loads[1].wait()
-    lax.fori_loop(0, 2, put_first, 0)
-    send(lambda side: send_a.at[side], halo_a, s_a, r_a, odd)
+    lax.fori_loop(0, 2, put_mixed, 0)
+    send(lambda side: send_x.at[side], halo_x, s_x, r_x, odd)
     lax.fori_loop(0, pairs, pack_g, 0)
     loads[2].wait()
     at_ends(red)
     lax.fori_loop(0, 2, put_tops, 0)
     send(lambda side: send_q.at[side], halo_q, s_q, r_q, odd)
-    even_core = far == 0
     enter(even_core)
-    send(lambda side: send_a.at[side], halo_a, s_a, r_a, even_core)
-    send(lambda side: send_h.at[side], halo_h, s_h, r_h, even_core)
-    send(lambda side: send_d.at[side], halo_d, s_d, r_d, even_core)
+    send_coefficients(even_core)
+    send(lambda side: send_x.at[side], halo_x, s_x, r_x, even_core)
     send(lambda side: send_q.at[side], halo_q, s_q, r_q, even_core)
 
     lax.fori_loop(1, pairs - 1, faces, 0)
@@ -269,19 +255,20 @@
     def black(k, carry):
         rhs = even_first(braw[2 * k + 1], braw[2 * k])
         reds = rr[k + 1]
-        off = gather(k, reds, even_first(rr[k + 2], rr[k]), fbo, fbs)
-        new = (2.0 * rhs + off) / db[k]
+        top = 2.0 * rhs + gather(k, reds, even_first(rr[k + 2], rr[k]), fbo, fbs)
+        topb[k] = top
+        new = top / db[k]
         dl[k + 1] = new - gb[k + 1]
         put_pressure(k, reds, new)
         return carry
 
-    lax.fori_loop(1, pairs - 1, black, 0)
+    lax.fori_loop(0, pairs, black, 0)
 
     def residual(k, carry):
         rho[k + 1] = gather(k, dl[k + 1], even_first(dl[k], dl[k + 2]), fro, frs)
         return carry
 
-    lax.fori_loop(1, pairs - 1, residual, 0)
+    lax.fori_loop(0, pairs, residual, 0)
 
     ny1, ny2 = ny // 2, ny // 4
     rows = [
@@ -327,12 +314,14 @@
         cof2[k] = c2[k]
         dia2[k] = d2[k]
     for side in range(2):
-        ends = (3 * side, 1 + side, 2 - side)
-        for i, end in enumerate(ends):
-            send_c1[side, i] = c1[end]
-        send_c1[side, 3] = d1[ends[2]]
-        send_c2[side, 0] = c2[side]
-        send_c2[side, 1] = d2[side]
+        send_c1[side, 0] = c1[1 + side]
+        send_c1[side, 1] = c1[2 - side]
+        diagonal = d1[2 - side]
+        send_c2[side, :, 0 : nx // 2] = jnp.where(
+            parity((ny2, nx // 2), side + 1), diagonal[:ny2], pltpu.roll(diagonal[ny2:], 1, 0)
+        )
+        send_c2[side, :, nx // 2 : 3 * nx // 4] = c2[side]
+        send_c2[side, :, 3 * nx // 4 : nx] = d2[side]
     send(lambda side: send_c1.at[side], halo_c1, s_c1, r_c1)
     send(lambda side: send_c2.at[side], halo_c2, s_c2, r_c2)
 
@@ -345,101 +334,102 @@
         out = scale * dot_parts(jnp.concatenate(rows, axis=0), weights)
         return [out[k * out_rows : (k + 1) * out_rows] for k in range(count)]
 
-    def first_stage(side, present, is_near):
-        wait_recv(side, present, halo_a, s_a, r_a)
-        k = (pairs - 1) * side
+    def along_z(k, carry):
+        put_rows(zbuf, k, 3.0 * rho[k + 1] + even_first(rho[k + 2], rho[k]))
+        return carry
+
+    lax.fori_loop(0, pairs, along_z, 0)
+    put_rows(zbuf, pairs, even_first(rho[1], 0.0))
+    put_rows(zbuf, pairs + 1, even_first(0.0, rho[pairs]))
+    parts = restrict(zbuf, 0, pairs + 2, ny1, wres[...], 0.5 ** 10)
+    for side in range(2):
+        ends = (3 * side, 1 + side, 4 + side)
+        for i, end in enumerate(ends):
+            v1[side, i] = parts[end]
+        send_2[side, 0] = parts[ends[0]]
+        send_2[side, 1] = parts[ends[2]]
+        send_2[side, 2] = (c1[ends[0]] + c1[ends[1]]) * (8.0 * parts[ends[1]] / d1[ends[1]])
+    send(lambda side: send_2.at[side, 0:2], halo_2, s_2, r_2)
+    copy_out(near, send_2.at[near, 2], halo_n, s_n, r_n).start()
+
+    def planes_there(side, present):
+        wait_recv(side, present, halo_c, s_c, r_c)
         mine = parity(plane, side)
-        field = halo_a[side]
-        coef = pltpu.roll(field, ny - 1, 0)
-        face = craw[(nz - 1) * side] + coef
-        value = (nr[k] + face * field) / (dr[k] + coef)
-        reds = jnp.where(mine, value, rr[k + 1])
-        rr[k + 1] = reds
-        rhs = even_first(braw[2 * k + 1], braw[2 * k])
-        top = 2.0 * rhs + gather(k, reds, even_first(rr[k + 2], rr[k]), fbo, fbs)
-        topb[side] = top
-        new = top / db[k]
-        delta = new - gb[k + 1]
-        dl[k + 1] = delta
-        put_pressure(k, reds, new)
-        own = gather(k, delta, even_first(dl[k], dl[k + 2]), fro, frs)
-        rho[k + 1] = own
-        inner = k + 1 - 2 * side
-        more = (cr[inner + 1] + cb[k + 1]) * delta
-        rho[inner + 1] = rho[inner + 1] + jnp.where(mine, more, 0.0)
-
-        def along_z(at):
-            return 3.0 * rho[at + 1] + even_first(rho[at + 2], rho[at])
-
-        put_rows(zbuf, 0, along_z(k))
-        put_rows(zbuf, 1, jnp.where(mine, own, 0.0))
-        parts = restrict(zbuf, 0, 2, ny1, wres[...], 0.5 ** 10)
-        send_2[side, 0] = parts[0]
-        send_2[side, 1] = parts[1]
-
-        @pl.when(present)
-        def _():
-            copy_out(side, send_2.at[side, 0:2], halo_2, s_2, r_2).start()
-
-        v1[side, 0] = parts[0]
-        v1[side, 2] = parts[1]
-        put_rows(zbuf, 2, along_z(inner))
-        (middle,) = restrict(zbuf, 2, 1, ny1, wres[...], 0.5 ** 10)
-        v1[side, 1] = middle
-        if is_near:
-            send_2[side, 2] = (cof1[k] + cof1[inner]) * (8.0 * middle / dia1[inner])
-            copy_out(side, send_2.at[side, 2], halo_n, s_n, r_n).start()
+        hc0, hc1 = halo_c[side, 1 - side], halo_c[side, side]
+        sides0, around = side_faces(hc0, hc0)
+        hsum[0] = 6.0 * hc0 + around + hc1
+        sides1, around = side_faces(hc1, hc1)
+        hsum[1] = 6.0 * hc1 + around + hc0
+        for i, (f0, f1) in enumerate(zip(sides0, sides1)):
+            hside[0, i] = f0
+            hside[1, i] = jnp.where(mine, f1, f0)
+        put_rows(zbuf, 0, hc0 + hc1)
+        rows = get_rows(zbuf, 0, 8, ny1) + get_rows(zbuf, 0, 9, ny1)
+        c1_there[side] = 0.125 * dot_parts(rows, wsum[...])
 
     def second_stage(side, present):
-        wait_recv(side, present, halo_h, s_h, r_h)
-        wait_recv(side, present, halo_d, s_d, r_d)
+        planes_there(side, present)
+        wait_recv(side, present, halo_x, s_x, r_x)
         wait_recv(side, present, halo_q, s_q, r_q)
         k = (pairs - 1) * side
         here = (nz - 1) * side
+        inner = k + 1 - 2 * side
         mine = parity(plane, side)
-        black_there = mine & present
-        field = halo_a[side]
-        half, mixed, tops = halo_h[side], halo_d[side], halo_q[side]
+        hc0, hc1 = halo_c[side, 1 - side], halo_c[side, side]
+        mixed, tops = halo_x[side], halo_q[side]
         c0, g0 = craw[here], graw[here]
-        half = jnp.concatenate([half, pltpu.roll(half, ny // 2 - 1, 0)], axis=0)
-        hc = jnp.where(mine, pltpu.roll(field, ny - 1, 0), half)
-        face = c0 + hc
-        value = jnp.where(present, (tops + face * g0) / (mixed + c0), 0.0)
-        sides, around = side_faces(hc, hc)
-        diagonal = 5.0 * hc + around + mixed
+        face, pair = c0 + hc0, hc0 + hc1
+        diagonal0, diagonal1 = hsum[0], hsum[1] + mixed
+
+        new = (jnp.where(mine, nr[k], tops) + face * jnp.where(mine, mixed, g0)) / (
+            jnp.where(mine, dr[k] + hc0, diagonal0 + c0)
+        )
+        there = jnp.where(present, new, 0.0)
+        there_old = jnp.where(present, tops / diagonal0, 0.0)
+        old = rr[k + 1]
+        reds = jnp.where(mine, new, old)
+        change = jnp.where(mine, new - old, 0.0)
+
+        top = topb[k] + fpair[k] * change + jnp.where(mine, 0.0, face * there)
+        for i, shifted in enumerate(shifts(change)):
+            top = top + fbs[k, i] * shifted
+        blacks = top / (db[k] + jnp.where(mine, 0.0, hc0))
+        put_pressure(k, reds, blacks)
+        delta = blacks - gb[k + 1]
+        change = delta - dl[k + 1]
+
         short = tops
-        for f, shifted in zip(sides, shifts(value)):
-            short = short + f * shifted
-        reds = rr[k + 1]
-        new = (jnp.where(mine, short, topb[side]) + face * jnp.where(mine, reds, value)) / (
-            jnp.where(mine, diagonal + c0, db[k] + hc)
-        )
-        old = dl[k + 1]
-        delta = new - gb[k + 1]
-        change = jnp.where(mine, 0.0, delta - old)
-        dl[k + 1] = jnp.where(mine, old, delta)
-        p_ref[here] = jnp.where(mine, reds, new)
-        delta_there = jnp.where(black_there, new - field, 0.0)
-        change_there = jnp.where(black_there, new - short / diagonal, 0.0)
-        add = fpair[k] * change
+        for i, shifted in enumerate(shifts(there_old)):
+            short = short + hside[0, i] * shifted
+        full = tops + face * new
+        for i, shifted in enumerate(shifts(there)):
+            full = full + hside[0, i] * shifted
+        blacks = full / (diagonal0 + c0)
+        part = jnp.where(mine, short, pair * (there_old - there)) / jnp.where(mine, diagonal0, diagonal1)
+        change_there = jnp.where(present, jnp.where(mine, blacks, 0.0) - part, 0.0)
+        delta_there = jnp.where(present, blacks - mixed, 0.0)
+
+        add = fpair[k] * change + jnp.where(mine, face * delta_there, 0.0)
         for i, shifted in enumerate(shifts(change)):
             add = add + frs[k, i] * shifted
-        put_rows(zbuf, 0, jnp.where(mine, add + face * delta_there, 0.0))
+        put_rows(zbuf, 0, jnp.where(mine, add, 0.0))
         put_rows(zbuf, 1, jnp.where(mine, 0.0, add))
-        add = face * delta
-        for f, shifted in zip(sides, shifts(change_there)):
-            add = add + f * shifted
-        put_rows(zbuf, 2, jnp.where(mine | jnp.logical_not(present), 0.0, add))
-        put_rows(zbuf, 3, jnp.where(black_there, mixed * change_there, 0.0))
-        parts = restrict(zbuf, 0, 4, ny1, wres[...], 0.5 ** 10)
-        v1[side, 0] = v1[side, 0] + 3.0 * (parts[0] + parts[1])
-        v1[side, 1] = v1[side, 1] + parts[1]
-        v1[side, 2] = v1[side, 2] + parts[0]
-        v1[side, 3] = parts[2]
-        v1[side, 4] = parts[3]
+        put_rows(zbuf, 2, jnp.where(mine, (cr[inner + 1] + cb[k + 1]) * change, 0.0))
+        add = pair * change_there + jnp.where(mine | jnp.logical_not(present), 0.0, face * delta)
+        for i, shifted in enumerate(shifts(change_there)):
+            add = add + hside[1, i] * shifted
+        put_rows(zbuf, 3, jnp.where(mine, 0.0, add))
+        put_rows(zbuf, 4, jnp.where(mine, add, 0.0))
+        put_rows(zbuf, 5, jnp.where(mine, 0.0, (mixed + hc1) * change_there))
+        own0, own1, own2, end0, end1, end2 = restrict(zbuf, 0, 6, ny1, wres[...], 0.5 ** 10)
+        v1[side, 0] = v1[side, 0] + (3.0 * (own0 + own1) + own2)
+        v1[side, 1] = v1[side, 1] + (3.0 * own2 + own1)
+        v1[side, 2] = v1[side, 2] + own0
+        v1[side, 3] = end0
+        v1[side, 4] = 3.0 * (end0 + end1) + end2
+        v1[side, 5] = 3.0 * end2 + end1
 
     true = me >= 0
-    first_stage(near, true, True)
     second_stage(near, true)
 
     def mask1(j):
@@ -481,20 +471,20 @@
     def diagonal_of(j):
         return 6.0 * cof[j] + plane_sum(cof[j]) + (cof[j - 1] + cof[j + 1])
 
-    cof.update({4 + i: halo_c1[near, i] for i in range(3)})
+    cof.update({4: c1_there[near], 5: halo_c1[near, 0], 6: halo_c1[near, 1]})
     dia.update({3: dia[3] + cof[4], 4: diagonal_of(4), 5: diagonal_of(5)})
     for j in (1, 2, 3, 4, 5):
         prepare(j, mask1(j), 8.0)
     wait_recv(near, true, halo_2, s_2, r_2)
     wait_recv(near, true, halo_n, s_n, r_n)
     rhs = {
-        4: halo_2[near, 0] + 3.0 * (v1[near, 3] + v1[near, 4]) + v1[near, 2],
+        4: halo_2[near, 0] + v1[near, 4] + v1[near, 2],
         3: v1[near, 0] + (halo_2[near, 1] + v1[near, 3]),
         2: v1[near, 1],
     }
     red = {j: red_of(j, rhs[j]) for j in (2, 3, 4)}
     black = {}
-    beyond = halo_n[near] + across(4, 5, red_of(5, v1[near, 4]))
+    beyond = halo_n[near] + across(4, 5, red_of(5, v1[near, 5]))
     black[4] = black_of(4, 8.0 * rhs[4] + beyond + flat(4, red[4]) + across(4, 3, red[3]))
     black[3] = black_of(
         3, 8.0 * rhs[3] + flat(3, red[3]) + across(3, 4, red[4]) + across(3, 2, red[2])
@@ -511,7 +501,6 @@
         part2 = flat(2, black2) + base3
         return red1, black2, part1, part2, across(1, 2, black2)
 
-    first_stage(far, has_far, False)
     red1, black2, part1, part2, cross = middle()
     send_2[far, 2] = jnp.where(mask1(0), part2, across(0, 1, red1))
     send_2[far, 3] = jnp.where(mask1(1), cross, part1)
@@ -523,24 +512,25 @@
     second_stage(far, has_far)
     red[1], black[2], part1, part2, cross = middle()
     wait_recv(far, has_far, halo_c1, s_c1, r_c1)
-    cof.update({-1 - i: halo_c1[far, i] for i in range(3)})
+    wait_recv(near, true, halo_c2, s_c2, r_c2)
+    wait_recv(far, has_far, halo_c2, s_c2, r_c2)
+    cof.update({-1: c1_there[far], -2: halo_c1[far, 0], -3: halo_c1[far, 1]})
+    packed = halo_c2[far, :, 0 : nx // 2]
+    packed = jnp.concatenate([packed, pltpu.roll(packed, ny2 - 1, 0)], axis=0)
     dia.update({
-        -1: diagonal_of(-1), -2: diagonal_of(-2), -3: halo_c1[far, 3], 0: dia[0] + cof[-1],
+        -1: diagonal_of(-1), -2: diagonal_of(-2), -3: packed, 0: dia[0] + cof[-1],
     })
     prepare(0, mask1(0), 8.0)
     for j in (-1, -2, -3):
         prepare(j, mask1(j), 8.0, has_far)
-    there1, there2 = v1[far, 3], v1[far, 4]
+    there1, there2 = v1[far, 3], v1[far, 5]
     more_red = red_of(-2, there2)
     more_black = black_of(-3, across(-3, -2, more_red))
     fix1 = jnp.where(mask1(-1), flat(-3, more_black), across(-1, -2, more_red))
     fix2 = jnp.where(mask1(-2), across(-2, -3, more_black), 8.0 * there2 + flat(-2, more_red))
     base0 = across(0, 1, red[1])
     end0 = v1[far, 0] + there1
-    end1 = 3.0 * (there1 + there2) + v1[far, 2]
-    wait_recv(near, true, halo_c2, s_c2, r_c2)
-    wait_recv(far, has_far, halo_c2, s_c2, r_c2)
-
+    end1 = v1[far, 4] + v1[far, 2]
     def mask2(j):
         return parity(plane2, j + far + 4)
 
@@ -548,10 +538,16 @@
         return far + j * (1 - 2 * far)
 
     levels = cof, dia, fac, for_red, for_black
-    cof = {-1: halo_c2[far, 0], 0: cof2[at2(0)], 1: cof2[at2(1)], 2: halo_c2[near, 0]}
+    def coef2(side):
+        return halo_c2[side, :, nx // 2 : 3 * nx // 4]
+
+    def diagonal2(side):
+        return halo_c2[side, :, 3 * nx // 4 : nx]
+
+    cof = {-1: coef2(far), 0: cof2[at2(0)], 1: cof2[at2(1)], 2: coef2(near)}
     dia = {
-        -1: halo_c2[far, 1] + cof[0], 0: dia2[at2(0)] + cof[-1],
-        1: dia2[at2(1)] + cof[2], 2: halo_c2[near, 1] + cof[1],
+        -1: diagonal2(far) + cof[0], 0: dia2[at2(0)] + cof[-1],
+        1: dia2[at2(1)] + cof[2], 2: diagonal2(near) + cof[1],
     }
     fac, for_red, for_black = {}, {}, {}
     for j in (0, 1, 2):
@@ -621,9 +617,8 @@
 
     for side in range(2):
         wait_sent(side, has[side], (
-            (send_a.at[side], halo_a, s_a, r_a),
-            (send_h.at[side], halo_h, s_h, r_h),
-            (send_d.at[side], halo_d, s_d, r_d),
+            (c_hbm.at[pl.ds((nz - 2) * side, 2)], halo_c, s_c, r_c),
+            (send_x.at[side], halo_x, s_x, r_x),
             (send_q.at[side], halo_q, s_q, r_q),
             (send_c1.at[side], halo_c1, s_c1, r_c1),
             (send_c2.at[side], halo_c2, s_c2, r_c2),
@@ -653,17 +648,18 @@
     work = [
         vmem(pairs + 2, nx // 128, ny + 16, 128), vmem(4, nx1 // 128, ny1 + 16, 128),
         pltpu.VMEM((nx, nx1), BF16), pltpu.VMEM((nx, nx1), BF16),
-        vmem(2, 5, ny1, nx1), vmem(2, ny, nx), vmem(pairs, ny1, nx1), vmem(pairs, ny1, nx1),
+        vmem(2, 6, ny1, nx1), vmem(pairs, ny, nx), vmem(2, ny, nx), vmem(2, 4, ny, nx),
+        vmem(2, ny1, nx1), vmem(pairs, ny1, nx1), vmem(pairs, ny1, nx1),
         vmem(2, ny2, nx2), vmem(2, ny2, nx2),
     ]
     messages = [
-        vmem(2, ny, nx), vmem(2, ny1, nx), vmem(2, ny, nx), vmem(2, ny, nx), vmem(2, 4, ny1, nx1), vmem(2, 2, ny2, nx2),
+        vmem(2, ny, nx), vmem(2, ny, nx), vmem(2, 2, ny1, nx1), vmem(2, ny2, nx),
     ]
     sent = messages + [vmem(2, 4, ny1, nx1), vmem(2, ny2, nx2)]
-    halos = messages + [
+    halos = [vmem(2, 2, ny, nx)] + messages + [
         vmem(2, 2, ny1, nx1), vmem(2, ny1, nx1), vmem(2, 2, ny1, nx1), vmem(2, 2, ny2, nx2),
     ]
-    sems = [pltpu.SemaphoreType.DMA((3,))] + [pltpu.SemaphoreType.DMA((2,))] * 20
+    sems = [pltpu.SemaphoreType.DMA((3,))] + [pltpu.SemaphoreType.DMA((2,))] * 18
 
     def run(*refs):
         kernel(size, *refs)

time: 22.9 us -> 21.2 us (0.926)
  Pallas kernels: 22.2 us -> 20.5 us
    pallas_call x1, Pallas kernels: 21.2 us -> 19.4 us  [on_device(): pl.pallas_call(run, out_shape=tuple((pltpu.VMEM(shape, F32) for shape in...]
where the time goes in v7:
time: 21.2 us; the launch traced here: 21.1 us
  Pallas kernels  20.5 us (97%)
  between operations  0.64 us (3%)
    pallas_call x1, Pallas kernels, on_device(): pl.pallas_call(run, out_shape=tuple((pltpu.VMEM(shape, F32) for shape in...  19.4 us
    pallas_call x1, Pallas kernels, on_device(): pl.pallas_call(write_out, out_shape=tuple((jax.ShapeDtypeStruct(shape, F3...  1.03 us

profile of v7, /device:TPU:25, one launch (start us, length us, event | category | flops | bytes accessed | tf_op | source)
XLA Modules:
  0.0 21.1 jit_solution(15876573476400143916)
XLA Ops:
  0.6 19.4 %shard_map.58 = (f32[8,64,512]{2,1,0:T(8,128)S(1)}, f32[4,32,256]{2,1,0:T(8,128)S(1)}, f32[2,16,128]{2,1,0:T(8,128)S(1)}) custom-call(f32[8,64,512]{2,1,0:T(8,128)} %refs_0_.1, f32[8,64,512]{2,1,0:T(8,128)} %refs_1_.1, f32[8,64,512]{2,1,0:T(8,128)} %refs_2_.1), custom_call_target="tpu_custom_call" | custom-call | tf_op jit(solution)/shard_map/pallas_call | solution.py:672
  20.1 1.0 %shard_map.59 = (f32[8,64,512]{2,1,0:T(8,128)}, f32[4,32,256]{2,1,0:T(8,128)}, f32[2,16,128]{2,1,0:T(8,128)}) custom-call(f32[8,64,512]{2,1,0:T(8,128)S(1)} %get-tuple-element.6.p_src, f32[4,32,256]{2,1,0:T(8,128)S(1)} %get-tuple-element.7.mid_src, f32[2,16,128]{2,1,0:T(8,128)S(1)} %get-tuple-element.8.low_src), custom_call_target="tpu_custom_call" | custom-call | tf_op jit(solution)/shard_map/pallas_call | solution.py:682

commit v8 on v7

--- a/solution.py
+++ b/solution.py
@@ -72,11 +72,11 @@
     zbuf, zmid, wres, wsum,
     v1, topb, hsum, hside, c1_there, cof1, dia1,
     cof2, dia2,
-    send_x, send_q, send_c1, send_c2, send_2, send_3,
-    halo_c, halo_x, halo_q, halo_c1, halo_c2, halo_2, halo_n, halo_f, halo_3,
+    send_x, send_q, send_c1, send_d1, send_c2, send_2, send_3,
+    halo_c, halo_x, halo_q, halo_c1, halo_d1, halo_c2, halo_2, halo_n, halo_f, halo_3,
     load_sem,
-    s_c, s_x, s_q, s_c1, s_c2, s_2, s_n, s_f, s_3,
-    r_c, r_x, r_q, r_c1, r_c2, r_2, r_n, r_f, r_3,
+    s_c, s_x, s_q, s_c1, s_d1, s_c2, s_2, s_n, s_f, s_3,
+    r_c, r_x, r_q, r_c1, r_d1, r_c2, r_2, r_n, r_f, r_3,
 ):
     me = lax.axis_index("gz")
     nz, ny, nx = craw.shape
@@ -150,9 +150,9 @@
     for side in range(2):
         @pl.when(jnp.logical_not(has[side]))
         def _(side=side):
-            for ref in (halo_x, halo_q, halo_c2):
+            for ref in (halo_x, halo_q, halo_c1, halo_d1, halo_c2):
                 ref[side] = jnp.zeros(ref.shape[1:], F32)
-            for ref in (halo_c, halo_c1, halo_2, halo_f):
+            for ref in (halo_c, halo_2, halo_f):
                 for i in range(ref.shape[1]):
                     ref[side, i] = jnp.zeros(ref.shape[2:], F32)
     wres[...] = weights_of(wres.shape, 3.0, 1.0)
@@ -222,12 +222,6 @@
         send_x[side] = jnp.where(parity(plane, side), craw[2 + (nz - 5) * side], graw[(nz - 1) * side])
         return carry
 
-    def put_tops(side, carry):
-        k = (pairs - 1) * side
-        rhs = even_first(braw[2 * k + 1], braw[2 * k])
-        send_q[side] = jnp.where(parity(plane, side), nr[k], 2.0 * rhs + fpair[k] * rr[k + 1])
-        return carry
-
     def at_ends(body):
         lax.fori_loop(0, 2, lambda i, carry: body((pairs - 1) * i, carry), 0)
 
@@ -238,12 +232,9 @@
     lax.fori_loop(0, pairs, pack_g, 0)
     loads[2].wait()
     at_ends(red)
-    lax.fori_loop(0, 2, put_tops, 0)
-    send(lambda side: send_q.at[side], halo_q, s_q, r_q, odd)
     enter(even_core)
     send_coefficients(even_core)
     send(lambda side: send_x.at[side], halo_x, s_x, r_x, even_core)
-    send(lambda side: send_q.at[side], halo_q, s_q, r_q, even_core)
 
     lax.fori_loop(1, pairs - 1, faces, 0)
     lax.fori_loop(1, pairs - 1, red, 0)
@@ -262,7 +253,16 @@
         put_pressure(k, reds, new)
         return carry
 
-    lax.fori_loop(0, pairs, black, 0)
+    at_ends(black)
+
+    def put_tops(side, carry):
+        k = (pairs - 1) * side
+        send_q[side] = jnp.where(parity(plane, side), rr[k + 1], topb[k])
+        return carry
+
+    lax.fori_loop(0, 2, put_tops, 0)
+    send(lambda side: send_q.at[side], halo_q, s_q, r_q)
+    lax.fori_loop(1, pairs - 1, black, 0)
 
     def residual(k, carry):
         rho[k + 1] = gather(k, dl[k + 1], even_first(dl[k], dl[k + 2]), fro, frs)
@@ -314,8 +314,8 @@
         cof2[k] = c2[k]
         dia2[k] = d2[k]
     for side in range(2):
-        send_c1[side, 0] = c1[1 + side]
-        send_c1[side, 1] = c1[2 - side]
+        send_c1[side] = c1[1 + side]
+        send_d1[side] = c1[2 - side]
         diagonal = d1[2 - side]
         send_c2[side, :, 0 : nx // 2] = jnp.where(
             parity((ny2, nx // 2), side + 1), diagonal[:ny2], pltpu.roll(diagonal[ny2:], 1, 0)
@@ -323,7 +323,6 @@
         send_c2[side, :, nx // 2 : 3 * nx // 4] = c2[side]
         send_c2[side, :, 3 * nx // 4 : nx] = d2[side]
     send(lambda side: send_c1.at[side], halo_c1, s_c1, r_c1)
-    send(lambda side: send_c2.at[side], halo_c2, s_c2, r_c2)
 
     def restrict(ref, first, count, out_rows, weights, scale):
         rows = [
@@ -351,6 +350,8 @@
         send_2[side, 2] = (c1[ends[0]] + c1[ends[1]]) * (8.0 * parts[ends[1]] / d1[ends[1]])
     send(lambda side: send_2.at[side, 0:2], halo_2, s_2, r_2)
     copy_out(near, send_2.at[near, 2], halo_n, s_n, r_n).start()
+    send(lambda side: send_d1.at[side], halo_d1, s_d1, r_d1)
+    send(lambda side: send_c2.at[side], halo_c2, s_c2, r_c2)
 
     def planes_there(side, present):
         wait_recv(side, present, halo_c, s_c, r_c)
@@ -370,42 +371,41 @@
     def second_stage(side, present):
         planes_there(side, present)
         wait_recv(side, present, halo_x, s_x, r_x)
-        wait_recv(side, present, halo_q, s_q, r_q)
         k = (pairs - 1) * side
         here = (nz - 1) * side
         inner = k + 1 - 2 * side
         mine = parity(plane, side)
-        hc0, hc1 = halo_c[side, 1 - side], halo_c[side, side]
-        mixed, tops = halo_x[side], halo_q[side]
+        hc0, hc1, mixed = halo_c[side, 1 - side], halo_c[side, side], halo_x[side]
         c0, g0 = craw[here], graw[here]
         face, pair = c0 + hc0, hc0 + hc1
-        diagonal0, diagonal1 = hsum[0], hsum[1] + mixed
-
-        new = (jnp.where(mine, nr[k], tops) + face * jnp.where(mine, mixed, g0)) / (
-            jnp.where(mine, dr[k] + hc0, diagonal0 + c0)
-        )
-        there = jnp.where(present, new, 0.0)
-        there_old = jnp.where(present, tops / diagonal0, 0.0)
+        diagonal = hsum[0]
+        for_new = 1.0 / (diagonal + c0)
+        for_old = 1.0 / jnp.where(mine, diagonal, hsum[1] + mixed)
+        for_own = 1.0 / (db[k] + jnp.where(mine, 0.0, hc0))
+
         old = rr[k + 1]
+        new = (nr[k] + face * mixed) / (dr[k] + hc0)
         reds = jnp.where(mine, new, old)
         change = jnp.where(mine, new - old, 0.0)
-
-        top = topb[k] + fpair[k] * change + jnp.where(mine, 0.0, face * there)
+        top = topb[k] + fpair[k] * change
         for i, shifted in enumerate(shifts(change)):
             top = top + fbs[k, i] * shifted
-        blacks = top / (db[k] + jnp.where(mine, 0.0, hc0))
+
+        wait_recv(side, present, halo_q, s_q, r_q)
+        tops = halo_q[side]
+        there = jnp.where(present, (tops * diagonal + face * g0) * for_new, 0.0)
+        change_there = jnp.where(mine, 0.0, there - tops)
+
+        blacks = (top + jnp.where(mine, 0.0, face * there)) * for_own
         put_pressure(k, reds, blacks)
         delta = blacks - gb[k + 1]
         change = delta - dl[k + 1]
 
-        short = tops
-        for i, shifted in enumerate(shifts(there_old)):
-            short = short + hside[0, i] * shifted
         full = tops + face * new
-        for i, shifted in enumerate(shifts(there)):
+        for i, shifted in enumerate(shifts(change_there)):
             full = full + hside[0, i] * shifted
-        blacks = full / (diagonal0 + c0)
-        part = jnp.where(mine, short, pair * (there_old - there)) / jnp.where(mine, diagonal0, diagonal1)
+        blacks = full * for_new
+        part = jnp.where(mine, tops, -(pair * change_there)) * for_old
         change_there = jnp.where(present, jnp.where(mine, blacks, 0.0) - part, 0.0)
         delta_there = jnp.where(present, blacks - mixed, 0.0)
 
@@ -468,10 +468,11 @@
         return for_black[j] * top
 
     wait_recv(near, true, halo_c1, s_c1, r_c1)
+    wait_recv(near, true, halo_d1, s_d1, r_d1)
     def diagonal_of(j):
         return 6.0 * cof[j] + plane_sum(cof[j]) + (cof[j - 1] + cof[j + 1])
 
-    cof.update({4: c1_there[near], 5: halo_c1[near, 0], 6: halo_c1[near, 1]})
+    cof.update({4: c1_there[near], 5: halo_c1[near], 6: halo_d1[near]})
     dia.update({3: dia[3] + cof[4], 4: diagonal_of(4), 5: diagonal_of(5)})
     for j in (1, 2, 3, 4, 5):
         prepare(j, mask1(j), 8.0)
@@ -509,53 +510,38 @@
     def _():
         copy_out(far, send_2.at[far, 2:4], halo_f, s_f, r_f).start()
 
+    def mask2(j):
+        return parity(plane2, j + far + 4)
+
+    def at2(j):
+        return far + j * (1 - 2 * far)
+
+    def coef2(side):
+        return halo_c2[side, :, nx // 2 : 3 * nx // 4]
+
+    def diagonal2(side):
+        return halo_c2[side, :, 3 * nx // 4 : nx]
+
+    wait_recv(near, true, halo_c2, s_c2, r_c2)
+    levels = cof, dia, fac, for_red, for_black
+    cof = {0: cof2[at2(0)], 1: cof2[at2(1)], 2: coef2(near)}
+    dia = {1: dia2[at2(1)] + cof[2], 2: diagonal2(near) + cof[1]}
+    fac, for_red, for_black = {}, {}, {}
+    for j in (1, 2):
+        prepare(j, mask2(j), 32.0)
+    lows = cof, dia, fac, for_red, for_black
+    cof, dia, fac, for_red, for_black = levels
+
     second_stage(far, has_far)
     red[1], black[2], part1, part2, cross = middle()
     wait_recv(far, has_far, halo_c1, s_c1, r_c1)
-    wait_recv(near, true, halo_c2, s_c2, r_c2)
-    wait_recv(far, has_far, halo_c2, s_c2, r_c2)
-    cof.update({-1: c1_there[far], -2: halo_c1[far, 0], -3: halo_c1[far, 1]})
-    packed = halo_c2[far, :, 0 : nx // 2]
-    packed = jnp.concatenate([packed, pltpu.roll(packed, ny2 - 1, 0)], axis=0)
-    dia.update({
-        -1: diagonal_of(-1), -2: diagonal_of(-2), -3: packed, 0: dia[0] + cof[-1],
-    })
+    cof.update({-1: c1_there[far], -2: halo_c1[far]})
+    dia.update({-1: diagonal_of(-1), 0: dia[0] + cof[-1]})
     prepare(0, mask1(0), 8.0)
-    for j in (-1, -2, -3):
-        prepare(j, mask1(j), 8.0, has_far)
-    there1, there2 = v1[far, 3], v1[far, 5]
-    more_red = red_of(-2, there2)
-    more_black = black_of(-3, across(-3, -2, more_red))
-    fix1 = jnp.where(mask1(-1), flat(-3, more_black), across(-1, -2, more_red))
-    fix2 = jnp.where(mask1(-2), across(-2, -3, more_black), 8.0 * there2 + flat(-2, more_red))
+    prepare(-1, mask1(-1), 8.0, has_far)
     base0 = across(0, 1, red[1])
-    end0 = v1[far, 0] + there1
+    end0 = v1[far, 0] + v1[far, 3]
     end1 = v1[far, 4] + v1[far, 2]
-    def mask2(j):
-        return parity(plane2, j + far + 4)
-
-    def at2(j):
-        return far + j * (1 - 2 * far)
-
-    levels = cof, dia, fac, for_red, for_black
-    def coef2(side):
-        return halo_c2[side, :, nx // 2 : 3 * nx // 4]
-
-    def diagonal2(side):
-        return halo_c2[side, :, 3 * nx // 4 : nx]
-
-    cof = {-1: coef2(far), 0: cof2[at2(0)], 1: cof2[at2(1)], 2: coef2(near)}
-    dia = {
-        -1: diagonal2(far) + cof[0], 0: dia2[at2(0)] + cof[-1],
-        1: dia2[at2(1)] + cof[2], 2: diagonal2(near) + cof[1],
-    }
-    fac, for_red, for_black = {}, {}, {}
-    for j in (0, 1, 2):
-        prepare(j, mask2(j), 32.0)
-    prepare(-1, mask2(-1), 32.0, has_far)
-    low_cof, low_fac, low_red, low_black = cof, fac, for_red, for_black
-    cof, dia, fac, for_red, for_black = levels
-
     wait_recv(far, has_far, halo_2, s_2, r_2)
     rhs[0] = halo_2[far, 1] + end0
     rhs[-1] = halo_2[far, 0] + end1
@@ -577,26 +563,51 @@
     send_3[1] = parts[1]
     copy_out(near, send_3, halo_3, s_3, r_3).start()
 
+    wait_recv(far, has_far, halo_d1, s_d1, r_d1)
+    wait_recv(far, has_far, halo_c2, s_c2, r_c2)
+    cof[-3] = halo_d1[far]
+    packed = halo_c2[far, :, 0 : nx // 2]
+    packed = jnp.concatenate([packed, pltpu.roll(packed, ny2 - 1, 0)], axis=0)
+    dia.update({-2: diagonal_of(-2), -3: packed})
+    for j in (-2, -3):
+        prepare(j, mask1(j), 8.0, has_far)
+    there2 = v1[far, 5]
+    more_red = red_of(-2, there2)
+    more_black = black_of(-3, across(-3, -2, more_red))
+    fix1 = jnp.where(mask1(-1), flat(-3, more_black), across(-1, -2, more_red))
+    fix2 = jnp.where(mask1(-2), across(-2, -3, more_black), 8.0 * there2 + flat(-2, more_red))
+
+    cof, dia, fac, for_red, for_black = lows
+    cof[-1] = coef2(far)
+    dia.update({-1: diagonal2(far) + cof[0], 0: dia2[at2(0)] + cof[-1]})
+    prepare(0, mask2(0), 32.0)
+    prepare(-1, mask2(-1), 32.0, has_far)
+    cof, dia, fac, for_red, for_black = levels
+
+    before1 = 8.0 * rhs[-1] + fix1 + flat(-1, red[-1]) + across(-1, 0, red[0])
+    before2 = fix2 + across(-2, -1, red[-1])
+    before0 = flat(0, black[0]) + across(0, 1, black[1])
+    before3 = across(-1, 0, black[0])
+    inner_rows = 3.0 * res[1] + res[2]
+    for j in range(4):
+        mid_ref[at1(j)] = red[j] + black[j]
     wait_recv(far, has_far, halo_f, s_f, r_f)
-    seconds = (halo_f[far, 0] + fix1, halo_f[far, 1] + fix2)
-    black[-1] = black_of(-1, 8.0 * rhs[-1] + seconds[0] + flat(-1, red[-1]) + across(-1, 0, red[0]))
-    black[-2] = black_of(-2, seconds[1] + across(-2, -1, red[-1]))
+    black[-1] = black_of(-1, before1 + halo_f[far, 0])
+    black[-2] = black_of(-2, before2 + halo_f[far, 1])
     more = {
-        0: flat(0, black[0]) + across(0, -1, black[-1]) + across(0, 1, black[1]),
-        -1: flat(-1, black[-1]) + across(-1, -2, black[-2]) + across(-1, 0, black[0]),
-        -2: seconds[1] + flat(-2, black[-2]) + across(-2, -1, black[-1]),
-        -3: seconds[0] + across(-3, -2, black[-2]),
+        0: before0 + across(0, -1, black[-1]),
+        -1: flat(-1, black[-1]) + across(-1, -2, black[-2]) + before3,
+        -2: (halo_f[far, 1] + fix2) + flat(-2, black[-2]) + across(-2, -1, black[-1]),
+        -3: (halo_f[far, 0] + fix1) + across(-3, -2, black[-2]),
     }
     for j, value in more.items():
         res[j] = jnp.where(mask1(j) if j == 0 else mask1(j) & has_far, value, 0.0)
 
-    put_rows(zmid, 2, 3.0 * (res[0] + res[1]) + (res[-1] + res[2]))
+    put_rows(zmid, 2, 3.0 * res[0] + (res[-1] + inner_rows))
     put_rows(zmid, 3, 3.0 * (res[-1] + res[-2]) + (res[0] + res[-3]))
     parts = parts + restrict(zmid, 2, 2, ny2, weights2, 0.5 ** 12)
-    for j in range(4):
-        mid_ref[at1(j)] = red[j] + black[j]
-
-    cof, fac, for_red, for_black = low_cof, low_fac, low_red, low_black
+
+    cof, dia, fac, for_red, for_black = lows
     rhs = {-1: parts[3], 0: parts[2]}
     red = {j: red_of(j, rhs[j]) for j in (-1, 0)}
     base0 = 32.0 * rhs[0] + flat(0, red[0]) + across(0, -1, red[-1])
@@ -621,6 +632,7 @@
             (send_x.at[side], halo_x, s_x, r_x),
             (send_q.at[side], halo_q, s_q, r_q),
             (send_c1.at[side], halo_c1, s_c1, r_c1),
+            (send_d1.at[side], halo_d1, s_d1, r_d1),
             (send_c2.at[side], halo_c2, s_c2, r_c2),
             (send_2.at[side, 0:2], halo_2, s_2, r_2),
         ))
@@ -653,13 +665,13 @@
         vmem(2, ny2, nx2), vmem(2, ny2, nx2),
     ]
     messages = [
-        vmem(2, ny, nx), vmem(2, ny, nx), vmem(2, 2, ny1, nx1), vmem(2, ny2, nx),
+        vmem(2, ny, nx), vmem(2, ny, nx), vmem(2, ny1, nx1), vmem(2, ny1, nx1), vmem(2, ny2, nx),
     ]
     sent = messages + [vmem(2, 4, ny1, nx1), vmem(2, ny2, nx2)]
     halos = [vmem(2, 2, ny, nx)] + messages + [
         vmem(2, 2, ny1, nx1), vmem(2, ny1, nx1), vmem(2, 2, ny1, nx1), vmem(2, 2, ny2, nx2),
     ]
-    sems = [pltpu.SemaphoreType.DMA((3,))] + [pltpu.SemaphoreType.DMA((2,))] * 18
+    sems = [pltpu.SemaphoreType.DMA((3,))] + [pltpu.SemaphoreType.DMA((2,))] * 20
 
     def run(*refs):
         kernel(size, *refs)

time: 21.2 us -> 20.6 us (0.972)
  Pallas kernels: 20.5 us -> 19.8 us
    pallas_call x1, Pallas kernels: 19.4 us -> 18.8 us  [on_device(): pl.pallas_call(run, out_shape=tuple((pltpu.VMEM(shape, F32) for shape in...]
where the time goes in v8:
time: 20.6 us; the launch traced here: 20.4 us
  Pallas kernels  19.8 us (96%)
  between operations  0.64 us (3%)
    pallas_call x1, Pallas kernels, on_device(): pl.pallas_call(run, out_shape=tuple((pltpu.VMEM(shape, F32) for shape in...  18.8 us
    pallas_call x1, Pallas kernels, on_device(): pl.pallas_call(write_out, out_shape=tuple((jax.ShapeDtypeStruct(shape, F3...  1.03 us

profile of v8, /device:TPU:25, one launch (start us, length us, event | category | flops | bytes accessed | tf_op | source)
XLA Modules:
  0.0 20.4 jit_solution(102746570021116857)
XLA Ops:
  0.6 18.8 %shard_map.58 = (f32[8,64,512]{2,1,0:T(8,128)S(1)}, f32[4,32,256]{2,1,0:T(8,128)S(1)}, f32[2,16,128]{2,1,0:T(8,128)S(1)}) custom-call(f32[8,64,512]{2,1,0:T(8,128)} %refs_0_.1, f32[8,64,512]{2,1,0:T(8,128)} %refs_1_.1, f32[8,64,512]{2,1,0:T(8,128)} %refs_2_.1), custom_call_target="tpu_custom_call" | custom-call | tf_op jit(solution)/shard_map/pallas_call | solution.py:684
  19.4 1.0 %shard_map.59 = (f32[8,64,512]{2,1,0:T(8,128)}, f32[4,32,256]{2,1,0:T(8,128)}, f32[2,16,128]{2,1,0:T(8,128)}) custom-call(f32[8,64,512]{2,1,0:T(8,128)S(1)} %get-tuple-element.6.p_src, f32[4,32,256]{2,1,0:T(8,128)S(1)} %get-tuple-element.7.mid_src, f32[2,16,128]{2,1,0:T(8,128)S(1)} %get-tuple-element.8.low_src), custom_call_target="tpu_custom_call" | custom-call | tf_op jit(solution)/shard_map/pallas_call | solution.py:694

commit v9 on v8

--- a/solution.py
+++ b/solution.py
@@ -72,7 +72,7 @@
     zbuf, zmid, wres, wsum,
     v1, topb, hsum, hside, c1_there, cof1, dia1,
     cof2, dia2,
-    send_x, send_q, send_c1, send_d1, send_c2, send_2, send_3,
+    send_x, send_q, send_c1, send_d1, send_c2, send_2, send_n, send_f, send_3,
     halo_c, halo_x, halo_q, halo_c1, halo_d1, halo_c2, halo_2, halo_n, halo_f, halo_3,
     load_sem,
     s_c, s_x, s_q, s_c1, s_d1, s_c2, s_2, s_n, s_f, s_3,
@@ -150,9 +150,9 @@
     for side in range(2):
         @pl.when(jnp.logical_not(has[side]))
         def _(side=side):
-            for ref in (halo_x, halo_q, halo_c1, halo_d1, halo_c2):
+            for ref in (halo_x, halo_q, halo_c1, halo_d1, halo_n):
                 ref[side] = jnp.zeros(ref.shape[1:], F32)
-            for ref in (halo_c, halo_2, halo_f):
+            for ref in (halo_c, halo_c2, halo_2, halo_f):
                 for i in range(ref.shape[1]):
                     ref[side, i] = jnp.zeros(ref.shape[2:], F32)
     wres[...] = weights_of(wres.shape, 3.0, 1.0)
@@ -225,50 +225,9 @@
     def at_ends(body):
         lax.fori_loop(0, 2, lambda i, carry: body((pairs - 1) * i, carry), 0)
 
-    at_ends(faces)
-    loads[1].wait()
-    lax.fori_loop(0, 2, put_mixed, 0)
-    send(lambda side: send_x.at[side], halo_x, s_x, r_x, odd)
-    lax.fori_loop(0, pairs, pack_g, 0)
-    loads[2].wait()
-    at_ends(red)
+    lax.fori_loop(0, pairs, faces, 0)
     enter(even_core)
     send_coefficients(even_core)
-    send(lambda side: send_x.at[side], halo_x, s_x, r_x, even_core)
-
-    lax.fori_loop(1, pairs - 1, faces, 0)
-    lax.fori_loop(1, pairs - 1, red, 0)
-
-    def put_pressure(k, reds, blacks):
-        p_ref[2 * k] = even_first(reds, blacks)
-        p_ref[2 * k + 1] = even_first(blacks, reds)
-
-    def black(k, carry):
-        rhs = even_first(braw[2 * k + 1], braw[2 * k])
-        reds = rr[k + 1]
-        top = 2.0 * rhs + gather(k, reds, even_first(rr[k + 2], rr[k]), fbo, fbs)
-        topb[k] = top
-        new = top / db[k]
-        dl[k + 1] = new - gb[k + 1]
-        put_pressure(k, reds, new)
-        return carry
-
-    at_ends(black)
-
-    def put_tops(side, carry):
-        k = (pairs - 1) * side
-        send_q[side] = jnp.where(parity(plane, side), rr[k + 1], topb[k])
-        return carry
-
-    lax.fori_loop(0, 2, put_tops, 0)
-    send(lambda side: send_q.at[side], halo_q, s_q, r_q)
-    lax.fori_loop(1, pairs - 1, black, 0)
-
-    def residual(k, carry):
-        rho[k + 1] = gather(k, dl[k + 1], even_first(dl[k], dl[k + 2]), fro, frs)
-        return carry
-
-    lax.fori_loop(0, pairs, residual, 0)
 
     ny1, ny2 = ny // 2, ny // 4
     rows = [
@@ -316,13 +275,48 @@
     for side in range(2):
         send_c1[side] = c1[1 + side]
         send_d1[side] = c1[2 - side]
-        diagonal = d1[2 - side]
-        send_c2[side, :, 0 : nx // 2] = jnp.where(
-            parity((ny2, nx // 2), side + 1), diagonal[:ny2], pltpu.roll(diagonal[ny2:], 1, 0)
-        )
-        send_c2[side, :, nx // 2 : 3 * nx // 4] = c2[side]
-        send_c2[side, :, 3 * nx // 4 : nx] = d2[side]
-    send(lambda side: send_c1.at[side], halo_c1, s_c1, r_c1)
+        send_c2[side, 0] = c2[side]
+        send_c2[side, 1] = d2[side]
+
+    loads[1].wait()
+    lax.fori_loop(0, 2, put_mixed, 0)
+    send(lambda side: send_x.at[side], halo_x, s_x, r_x)
+    lax.fori_loop(0, pairs, pack_g, 0)
+    loads[2].wait()
+    at_ends(red)
+
+    lax.fori_loop(1, pairs - 1, red, 0)
+
+    def put_pressure(k, reds, blacks):
+        p_ref[2 * k] = even_first(reds, blacks)
+        p_ref[2 * k + 1] = even_first(blacks, reds)
+
+    def black(k, carry):
+        rhs = even_first(braw[2 * k + 1], braw[2 * k])
+        reds = rr[k + 1]
+        top = 2.0 * rhs + gather(k, reds, even_first(rr[k + 2], rr[k]), fbo, fbs)
+        topb[k] = top
+        new = top / db[k]
+        dl[k + 1] = new - gb[k + 1]
+        put_pressure(k, reds, new)
+        return carry
+
+    at_ends(black)
+
+    def put_tops(side, carry):
+        k = (pairs - 1) * side
+        send_q[side] = jnp.where(parity(plane, side), rr[k + 1], topb[k])
+        return carry
+
+    lax.fori_loop(0, 2, put_tops, 0)
+    send(lambda side: send_q.at[side], halo_q, s_q, r_q)
+    lax.fori_loop(1, pairs - 1, black, 0)
+
+    def residual(k, carry):
+        rho[k + 1] = gather(k, dl[k + 1], even_first(dl[k], dl[k + 2]), fro, frs)
+        return carry
+
+    lax.fori_loop(0, pairs, residual, 0)
 
     def restrict(ref, first, count, out_rows, weights, scale):
         rows = [
@@ -342,14 +336,60 @@
     put_rows(zbuf, pairs + 1, even_first(0.0, rho[pairs]))
     parts = restrict(zbuf, 0, pairs + 2, ny1, wres[...], 0.5 ** 10)
     for side in range(2):
-        ends = (3 * side, 1 + side, 4 + side)
-        for i, end in enumerate(ends):
+        for i, end in enumerate((3 * side, 1 + side, 4 + side)):
             v1[side, i] = parts[end]
-        send_2[side, 0] = parts[ends[0]]
-        send_2[side, 1] = parts[ends[2]]
-        send_2[side, 2] = (c1[ends[0]] + c1[ends[1]]) * (8.0 * parts[ends[1]] / d1[ends[1]])
-    send(lambda side: send_2.at[side, 0:2], halo_2, s_2, r_2)
-    copy_out(near, send_2.at[near, 2], halo_n, s_n, r_n).start()
+
+    def mask1(j):
+        return parity(plane1, j + far + 4)
+
+    def at1(j):
+        return 3 * far + j * (1 - 2 * far)
+
+    cof = {j: cof1[at1(j)] for j in range(4)}
+    dia = {j: dia1[at1(j)] for j in range(4)}
+    fac, for_red, for_black = {}, {}, {}
+
+    def prepare(j, mask, factor, present=None):
+        fac[j] = side_faces(cof[j], cof[j])[0]
+        if j in dia:
+            for_red[j] = jnp.where(mask, factor / dia[j], 0.0)
+            for_black[j] = jnp.where(mask, 0.0, 1.0 / dia[j])
+            if present is not None:
+                for_red[j] = jnp.where(present, for_red[j], 0.0)
+                for_black[j] = jnp.where(present, for_black[j], 0.0)
+
+    def flat(j, field):
+        total = None
+        for face, shifted in zip(fac[j], shifts(field)):
+            term = face * shifted
+            total = term if total is None else total + term
+        return total
+
+    def across(i, j, field):
+        return (cof[i] + cof[j]) * field
+
+    def red_of(j, right):
+        return for_red[j] * right
+
+    def black_of(j, top):
+        return for_black[j] * top
+
+    alone = dia[0]
+    for j in (0, 1, 2):
+        prepare(j, mask1(j), 8.0)
+    alone_red, alone_black = for_red[0], for_black[0]
+    right0, right1 = v1[far, 0], v1[far, 1]
+    red0, red1 = alone_red * right0, red_of(1, right1)
+    top0 = 8.0 * right0 + flat(0, red0) + across(0, 1, red1)
+    send_2[near, 0] = v1[near, 0]
+    send_2[near, 1] = v1[near, 2]
+    send_n[near] = across(3, 2, red_of(2, v1[near, 1]))
+    send_2[far, 0] = jnp.where(mask1(0), red0, pltpu.roll(alone, 1, 0))
+    send_2[far, 1] = v1[far, 2]
+    send_n[far] = jnp.where(mask1(0), pltpu.roll(dia[2], 1, 0), top0)
+    send(lambda side: send_2.at[side], halo_2, s_2, r_2)
+    send(lambda side: send_n.at[side], halo_n, s_n, r_n)
+    send(lambda side: send_c1.at[side], halo_c1, s_c1, r_c1)
     send(lambda side: send_d1.at[side], halo_d1, s_d1, r_d1)
     send(lambda side: send_c2.at[side], halo_c2, s_c2, r_c2)
 
@@ -412,60 +452,23 @@
         add = fpair[k] * change + jnp.where(mine, face * delta_there, 0.0)
         for i, shifted in enumerate(shifts(change)):
             add = add + frs[k, i] * shifted
-        put_rows(zbuf, 0, jnp.where(mine, add, 0.0))
-        put_rows(zbuf, 1, jnp.where(mine, 0.0, add))
-        put_rows(zbuf, 2, jnp.where(mine, (cr[inner + 1] + cb[k + 1]) * change, 0.0))
+        own, third = add, (cr[inner + 1] + cb[k + 1]) * change
         add = pair * change_there + jnp.where(mine | jnp.logical_not(present), 0.0, face * delta)
         for i, shifted in enumerate(shifts(change_there)):
             add = add + hside[1, i] * shifted
-        put_rows(zbuf, 3, jnp.where(mine, 0.0, add))
-        put_rows(zbuf, 4, jnp.where(mine, add, 0.0))
-        put_rows(zbuf, 5, jnp.where(mine, 0.0, (mixed + hc1) * change_there))
-        own0, own1, own2, end0, end1, end2 = restrict(zbuf, 0, 6, ny1, wres[...], 0.5 ** 10)
-        v1[side, 0] = v1[side, 0] + (3.0 * (own0 + own1) + own2)
-        v1[side, 1] = v1[side, 1] + (3.0 * own2 + own1)
-        v1[side, 2] = v1[side, 2] + own0
-        v1[side, 3] = end0
-        v1[side, 4] = 3.0 * (end0 + end1) + end2
-        v1[side, 5] = 3.0 * end2 + end1
+        beyond = (mixed + hc1) * change_there
+        put_rows(zbuf, 0, 3.0 * own + jnp.where(mine, third, add))
+        put_rows(zbuf, 1, 3.0 * add + jnp.where(mine, own, beyond))
+        put_rows(zbuf, 2, jnp.where(mine, 3.0 * third, own))
+        put_rows(zbuf, 3, jnp.where(mine, add, 3.0 * beyond))
+        parts = restrict(zbuf, 0, 4, ny1, wres[...], 0.5 ** 10)
+        v1[side, 0] = v1[side, 0] + parts[0]
+        v1[side, 2] = v1[side, 2] + parts[1]
+        v1[side, 1] = v1[side, 1] + parts[2]
+        v1[side, 3] = parts[3]
 
     true = me >= 0
     second_stage(near, true)
-
-    def mask1(j):
-        return parity(plane1, j + far + 4)
-
-    def at1(j):
-        return 3 * far + j * (1 - 2 * far)
-
-    cof = {j: cof1[at1(j)] for j in range(4)}
-    dia = {j: dia1[at1(j)] for j in range(4)}
-    fac, for_red, for_black = {}, {}, {}
-
-    def prepare(j, mask, factor, present=None):
-        fac[j] = side_faces(cof[j], cof[j])[0]
-        if j in dia:
-            for_red[j] = jnp.where(mask, factor / dia[j], 0.0)
-            for_black[j] = jnp.where(mask, 0.0, 1.0 / dia[j])
-            if present is not None:
-                for_red[j] = jnp.where(present, for_red[j], 0.0)
-                for_black[j] = jnp.where(present, for_black[j], 0.0)
-
-    def flat(j, field):
-        total = None
-        for face, shifted in zip(fac[j], shifts(field)):
-            term = face * shifted
-            total = term if total is None else total + term
-        return total
-
-    def across(i, j, field):
-        return (cof[i] + cof[j]) * field
-
-    def red_of(j, right):
-        return for_red[j] * right
-
-    def black_of(j, top):
-        return for_black[j] * top
 
     wait_recv(near, true, halo_c1, s_c1, r_c1)
     wait_recv(near, true, halo_d1, s_d1, r_d1)
@@ -474,18 +477,18 @@
 
     cof.update({4: c1_there[near], 5: halo_c1[near], 6: halo_d1[near]})
     dia.update({3: dia[3] + cof[4], 4: diagonal_of(4), 5: diagonal_of(5)})
-    for j in (1, 2, 3, 4, 5):
+    for j in (3, 4, 5):
         prepare(j, mask1(j), 8.0)
     wait_recv(near, true, halo_2, s_2, r_2)
     wait_recv(near, true, halo_n, s_n, r_n)
     rhs = {
-        4: halo_2[near, 0] + v1[near, 4] + v1[near, 2],
-        3: v1[near, 0] + (halo_2[near, 1] + v1[near, 3]),
+        4: halo_2[near, 0] + v1[near, 2],
+        3: v1[near, 0] + halo_2[near, 1],
         2: v1[near, 1],
     }
     red = {j: red_of(j, rhs[j]) for j in (2, 3, 4)}
     black = {}
-    beyond = halo_n[near] + across(4, 5, red_of(5, v1[near, 5]))
+    beyond = halo_n[near] + across(4, 5, red_of(5, v1[near, 3]))
     black[4] = black_of(4, 8.0 * rhs[4] + beyond + flat(4, red[4]) + across(4, 3, red[3]))
     black[3] = black_of(
         3, 8.0 * rhs[3] + flat(3, red[3]) + across(3, 4, red[4]) + across(3, 2, red[2])
@@ -503,12 +506,22 @@
         return red1, black2, part1, part2, across(1, 2, black2)
 
     red1, black2, part1, part2, cross = middle()
-    send_2[far, 2] = jnp.where(mask1(0), part2, across(0, 1, red1))
-    send_2[far, 3] = jnp.where(mask1(1), cross, part1)
+    black0 = alone_black * top0
+    black1 = black_of(1, part1 + across(1, 0, red0))
+    res0 = flat(0, black0) + across(0, 1, black1)
+    res1 = flat(1, black1) + across(1, 0, black0) + cross
+    res2 = part2 + across(2, 1, black1)
+    res0 = jnp.where(mask1(0), res0, 0.0)
+    weights2 = wres[0 : nx // 2, 0 : nx // 4]
+    put_rows(zmid, 0, jnp.where(mask1(1), 3.0 * res1, 3.0 * res0 + jnp.where(mask1(2), res2, 0.0)))
+    put_rows(zmid, 1, res0)
+    parts = restrict(zmid, 0, 2, ny2, weights2, 0.5 ** 12)
+    send_f[0] = parts[0]
+    send_f[1] = parts[1]
 
     @pl.when(has_far)
     def _():
-        copy_out(far, send_2.at[far, 2:4], halo_f, s_f, r_f).start()
+        copy_out(far, send_f, halo_f, s_f, r_f).start()
 
     def mask2(j):
         return parity(plane2, j + far + 4)
@@ -517,10 +530,10 @@
         return far + j * (1 - 2 * far)
 
     def coef2(side):
-        return halo_c2[side, :, nx // 2 : 3 * nx // 4]
+        return halo_c2[side, 0]
 
     def diagonal2(side):
-        return halo_c2[side, :, 3 * nx // 4 : nx]
+        return halo_c2[side, 1]
 
     wait_recv(near, true, halo_c2, s_c2, r_c2)
     levels = cof, dia, fac, for_red, for_black
@@ -534,19 +547,18 @@
 
     second_stage(far, has_far)
     red[1], black[2], part1, part2, cross = middle()
-    wait_recv(far, has_far, halo_c1, s_c1, r_c1)
-    cof.update({-1: c1_there[far], -2: halo_c1[far]})
-    dia.update({-1: diagonal_of(-1), 0: dia[0] + cof[-1]})
+    cof[-1] = c1_there[far]
+    dia[0] = alone + cof[-1]
     prepare(0, mask1(0), 8.0)
-    prepare(-1, mask1(-1), 8.0, has_far)
     base0 = across(0, 1, red[1])
-    end0 = v1[far, 0] + v1[far, 3]
-    end1 = v1[far, 4] + v1[far, 2]
+    end0 = v1[far, 0]
+    end1 = 8.0 * v1[far, 2]
     wait_recv(far, has_far, halo_2, s_2, r_2)
     rhs[0] = halo_2[far, 1] + end0
-    rhs[-1] = halo_2[far, 0] + end1
     red[0] = red_of(0, rhs[0])
-    red[-1] = red_of(-1, rhs[-1])
+    first = halo_2[far, 0]
+    diagonal = pltpu.roll(first, ny1 - 1, 0)
+    red[-1] = jnp.where(mask1(-1) & has_far, (first * diagonal + end1) / (diagonal + cof[0]), 0.0)
     black[0] = black_of(0, 8.0 * rhs[0] + base0 + across(0, -1, red[-1]) + flat(0, red[0]))
     black[1] = black_of(1, part1 + across(1, 0, red[0]))
     res = {
@@ -555,7 +567,6 @@
         1: flat(1, black[1]) + across(1, 0, black[0]) + cross,
     }
     res = {j: jnp.where(mask1(j), value, 0.0) for j, value in res.items()}
-    weights2 = wres[0 : nx // 2, 0 : nx // 4]
     put_rows(zmid, 0, 3.0 * (res[3] + res[2]) + res[1])
     put_rows(zmid, 1, res[3])
     parts = restrict(zmid, 0, 2, ny2, weights2, 0.5 ** 12)
@@ -563,19 +574,37 @@
     send_3[1] = parts[1]
     copy_out(near, send_3, halo_3, s_3, r_3).start()
 
+    wait_recv(far, has_far, halo_n, s_n, r_n)
+    wait_recv(far, has_far, halo_c1, s_c1, r_c1)
     wait_recv(far, has_far, halo_d1, s_d1, r_d1)
     wait_recv(far, has_far, halo_c2, s_c2, r_c2)
-    cof[-3] = halo_d1[far]
-    packed = halo_c2[far, :, 0 : nx // 2]
-    packed = jnp.concatenate([packed, pltpu.roll(packed, ny2 - 1, 0)], axis=0)
-    dia.update({-2: diagonal_of(-2), -3: packed})
-    for j in (-2, -3):
+    cof.update({-2: halo_c1[far], -3: halo_d1[far]})
+    second = halo_n[far]
+    diagonal = 6.0 * cof[-1] + plane_sum(cof[-1]) + cof[-2]
+    dia.update({-1: diagonal + cof[0], -2: diagonal_of(-2), -3: pltpu.roll(second, ny1 - 1, 0)})
+    for j in (-1, -2, -3):
         prepare(j, mask1(j), 8.0, has_far)
-    there2 = v1[far, 5]
-    more_red = red_of(-2, there2)
-    more_black = black_of(-3, across(-3, -2, more_red))
-    fix1 = jnp.where(mask1(-1), flat(-3, more_black), across(-1, -2, more_red))
-    fix2 = jnp.where(mask1(-2), across(-2, -3, more_black), 8.0 * there2 + flat(-2, more_red))
+    there2 = v1[far, 3]
+    more_red1 = jnp.where(mask1(-1) & has_far, red[-1] - first, 0.0)
+    more_red2 = red_of(-2, there2)
+    top = second + end1 + flat(-1, more_red1) + across(-1, -2, more_red2) + across(-1, 0, red[0])
+    black[-1] = black_of(-1, top)
+    more1 = jnp.where(mask1(-1) | jnp.logical_not(has_far), 0.0, black[-1] - second / diagonal)
+    more2 = black_of(-2, 8.0 * there2 + flat(-2, more_red2) + across(-2, -1, more_red1))
+    more3 = black_of(-3, across(-3, -2, more_red2))
+    more = {
+        0: flat(0, black[0]) + across(0, 1, black[1]) + across(0, -1, black[-1]),
+        -1: flat(-1, more1) + across(-1, -2, more2) + across(-1, 0, black[0]),
+        -2: flat(-2, more2) + across(-2, -1, more1) + across(-2, -3, more3),
+        -3: flat(-3, more3) + across(-3, -2, more2),
+    }
+    for j, value in more.items():
+        res[j] = jnp.where(mask1(j) if j == 0 else mask1(j) & has_far, value, 0.0)
+    put_rows(zmid, 2, 3.0 * (res[0] + res[1]) + (res[-1] + res[2]))
+    put_rows(zmid, 3, 3.0 * (res[-1] + res[-2]) + (res[0] + res[-3]))
+    parts = parts + restrict(zmid, 2, 2, ny2, weights2, 0.5 ** 12)
+    for j in range(4):
+        mid_ref[at1(j)] = red[j] + black[j]
 
     cof, dia, fac, for_red, for_black = lows
     cof[-1] = coef2(far)
@@ -584,31 +613,9 @@
     prepare(-1, mask2(-1), 32.0, has_far)
     cof, dia, fac, for_red, for_black = levels
 
-    before1 = 8.0 * rhs[-1] + fix1 + flat(-1, red[-1]) + across(-1, 0, red[0])
-    before2 = fix2 + across(-2, -1, red[-1])
-    before0 = flat(0, black[0]) + across(0, 1, black[1])
-    before3 = across(-1, 0, black[0])
-    inner_rows = 3.0 * res[1] + res[2]
-    for j in range(4):
-        mid_ref[at1(j)] = red[j] + black[j]
     wait_recv(far, has_far, halo_f, s_f, r_f)
-    black[-1] = black_of(-1, before1 + halo_f[far, 0])
-    black[-2] = black_of(-2, before2 + halo_f[far, 1])
-    more = {
-        0: before0 + across(0, -1, black[-1]),
-        -1: flat(-1, black[-1]) + across(-1, -2, black[-2]) + before3,
-        -2: (halo_f[far, 1] + fix2) + flat(-2, black[-2]) + across(-2, -1, black[-1]),
-        -3: (halo_f[far, 0] + fix1) + across(-3, -2, black[-2]),
-    }
-    for j, value in more.items():
-        res[j] = jnp.where(mask1(j) if j == 0 else mask1(j) & has_far, value, 0.0)
-
-    put_rows(zmid, 2, 3.0 * res[0] + (res[-1] + inner_rows))
-    put_rows(zmid, 3, 3.0 * (res[-1] + res[-2]) + (res[0] + res[-3]))
-    parts = parts + restrict(zmid, 2, 2, ny2, weights2, 0.5 ** 12)
-
     cof, dia, fac, for_red, for_black = lows
-    rhs = {-1: parts[3], 0: parts[2]}
+    rhs = {-1: parts[3] + halo_f[far, 0], 0: parts[2] + halo_f[far, 1]}
     red = {j: red_of(j, rhs[j]) for j in (-1, 0)}
     base0 = 32.0 * rhs[0] + flat(0, red[0]) + across(0, -1, red[-1])
     base1 = across(1, 0, red[0])
@@ -634,12 +641,11 @@
             (send_c1.at[side], halo_c1, s_c1, r_c1),
             (send_d1.at[side], halo_d1, s_d1, r_d1),
             (send_c2.at[side], halo_c2, s_c2, r_c2),
-            (send_2.at[side, 0:2], halo_2, s_2, r_2),
+            (send_2.at[side], halo_2, s_2, r_2),
+            (send_n.at[side], halo_n, s_n, r_n),
         ))
-    wait_sent(near, true, (
-        (send_2.at[near, 2], halo_n, s_n, r_n), (send_3, halo_3, s_3, r_3),
-    ))
-    wait_sent(far, has_far, ((send_2.at[far, 2:4], halo_f, s_f, r_f),))
+    wait_sent(near, true, ((send_3, halo_3, s_3, r_3),))
+    wait_sent(far, has_far, ((send_f, halo_f, s_f, r_f),))
 
 
 def on_device(size, pressure_guess, source, conductance):
@@ -660,17 +666,16 @@
     work = [
         vmem(pairs + 2, nx // 128, ny + 16, 128), vmem(4, nx1 // 128, ny1 + 16, 128),
         pltpu.VMEM((nx, nx1), BF16), pltpu.VMEM((nx, nx1), BF16),
-        vmem(2, 6, ny1, nx1), vmem(pairs, ny, nx), vmem(2, ny, nx), vmem(2, 4, ny, nx),
+        vmem(2, 4, ny1, nx1), vmem(pairs, ny, nx), vmem(2, ny, nx), vmem(2, 4, ny, nx),
         vmem(2, ny1, nx1), vmem(pairs, ny1, nx1), vmem(pairs, ny1, nx1),
         vmem(2, ny2, nx2), vmem(2, ny2, nx2),
     ]
     messages = [
-        vmem(2, ny, nx), vmem(2, ny, nx), vmem(2, ny1, nx1), vmem(2, ny1, nx1), vmem(2, ny2, nx),
+        vmem(2, ny, nx), vmem(2, ny, nx), vmem(2, ny1, nx1), vmem(2, ny1, nx1), vmem(2, 2, ny2, nx2),
+        vmem(2, 2, ny1, nx1), vmem(2, ny1, nx1),
     ]
-    sent = messages + [vmem(2, 4, ny1, nx1), vmem(2, ny2, nx2)]
-    halos = [vmem(2, 2, ny, nx)] + messages + [
-        vmem(2, 2, ny1, nx1), vmem(2, ny1, nx1), vmem(2, 2, ny1, nx1), vmem(2, 2, ny2, nx2),
-    ]
+    sent = messages + [vmem(2, ny2, nx2), vmem(2, ny2, nx2)]
+    halos = [vmem(2, 2, ny, nx)] + messages + [vmem(2, 2, ny2, nx2), vmem(2, 2, ny2, nx2)]
     sems = [pltpu.SemaphoreType.DMA((3,))] + [pltpu.SemaphoreType.DMA((2,))] * 20
 
     def run(*refs):

time: 20.6 us -> 20.3 us (0.985)
  no operation moved by 1% of the time
where the time goes in v9:
time: 20.3 us
  Pallas kernels  19.6 us (97%)
  between operations  0.64 us (3%)
    pallas_call x1, Pallas kernels, on_device(): pl.pallas_call(run, out_shape=tuple((pltpu.VMEM(shape, F32) for shape in...  18.6 us
    pallas_call x1, Pallas kernels, on_device(): pl.pallas_call(write_out, out_shape=tuple((jax.ShapeDtypeStruct(shape, F3...  1.03 us

profile of v9, /device:TPU:25, one launch (start us, length us, event | category | flops | bytes accessed | tf_op | source)
XLA Modules:
  0.0 20.3 jit_solution(7335895213026763301)
XLA Ops:
  0.6 18.6 %shard_map.58 = (f32[8,64,512]{2,1,0:T(8,128)S(1)}, f32[4,32,256]{2,1,0:T(8,128)S(1)}, f32[2,16,128]{2,1,0:T(8,128)S(1)}) custom-call(f32[8,64,512]{2,1,0:T(8,128)} %refs_0_.1, f32[8,64,512]{2,1,0:T(8,128)} %refs_1_.1, f32[8,64,512]{2,1,0:T(8,128)} %refs_2_.1), custom_call_target="tpu_custom_call" | custom-call | tf_op jit(solution)/shard_map/pallas_call | solution.py:689
  19.2 1.0 %shard_map.59 = (f32[8,64,512]{2,1,0:T(8,128)}, f32[4,32,256]{2,1,0:T(8,128)}, f32[2,16,128]{2,1,0:T(8,128)}) custom-call(f32[8,64,512]{2,1,0:T(8,128)S(1)} %get-tuple-element.6.p_src, f32[4,32,256]{2,1,0:T(8,128)S(1)} %get-tuple-element.7.mid_src, f32[2,16,128]{2,1,0:T(8,128)S(1)} %get-tuple-element.8.low_src), custom_call_target="tpu_custom_call" | custom-call | tf_op jit(solution)/shard_map/pallas_call | solution.py:699
